TPU v7x, 128 devices: a whole 4x4x4 slice. The times are simulated.
128 devices in a mesh: ctx: 16 (over z_hi, x, core), tp: 8 (over z_lo, y).
Axes of the slice: x: 4, y: 4, z: 4 (z_hi: 2, z_lo: 2; z = z_hi * 2 + z_lo), core: 2. Of those that a mesh axis runs over, the one named last changes fastest.
Arguments:
- block_input: bfloat16 [8192, 1536], P('ctx'), may hold values from -6 to 6
- positions: int32 [8192], replicated, may hold values from 0 to 8191, as said below
- attn_gain: bfloat16 [1536], P('ctx'), may hold values from 0.5 to 1.5
- query_weight: bfloat16 [1536, 1536], P('ctx', 'tp'), may hold values from -0.15625 to 0.15625
- key_weight: bfloat16 [1536, 512], P('ctx', 'tp'), may hold values from -0.15625 to 0.15625
- value_weight: bfloat16 [1536, 512], P('ctx', 'tp'), may hold values from -0.15625 to 0.15625
- query_gain: bfloat16 [64], P('ctx'), may hold values from 0.25 to 1.75
- key_gain: bfloat16 [64], P('ctx'), may hold values from 0.25 to 1.75
- output_weight: bfloat16 [1536, 1536], P('tp', 'ctx'), may hold values from -2.5 to 2.5
- ffn_gain: bfloat16 [1536], P('ctx'), may hold values from 0.5 to 1.5
- gate_weight: bfloat16 [1536, 6912], P('ctx', 'tp'), may hold values from -0.15625 to 0.15625
- up_weight: bfloat16 [1536, 6912], P('ctx', 'tp'), may hold values from -0.15625 to 0.15625
- down_weight: bfloat16 [6912, 1536], P('tp', 'ctx'), may hold values from -0.078125 to 0.078125
- out_cotangent: bfloat16 [8192, 1536], P('ctx'), may hold values from -6 to 6
Outputs:
- block_output: bfloat16 [8192, 1536], P('ctx')
- grad_input: float32 [8192, 1536], P('ctx')
- grad_attn_gain: float32 [1536], P('ctx')
- grad_query_weight: float32 [1536, 1536], P('ctx', 'tp')
- grad_key_weight: float32 [1536, 512], P('ctx', 'tp')
- grad_value_weight: float32 [1536, 512], P('ctx', 'tp')
- grad_query_gain: float32 [64], P('ctx')
- grad_key_gain: float32 [64], P('ctx')
- grad_output_weight: float32 [1536, 1536], P('tp', 'ctx')
- grad_ffn_gain: float32 [1536], P('ctx')
- grad_gate_weight: float32 [1536, 6912], P('ctx', 'tp')
- grad_up_weight: float32 [1536, 6912], P('ctx', 'tp')
- grad_down_weight: float32 [6912, 1536], P('tp', 'ctx')
Inputs may be any that keep to these rules, and one draw needn't show every extreme that they name: positions holds every one of 0 to 8191 once; each aligned run of 256 stored rows holds 256 consecutive increasing positions, the runs in any order.
All inputs are finite; a program needn't handle non-finite values.
Results may differ from a plain program's by a relative error of at most 0.039.
Values may be sent and summed in bfloat16 or wider, within the bound.
A program may use at most 128 MiB of HBM per device.

v0:
```python
import math

import jax
import jax.numpy as jnp
from jax import lax
from jax.sharding import PartitionSpec as P

HD = 64


EPS = 1e-05
THETA = 1000000.0
NEG = -1e30


def cut_along(shard, dim, devices):
    dims = shard.shape
    blocks = shard.reshape(*dims[:dim], devices, dims[dim] // devices, *dims[dim + 1 :])
    return jnp.moveaxis(blocks, dim, 0)


def sum_at_owner(shard, axis, dim):
    blocks = cut_along(shard, dim, lax.axis_size(axis))
    arrived = lax.all_to_all(blocks, axis, split_axis=0, concat_axis=0, tiled=True)
    return arrived.astype(jnp.float32).sum(axis=0)


def copy_for_each(shard, axis):
    copies = jnp.broadcast_to(shard, (lax.axis_size(axis), *shard.shape))
    return lax.all_to_all(copies, axis, split_axis=0, concat_axis=0, tiled=True)


def joined_along(blocks, dim):
    blocks = jnp.moveaxis(blocks, 0, dim)
    dims = blocks.shape
    return blocks.reshape(*dims[:dim], dims[dim] * dims[dim + 1], *dims[dim + 2 :])


def gather_directly(shard, axis, dim):
    blocks = copy_for_each(shard, axis)
    return joined_along(blocks, dim)


def sent_together(arrays, axis, dim, along):
    widths = [math.prod(a.shape[along:]) for a in arrays]
    both = jnp.concatenate(
        [a.reshape(*a.shape[:along], w) for a, w in zip(arrays, widths)], axis=along
    )
    whole = lax.all_gather(both, axis, axis=dim, tiled=True)
    blocks = jnp.split(whole, [sum(widths[:k]) for k in range(1, len(widths))], axis=along)
    return tuple(
        (b.reshape(*whole.shape[:along], *a.shape[along:]) for a, b in zip(arrays, blocks))
    )


def in_one_piece(arrays, axis, dim, along):
    ends, at = ([], 0)
    for a in arrays[:-1]:
        at += a.shape[along]
        ends.append(at)
    both = jnp.concatenate(arrays, axis=along)
    return tuple(jnp.split(lax.all_gather(both, axis, axis=dim, tiled=True), ends, axis=along))


def sent_together_2(arrays, axis, dim, along):
    ends, at = ([], 0)
    for a in arrays[:-1]:
        at += a.shape[along]
        ends.append(at)
    both = jnp.concatenate(arrays, axis=along)
    return tuple(
        jnp.split(lax.psum_scatter(both, axis, scatter_dimension=dim, tiled=True), ends, axis=along)
    )


def dot_nt(left, right):
    return lax.dot_general(
        left, right, (((1,), (1,)), ((), ())), preferred_element_type=jnp.float32
    )


def dot_tn(left, right):
    return lax.dot_general(
        left, right, (((0,), (0,)), ((), ())), preferred_element_type=jnp.float32
    )


def rms_forward(value):
    inverse = lax.rsqrt(jnp.mean(value * value, axis=-1, keepdims=True) + EPS)
    return (value * inverse, inverse)


def rms_backward(grad_hat, normed, inverse):
    return inverse * (grad_hat - normed * jnp.mean(grad_hat * normed, axis=-1, keepdims=True))


def rotary_tables(places, width):
    half_width = width // 2
    freq_table = THETA ** (-(jnp.arange(half_width, dtype=jnp.float32) * 2.0 / width))
    angles = places.astype(jnp.float32)[:, None] * freq_table[None, :]
    cosine_table = jnp.concatenate([jnp.cos(angles), jnp.cos(angles)], axis=-1)
    sine_table = jnp.concatenate([jnp.sin(angles), jnp.sin(angles)], axis=-1)
    return (cosine_table[:, None, :], sine_table[:, None, :])


def rotate(value, cosine_table, sine_table):
    half_width = value.shape[-1] // 2
    turned = jnp.concatenate([-value[..., half_width:], value[..., :half_width]], axis=-1)
    return value * cosine_table + turned * sine_table


def rotate_back(grad_rot, cosine_table, sine_table):
    half_width = grad_rot.shape[-1] // 2
    scaled = grad_rot * sine_table
    return grad_rot * cosine_table + jnp.concatenate(
        [scaled[..., half_width:], -scaled[..., :half_width]], axis=-1
    )


def key_blocks(key_rows, value_rows, places, head_count):
    key_count = key_rows.shape[0]
    block_size = math.gcd(key_count, 1024)
    number = key_count // block_size
    head_width = key_rows.shape[1] // head_count

    def arrange(array_in):
        return array_in.reshape(number, block_size, head_count, head_width).transpose(0, 2, 1, 3)

    return (arrange(key_rows), arrange(value_rows), places.reshape(number, block_size))


def attend_piece(carried, key_rows, value_rows, places, queries, rows_pos, score_scale):
    key_split, value_split, pos_split = key_blocks(key_rows, value_rows, places, queries.shape[0])

    def block_step(running, current):
        row_max, row_sum, accumulated = running
        key_part, value_part, key_pos = current
        scores = (
            jnp.einsum("hrd,hkd->hrk", queries, key_part, preferred_element_type=jnp.float32)
            * score_scale
        )
        allowed = (key_pos[None, :] <= rows_pos[:, None])[None]
        scores = jnp.where(allowed, scores, NEG)
        new_max = jnp.maximum(row_max, jnp.max(scores, axis=-1, keepdims=True))
        factor = jnp.exp(row_max - new_max)
        weights = jnp.where(allowed, jnp.exp(scores - new_max), 0.0)
        row_sum = row_sum * factor + jnp.sum(weights, axis=-1, keepdims=True)
        accumulated = accumulated * factor + jnp.einsum(
            "hrk,hkd->hrd",
            weights.astype(jnp.bfloat16),
            value_part,
            preferred_element_type=jnp.float32,
        )
        return ((new_max, row_sum, accumulated), None)

    result, unused = lax.scan(block_step, carried, (key_split, value_split, pos_split))
    return result


def row_reduce(partial_rows):
    return sum_at_owner(partial_rows.astype(jnp.bfloat16), "tp", 0)


def row_collect(share_rows):
    return gather_directly(share_rows, "tp", 0)


def body(
    block_input,
    positions,
    attn_gain,
    query_weight,
    key_weight,
    value_weight,
    query_gain,
    key_gain,
    output_weight,
    ffn_gain,
    gate_weight,
    up_weight,
    down_weight,
    out_cotangent,
):
    tok_rows = block_input.shape[0]
    query_heads = query_weight.shape[1] // HD
    pair_heads = key_weight.shape[1] // HD
    group_size = query_heads // pair_heads
    row_count = group_size * tok_rows
    score_scale = HD ** (-0.5)
    start_row = lax.axis_index("ctx") * tok_rows
    own_pos = lax.dynamic_slice_in_dim(positions, start_row, tok_rows, 0)
    rows_pos = jnp.tile(own_pos, group_size)
    share_rows = tok_rows // lax.axis_size("tp")
    share_start = lax.axis_index("tp") * share_rows

    def own_rows(array_in):
        return lax.dynamic_slice_in_dim(array_in, share_start, share_rows, 0)

    gathered = (
        *sent_together((attn_gain, query_weight, key_weight, value_weight), "ctx", 0, 1),
        lax.all_gather(query_gain, "ctx", axis=0, tiled=True),
        lax.all_gather(key_gain, "ctx", axis=0, tiled=True),
        lax.all_gather(output_weight, "ctx", axis=1, tiled=True),
        *sent_together((ffn_gain, gate_weight, up_weight), "ctx", 0, 1),
        lax.all_gather(down_weight, "ctx", axis=1, tiled=True),
    )
    (
        norm_first,
        query_full,
        key_full,
        value_full,
        query_scale,
        key_scale,
        output_full,
        norm_second,
        gate_full,
        up_full,
        down_full,
    ) = gathered
    residual_in = block_input.astype(jnp.float32)
    normed_one, inverse_one = rms_forward(residual_in)
    hidden_one = (normed_one * norm_first.astype(jnp.float32)).astype(jnp.bfloat16)
    query_raw = jnp.dot(hidden_one, query_full, preferred_element_type=jnp.float32).reshape(
        tok_rows, query_heads, HD
    )
    key_raw = jnp.dot(hidden_one, key_full, preferred_element_type=jnp.float32).reshape(
        tok_rows, pair_heads, HD
    )
    value_rows = jnp.dot(hidden_one, value_full, preferred_element_type=jnp.float32).astype(
        jnp.bfloat16
    )
    cosine_table, sine_table = rotary_tables(own_pos, HD)
    query_hat, query_inv = rms_forward(query_raw)
    query_rot = rotate(
        query_hat * query_scale.astype(jnp.float32), cosine_table, sine_table
    ).astype(jnp.bfloat16)
    key_hat, key_inv = rms_forward(key_raw)
    key_rot = rotate(key_hat * key_scale.astype(jnp.float32), cosine_table, sine_table).astype(
        jnp.bfloat16
    )
    key_rows = key_rot.reshape(tok_rows, pair_heads * HD)
    queries = (
        query_rot.reshape(tok_rows, pair_heads, group_size, HD)
        .transpose(1, 2, 0, 3)
        .reshape(pair_heads, row_count, HD)
    )
    start_state = (
        jnp.full((pair_heads, row_count, 1), NEG, jnp.float32),
        jnp.zeros((pair_heads, row_count, 1), jnp.float32),
        jnp.zeros((pair_heads, row_count, HD), jnp.float32),
    )
    keys_all, values_all = in_one_piece((key_rows, value_rows), "ctx", 0, 1)
    row_max, row_sum, accumulated = attend_piece(
        start_state, keys_all, values_all, positions, queries, rows_pos, score_scale
    )
    attn_heads = accumulated / row_sum
    attn_flat = (
        attn_heads.reshape(pair_heads, group_size, tok_rows, HD)
        .transpose(2, 0, 1, 3)
        .reshape(tok_rows, query_heads * HD)
    )
    attn_low = attn_flat.astype(jnp.bfloat16)
    attn_part = jnp.dot(attn_low, output_full, preferred_element_type=jnp.float32)
    residual_mid = own_rows(residual_in) + row_reduce(attn_part)
    normed_two, inverse_two = rms_forward(residual_mid)
    hidden_two = row_collect((normed_two * norm_second.astype(jnp.float32)).astype(jnp.bfloat16))
    cot_rows = own_rows(out_cotangent)
    gate_pre = jnp.dot(hidden_two, gate_full, preferred_element_type=jnp.float32)
    up_pre = jnp.dot(hidden_two, up_full, preferred_element_type=jnp.float32)
    sigmoid_gate = jax.nn.sigmoid(gate_pre)
    activation = (gate_pre * sigmoid_gate * up_pre).astype(jnp.bfloat16)
    ffn_part = jnp.dot(activation, down_full, preferred_element_type=jnp.float32)
    block_output = row_collect((residual_mid + row_reduce(ffn_part)).astype(jnp.bfloat16))
    grad_act = dot_nt(out_cotangent, down_full)
    grad_gate = (grad_act * up_pre * sigmoid_gate * (1.0 + gate_pre * (1.0 - sigmoid_gate))).astype(
        jnp.bfloat16
    )
    grad_up = (grad_act * gate_pre * sigmoid_gate).astype(jnp.bfloat16)
    down_grad = dot_tn(activation, out_cotangent)
    gate_grad = dot_tn(hidden_two, grad_gate)
    up_grad = dot_tn(hidden_two, grad_up)
    back_part_two = dot_nt(grad_gate, gate_full) + dot_nt(grad_up, up_full)
    back_two = row_reduce(back_part_two)
    gain_two_grad = jnp.sum(back_two * normed_two, axis=0)
    grad_mid = cot_rows.astype(jnp.float32) + rms_backward(
        back_two * norm_second.astype(jnp.float32), normed_two, inverse_two
    )
    grad_branch_rows = grad_mid.astype(jnp.bfloat16)
    grad_branch = row_collect(grad_branch_rows)
    output_grad = dot_tn(attn_low, grad_branch)
    grad_flat = dot_nt(grad_branch, output_full)
    grad_heads = (
        grad_flat.reshape(tok_rows, pair_heads, group_size, HD)
        .transpose(1, 2, 0, 3)
        .reshape(pair_heads, row_count, HD)
    )
    grad_scaled = (grad_heads / row_sum).astype(jnp.bfloat16)
    row_drift = jnp.sum(grad_heads * attn_heads, axis=-1, keepdims=True) / row_sum
    keys_all, values_all = (keys_all, values_all)
    key_split, value_split, pos_split = key_blocks(keys_all, values_all, positions, pair_heads)

    def back_step(grad_query, current):
        key_part, value_part, key_pos = current
        scores = (
            jnp.einsum("hrd,hkd->hrk", queries, key_part, preferred_element_type=jnp.float32)
            * score_scale
        )
        allowed = (key_pos[None, :] <= rows_pos[:, None])[None]
        weights = jnp.exp(jnp.where(allowed, scores - row_max, NEG))
        value_grad = jnp.einsum(
            "hrk,hrd->hkd",
            weights.astype(jnp.bfloat16),
            grad_scaled,
            preferred_element_type=jnp.float32,
        )
        prob_grad = jnp.einsum(
            "hrd,hkd->hrk", grad_scaled, value_part, preferred_element_type=jnp.float32
        )
        score_grad = (weights * (prob_grad - row_drift)).astype(jnp.bfloat16)
        grad_query = grad_query + jnp.einsum(
            "hrk,hkd->hrd", score_grad, key_part, preferred_element_type=jnp.float32
        )
        key_grad = jnp.einsum(
            "hrk,hrd->hkd", score_grad, queries, preferred_element_type=jnp.float32
        )
        return (grad_query, (key_grad, value_grad))

    grad_query, (key_grads, value_grads) = lax.scan(
        back_step,
        jnp.zeros((pair_heads, row_count, HD), jnp.float32),
        (key_split, value_split, pos_split),
    )
    key_grads = key_grads.transpose(0, 2, 1, 3).reshape(-1, pair_heads * HD) * score_scale
    value_grads = value_grads.transpose(0, 2, 1, 3).reshape(-1, pair_heads * HD)
    key_back, value_back = tuple(
        (
            part.astype(jnp.float32)
            for part in sent_together_2(
                (key_grads.astype(jnp.bfloat16), value_grads.astype(jnp.bfloat16)), "ctx", 0, 1
            )
        )
    )
    query_grad_rows = (
        (grad_query * score_scale)
        .reshape(pair_heads, group_size, tok_rows, HD)
        .transpose(2, 0, 1, 3)
        .reshape(tok_rows, query_heads, HD)
    )
    query_unrot = rotate_back(query_grad_rows, cosine_table, sine_table)
    query_gain_grad = jnp.sum(query_unrot * query_hat, axis=(0, 1))
    query_pre = (
        rms_backward(query_unrot * query_scale.astype(jnp.float32), query_hat, query_inv)
        .reshape(tok_rows, query_heads * HD)
        .astype(jnp.bfloat16)
    )
    key_unrot = rotate_back(key_back.reshape(tok_rows, pair_heads, HD), cosine_table, sine_table)
    key_gain_grad = jnp.sum(key_unrot * key_hat, axis=(0, 1))
    key_pre = (
        rms_backward(key_unrot * key_scale.astype(jnp.float32), key_hat, key_inv)
        .reshape(tok_rows, pair_heads * HD)
        .astype(jnp.bfloat16)
    )
    value_pre = value_back.astype(jnp.bfloat16)
    query_wgrad = dot_tn(hidden_one, query_pre)
    key_wgrad = dot_tn(hidden_one, key_pre)
    value_wgrad = dot_tn(hidden_one, value_pre)
    back_part = (
        dot_nt(query_pre, query_full) + dot_nt(key_pre, key_full) + dot_nt(value_pre, value_full)
    )
    back_one = row_reduce(back_part)
    normed_rows = own_rows(normed_one)
    gain_one_part = jnp.sum(back_one * normed_rows, axis=0)
    input_rows = grad_mid + rms_backward(
        back_one * norm_first.astype(jnp.float32), normed_rows, own_rows(inverse_one)
    )
    grad_input, gain_one_all, gain_two_all, query_gain_all, key_gain_all = (
        lax.all_gather(input_rows.astype(jnp.bfloat16), "tp", axis=0, tiled=True).astype(
            input_rows.dtype
        ),
        *tuple(
            (
                part.astype(jnp.float32)
                for part in in_one_piece(
                    (
                        gain_one_part[None].astype(jnp.bfloat16),
                        gain_two_grad[None].astype(jnp.bfloat16),
                        query_gain_grad[None].astype(jnp.bfloat16),
                        key_gain_grad[None].astype(jnp.bfloat16),
                    ),
                    "tp",
                    0,
                    1,
                )
            )
        ),
    )
    gain_one_grad = jnp.sum(gain_one_all, axis=0)
    gain_two_grad = jnp.sum(gain_two_all, axis=0)
    query_gain_sum = jnp.sum(query_gain_all, axis=0)
    key_gain_sum = jnp.sum(key_gain_all, axis=0)
    all_grads = (
        lax.psum_scatter(
            gain_one_grad.astype(jnp.bfloat16), "ctx", scatter_dimension=0, tiled=True
        ).astype(jnp.float32),
        *tuple(
            (
                part.astype(jnp.float32)
                for part in sent_together_2(
                    (
                        query_wgrad.astype(jnp.bfloat16),
                        key_wgrad.astype(jnp.bfloat16),
                        value_wgrad.astype(jnp.bfloat16),
                    ),
                    "ctx",
                    0,
                    1,
                )
            )
        ),
        lax.psum_scatter(
            query_gain_sum.astype(jnp.bfloat16), "ctx", scatter_dimension=0, tiled=True
        ).astype(jnp.float32),
        lax.psum_scatter(
            key_gain_sum.astype(jnp.bfloat16), "ctx", scatter_dimension=0, tiled=True
        ).astype(jnp.float32),
        lax.psum_scatter(
            output_grad.astype(jnp.bfloat16), "ctx", scatter_dimension=1, tiled=True
        ).astype(jnp.float32),
        lax.psum_scatter(
            gain_two_grad.astype(jnp.bfloat16), "ctx", scatter_dimension=0, tiled=True
        ).astype(jnp.float32),
        *tuple(
            (
                part.astype(jnp.float32)
                for part in sent_together_2(
                    (gate_grad.astype(jnp.bfloat16), up_grad.astype(jnp.bfloat16)), "ctx", 0, 1
                )
            )
        ),
        lax.psum_scatter(
            down_grad.astype(jnp.bfloat16), "ctx", scatter_dimension=1, tiled=True
        ).astype(jnp.float32),
    )
    return (
        block_output,
        grad_input,
        all_grads[0],
        all_grads[1],
        all_grads[2],
        all_grads[3],
        all_grads[4],
        all_grads[5],
        all_grads[6],
        all_grads[7],
        all_grads[8],
        all_grads[9],
        all_grads[10],
    )


def solution(mesh):
    in_specs = (
        P("ctx", None),
        P(),
        P("ctx"),
        P("ctx", "tp"),
        P("ctx", "tp"),
        P("ctx", "tp"),
        P("ctx"),
        P("ctx"),
        P("tp", "ctx"),
        P("ctx"),
        P("ctx", "tp"),
        P("ctx", "tp"),
        P("tp", "ctx"),
        P("ctx", None),
    )
    out_specs = (
        P("ctx", None),
        P("ctx", None),
        P("ctx"),
        P("ctx", "tp"),
        P("ctx", "tp"),
        P("ctx", "tp"),
        P("ctx"),
        P("ctx"),
        P("tp", "ctx"),
        P("ctx"),
        P("ctx", "tp"),
        P("ctx", "tp"),
        P("tp", "ctx"),
    )
    return jax.shard_map(body, mesh=mesh, in_specs=in_specs, out_specs=out_specs, check_vma=False)
```

profile of v0, /device:TPU:0, one launch (start us, length us, event | category | flops | bytes accessed | tf_op | source)
XLA Modules:
  0.0 982.1 jit_solution(982562461191315336)
XLA Ops:
  10.7 28.5 %all_gather.27 = bf16[1536,321]{1,0:T(8,128)(2,1)S(1)} all-gather(bf16[96,321]{1,0:T(8,128)(2,1)S(1)} %pad_maximum_fusion.7), channel_id=1, replica_groups=mesh['ctx'=16,'tp'=8] {'ctx'}, dimensions={0}, use_global_device_ids=true | all-gather | bytes 1047744 | tf_op jit(solution)/shard_map/all_gather | solution.py:49
  43.9 34.0 %all-reduce.7 = (bf16[64]{0:T(256)(128)(2,1)S(1)}, bf16[64]{0:T(256)(128)(2,1)}) all-reduce(bf16[64]{0:T(256)(128)(2,1)S(1)} %dynamic-update-slice, bf16[64]{0:T(256)(128)(2,1)S(1)} %dynamic-update-slice.1), channel_id=1, replica_groups=mesh['ctx'=16,'tp'=8] {'ctx'}, use_global_device_ids=true, to_apply=%add | all-reduce | flops 128 | bytes 512
  92.3 22.0 %all_gather.31 = bf16[192,1536]{0,1:T(8,128)(2,1)S(1)} all-gather(bf16[192,96]{0,1:T(8,128)(2,1)} %copy.99), channel_id=1, replica_groups=mesh['ctx'=16,'tp'=8] {'ctx'}, dimensions={1}, use_global_device_ids=true | all-gather | bytes 626688 | tf_op jit(solution)/shard_map/all_gather | solution.py:203
  114.3 15.2 %all-gather.6.cloned.1.call-done = bf16[8192,128]{0,1:T(8,128)(2,1)} async-done(((bf16[512,128]{0,1:T(8,128)(2,1)}), bf16[8192,128]{0,1:T(8,128)(2,1)}) %all-gather.6.cloned.1.call-update) | async-done | bytes 2097168 | tf_op jit(solution)/shard_map/all_gather | solution.py:62
  138.0 98.6 %while.30 = (s32[]{:T(128)}, f32[1,1536,1]{1,2,0:T(1,128)S(1)}, f32[1,1536,1]{1,2,0:T(1,128)S(1)}, f32[1,1536,64]{1,2,0:T(8,128)S(1)}, s32[8,1024]{1,0:T(8,128)}...) while((s32[]{:T(128)}, f32[1,1536,1]{1,2,0:T(1,128)S(1)}, ...), condition=%wide.region_6.7_spmd.clone, body=%wide.region_3.6_spmd.clone.sunk | while | flops 428123136 | bytes 45712536 | solution.py:156
  138.8 4.6 fusion.151
  143.5 4.6 fusion.155
  151.1 4.6 fusion.151
  155.8 4.6 fusion.155
  163.4 4.7 fusion.151
  168.1 4.6 fusion.155
  175.8 4.6 fusion.151
  180.5 4.7 fusion.155
  188.3 4.6 fusion.151
  192.9 4.6 fusion.155
  200.5 4.6 fusion.151
  205.2 4.6 fusion.155
  212.8 4.6 fusion.151
  217.5 4.6 fusion.155
  225.1 4.6 fusion.151
  229.8 4.7 fusion.155
  247.9 20.0 %all-to-all-done = bf16[8,64,1536]{2,1,0:T(8,128)(2,1)} async-done(((bf16[8,64,1536]{2,1,0:T(8,128)(2,1)}), bf16[8,64,1536]{2,1,0:T(8,128)(2,1)}, u32[]{:S(2)}, u32[]{:S(2)}) %all-to-all-start) | async-done | bytes 1572896 | tf_op jit(solution)/shard_map/all_to_all | solution.py:24
  272.9 26.3 %all_to_all.35 = bf16[8,64,1536]{2,1,0:T(8,128)(2,1)S(1)} all-to-all(bf16[8,64,1536]{2,1,0:T(8,128)(2,1)S(1)} %broadcast_in_dim.41), channel_id=1, replica_groups=mesh['ctx'=16,'tp'=8] {'tp'}, dimensions={0} | all-to-all | bytes 3145728 | tf_op jit(solution)/shard_map/all_to_all | solution.py:30
  306.7 6.1 multiply_convert_fusion.2
  312.8 5.2 fusion.59
  322.7 22.9 %all_to_all.36 = bf16[8,64,1536]{2,1,0:T(8,128)(2,1)S(1)} all-to-all(bf16[8,64,1536]{2,1,0:T(8,128)(2,1)S(1)} %bitcast.279), channel_id=1, replica_groups=mesh['ctx'=16,'tp'=8] {'tp'}, dimensions={0} | all-to-all | bytes 3145728 | tf_op jit(solution)/shard_map/all_to_all | solution.py:24
  353.7 17.9 %all-to-all-done.5 = bf16[8,64,1536]{2,1,0:T(8,128)(2,1)S(1)} async-done(((bf16[8,64,1536]{2,1,0:T(8,128)(2,1)}), bf16[8,64,1536]{2,1,0:T(8,128)(2,1)S(1)}, u32[]{:S(2)}, u32[]{:S(2)}) %all-to-all-start.5) | async-done | bytes 1572896 | tf_op jit(solution)/shard_map/all_to_all | solution.py:30
  374.1 163.2 %while.31 = (s32[]{:T(128)}, f32[1,1536,64]{1,2,0:T(8,128)}, f32[8,1,1024,64]{2,3,1,0:T(8,128)}, bf16[8,1,1024,64]{2,3,1,0:T(8,128)(2,1)}, s32[8,1024]{1,0:T(8,1...) while((s32[]{:T(128)}, f32[1,1536,64]{1,2,0:T(8,128)}, ...), condition=%wide.region_14.15_spmd.clone, body=%wide.region_13.14_spmd.clone.sunk | while | flops 1019412480 | bytes 33092372 | solution.py:328
  375.7 5.1 fusion.166
  396.0 5.1 fusion.166
  416.4 5.1 fusion.166
  436.8 5.1 fusion.166
  457.2 5.1 fusion.166
  477.6 5.1 fusion.166
  498.0 5.1 fusion.166
  518.4 5.1 fusion.166
  544.5 4.8 convolution_convert_fusion
  554.4 55.2 %reduce-scatter.12.cloned.1.call-done = bf16[512,128]{0,1:T(8,128)(2,1)} async-done(((bf16[8192,128]{0,1:T(8,128)(2,1)}), bf16[512,128]{0,1:T(8,128)(2,1)}) %reduce-scatter.12.cloned.1.call-update) | async-done | bytes 131088 | tf_op jit(solution)/shard_map/reduce_scatter | solution.py:72
  623.0 7.9 copy.120
  632.2 4.8 convolution_convert_fusion.3
  637.0 4.7 all-to-all-start.2
  645.1 17.1 %all-to-all-done.2 = bf16[8,64,1536]{2,1,0:T(8,128)(2,1)} async-done(((bf16[8,64,1536]{2,1,0:T(8,128)(2,1)}), bf16[8,64,1536]{2,1,0:T(8,128)(2,1)}, u32[]{:S(2)}, u32[]{:S(2)}) %all-to-all-start.2) | async-done | bytes 1572896 | tf_op jit(solution)/shard_map/all_to_all | solution.py:24
  669.8 16.7 %all-to-all-done.6 = bf16[8,64,1536]{2,1,0:T(8,128)(2,1)S(1)} async-done(((bf16[8,64,1536]{2,1,0:T(8,128)(2,1)}), bf16[8,64,1536]{2,1,0:T(8,128)(2,1)S(1)}, u32[]{:S(2)}, u32[]{:S(2)}) %all-to-all-start.6) | async-done | bytes 1572896 | tf_op jit(solution)/shard_map/all_to_all | solution.py:24
  697.7 72.1 %reduce-scatter.14.cloned.1.call-done = bf16[864,96]{0,1:T(8,128)(2,1)} async-done(((bf16[864,1536]{0,1:T(8,128)(2,1)}), bf16[864,96]{0,1:T(8,128)(2,1)}) %reduce-scatter.14.cloned.1.call-update) | async-done | bytes 165904 | tf_op jit(solution)/shard_map/reduce_scatter | solution.py:440
  771.6 28.2 %all-gather = bf16[8,1,3200]{2,1,0:T(2,128)(2,1)S(1)} all-gather(bf16[1,1,3200]{2,1,0:T(2,128)(2,1)S(1)} %bitcast.289), channel_id=1, replica_groups=mesh['ctx'=16,'tp'=8] {'tp'}, dimensions={0}, use_global_device_ids=true | all-gather | bytes 57600 | tf_op jit(solution)/shard_map/all_gather | solution.py:62
  800.0 34.6 %all-reduce.6 = (bf16[1536]{0:T(1024)(128)(2,1)S(1)}, bf16[64]{0:T(256)(128)(2,1)S(1)}, bf16[64]{0:T(256)(128)(2,1)S(1)}, bf16[1536]{0:T(1024)(128)(2,1)S(1)}) all-reduce(bf16[1536]{0:T(1024)(128)(2,1)S(1)} %get-tuple-element.354, bf16[64]{0:T(256)(128)(2,1)S(1)} %get-tuple-element.356, ...), channel_id=3, replica_groups=mesh['ctx'=16,'tp'=8] {'ctx'}, use_global_device_ids=true, to_apply=%region_25.26.clone | all-reduce | flops 3200 | bytes 12800
  844.1 85.7 %reduce-scatter.20.cloned.1.call-done = bf16[96,1728]{1,0:T(8,128)(2,1)} async-done(((bf16[1536,1728]{1,0:T(8,128)(2,1)}), bf16[96,1728]{1,0:T(8,128)(2,1)}) %reduce-scatter.20.cloned.1.call-update) | async-done | bytes 331792
  933.0 37.7 %all-gather.12.cloned.1.call-done = bf16[512,1536]{1,0:T(8,128)(2,1)} async-done(((bf16[64,1536]{1,0:T(8,128)(2,1)}), bf16[512,1536]{1,0:T(8,128)(2,1)}) %all-gather.12.cloned.1.call-update) | async-done | bytes 1572880 | tf_op jit(solution)/shard_map/all_gather | solution.py:377
  (502 shorter events, 281.5 us)
Async XLA Ops:
  7.2 32.2 %copy-start.4 = (bf16[512,1536]{1,0:T(8,128)(2,1)S(1)}, bf16[512,1536]{1,0:T(8,128)(2,1)}, u32[]{:S(2)}) copy-start(bf16[512,1536]{1,0:T(8,128)(2,1)} %param.18) | copy-start | bytes 4718596
  7.2 122.3 %all-gather.6.cloned.1.call-start = ((), (), s32[]{:S(2)}) async-start(), calls=%async_computation.12 | async-start | bytes 2228224 | tf_op jit(solution)/shard_map/all_gather | solution.py:62
  39.2 47.1 %copy-start.10 = (bf16[1536,321]{1,0:T(8,128)(2,1)}, bf16[1536,321]{1,0:T(8,128)(2,1)S(1)}, u32[]{:S(2)}) copy-start(bf16[1536,321]{1,0:T(8,128)(2,1)S(1)} %all_gather.27) | copy-start | bytes 2958340
  39.4 46.9 %copy-start.41 = (f32[1536]{0:T(1024)}, f32[1536]{0:T(1024)S(1)}, u32[]{:S(2)}) copy-start(f32[1536]{0:T(1024)S(1)} %convert_reduce_fusion.5) | copy-start | bytes 18436
  39.8 46.5 %copy-start.52 = (f32[512]{0:T(512)}, f32[512]{0:T(512)S(1)}, u32[]{:S(2)}) copy-start(f32[512]{0:T(512)S(1)} %add_rsqrt_fusion.2) | copy-start | bytes 6148
  40.6 44.8 %copy-start.16 = (f32[512,64]{0,1:T(8,128)}, f32[512,64]{0,1:T(8,128)S(1)}, u32[]{:S(2)}) copy-start(f32[512,64]{0,1:T(8,128)S(1)} %get-tuple-element.442) | copy-start | bytes 393220
  42.1 45.2 %copy-start.45 = (f32[512]{0:T(512)}, f32[512]{0:T(512)S(1)}, u32[]{:S(2)}) copy-start(f32[512]{0:T(512)S(1)} %add_rsqrt_fusion.1) | copy-start | bytes 6148
  80.2 7.2 copy-start.26
  80.2 7.2 copy-start.28
  81.0 8.9 copy-start.18
  81.0 8.9 copy-start.24
  82.7 188.1 %all-gather.8.cloned.1.call-start = ((), (), s32[]{:S(2)}) async-start(), calls=%async_computation.13 | async-start | bytes 5849088 | tf_op jit(solution)/shard_map/all_gather | solution.py:49
  85.5 221.2 %all-gather.10.cloned.1.call-start = ((), (), s32[]{:S(2)}) async-start(), calls=%async_computation.14 | async-start | bytes 2924544 | tf_op jit(solution)/shard_map/all_gather | solution.py:205
  87.4 26.9 %copy-start.8 = (f32[512,192]{0,1:T(8,128)}, f32[512,192]{0,1:T(8,128)S(1)}, u32[]{:S(2)}) copy-start(f32[512,192]{0,1:T(8,128)S(1)} %fusion.65) | copy-start | bytes 1179652
  241.5 26.4 %all-to-all-start = ((bf16[8,64,1536]{2,1,0:T(8,128)(2,1)}), bf16[8,64,1536]{2,1,0:T(8,128)(2,1)}, u32[]{:S(2)}, u32[]{:S(2)}) async-start(bf16[8,64,1536]{2,1,0:T(8,128)(2,1)} %bitcast.265), calls=%async_computation | async-start | bytes 3145728 | tf_op jit(solution)/shard_map/all_to_all | solution.py:24
  270.7 75.9 %copy-start.6 = (f32[64,1536]{1,0:T(8,128)}, f32[64,1536]{1,0:T(8,128)S(1)}, u32[]{:S(2)}) copy-start(f32[64,1536]{1,0:T(8,128)S(1)} %get-tuple-element.407) | copy-start | bytes 1179652
  272.7 26.6 %copy-start.47 = (bf16[1536,1729]{1,0:T(8,128)(2,1)S(1)}, bf16[1536,1729]{1,0:T(8,128)(2,1)}, u32[]{:S(2)}) copy-start(bf16[1536,1729]{1,0:T(8,128)(2,1)} %all-gather.8.cloned.1.call-done) | copy-start | bytes 15934468
  322.6 23.2 %copy-start.38 = (f32[1536]{0:T(1024)S(1)}, f32[1536]{0:T(1024)}, u32[]{:S(2)}) copy-start(f32[1536]{0:T(1024)} %copy-done.37) | copy-start | bytes 18436
  322.6 23.2 %copy-start.50 = (f32[64]{0:T(128)S(1)}, f32[64]{0:T(128)}, u32[]{:S(2)}) copy-start(f32[64]{0:T(128)} %copy-done.49) | copy-start | bytes 772
  349.0 22.6 %all-to-all-start.5 = ((bf16[8,64,1536]{2,1,0:T(8,128)(2,1)}), bf16[8,64,1536]{2,1,0:T(8,128)(2,1)S(1)}, u32[]{:S(2)}, u32[]{:S(2)}) async-start(bf16[8,64,1536]{2,1,0:T(8,128)(2,1)} %broadcast_in_dim.43), calls=%async_computation.5 | async-start | bytes 3145728 | tf_op jit(solution)/shard_map/all_to_all | solution.py:30
  352.6 21.2 %copy-start.44 = (f32[1536]{0:T(1024)S(1)}, f32[1536]{0:T(1024)}, u32[]{:S(2)}) copy-start(f32[1536]{0:T(1024)} %copy-done.43) | copy-start | bytes 18436
  352.6 257.0 %reduce-scatter.12.cloned.1.call-start = ((), (), s32[]{:S(2)}) async-start(), calls=%async_computation.15 | async-start | bytes 2228224 | tf_op jit(solution)/shard_map/reduce_scatter | solution.py:72
  374.1 6.7 copy-start.2
  374.1 6.6 copy-start.33
  394.4 6.6 copy-start.33
  414.9 6.6 copy-start.33
  435.3 6.6 copy-start.33
  455.7 6.6 copy-start.2
  455.7 6.6 copy-start.33
  542.1 154.1 %reduce-scatter.18.cloned.1.call-start = ((), (), s32[]{:S(2)}) async-start(), calls=%async_computation.19 | async-start | bytes 835584
  544.4 225.4 %reduce-scatter.14.cloned.1.call-start = ((), (), s32[]{:S(2)}) async-start(), calls=%async_computation.17 | async-start | bytes 2924544 | tf_op jit(solution)/shard_map/reduce_scatter | solution.py:440
  549.4 290.8 %reduce-scatter.16.cloned.1.call-start = ((), (), s32[]{:S(2)}) async-start(), calls=%async_computation.18 | async-start | bytes 1253376
  552.6 57.0 %copy-start.29 = (f32[512,32]{0,1:T(8,128)S(1)}, f32[512,32]{0,1:T(8,128)}, u32[]{:S(2)}) copy-start(f32[512,32]{0,1:T(8,128)} %copy-done.28) | copy-start | bytes 196612
  552.7 57.8 %copy-start.17 = (f32[512,64]{0,1:T(8,128)S(1)}, f32[512,64]{0,1:T(8,128)}, u32[]{:S(2)}) copy-start(f32[512,64]{0,1:T(8,128)} %copy-done.16) | copy-start | bytes 393220
  552.8 57.8 %copy-start.27 = (f32[512,32]{0,1:T(8,128)S(1)}, f32[512,32]{0,1:T(8,128)}, u32[]{:S(2)}) copy-start(f32[512,32]{0,1:T(8,128)} %copy-done.26) | copy-start | bytes 196612
  552.8 57.8 %copy-start.46 = (f32[512]{0:T(512)S(1)}, f32[512]{0:T(512)}, u32[]{:S(2)}) copy-start(f32[512]{0:T(512)} %copy-done.45) | copy-start | bytes 6148
  552.8 57.8 %copy-start.55 = (f32[64]{0:T(128)S(1)}, f32[64]{0:T(128)}, u32[]{:S(2)}) copy-start(f32[64]{0:T(128)} %copy-done.54) | copy-start | bytes 772
  615.4 314.4 %reduce-scatter.20.cloned.1.call-start = ((), (), s32[]{:S(2)}) async-start(), calls=%async_computation.20 | async-start | bytes 5849088
  637.0 25.2 %all-to-all-start.2 = ((bf16[8,64,1536]{2,1,0:T(8,128)(2,1)}), bf16[8,64,1536]{2,1,0:T(8,128)(2,1)}, u32[]{:S(2)}, u32[]{:S(2)}) async-start(bf16[8,64,1536]{2,1,0:T(8,128)(2,1)} %bitcast.278), calls=%async_computation.2 | async-start | bytes 3145728 | tf_op jit(solution)/shard_map/all_to_all | solution.py:24
  662.1 24.3 %all-to-all-start.6 = ((bf16[8,64,1536]{2,1,0:T(8,128)(2,1)}), bf16[8,64,1536]{2,1,0:T(8,128)(2,1)S(1)}, u32[]{:S(2)}, u32[]{:S(2)}) async-start(bf16[8,64,1536]{2,1,0:T(8,128)(2,1)} %bitcast.266), calls=%async_computation.7 | async-start | bytes 3145728 | tf_op jit(solution)/shard_map/all_to_all | solution.py:24
  665.7 305.0 %all-gather.12.cloned.1.call-start = ((), (), s32[]{:S(2)}) async-start(), calls=%async_computation.16 | async-start | bytes 1769472 | tf_op jit(solution)/shard_map/all_gather | solution.py:377
  668.0 19.9 %copy-start.7 = (f32[64,1536]{1,0:T(8,128)S(1)}, f32[64,1536]{1,0:T(8,128)}, u32[]{:S(2)}) copy-start(f32[64,1536]{1,0:T(8,128)} %copy-done.6) | copy-start | bytes 1179652
  668.0 19.9 %copy-start.15 = (f32[64,1536]{1,0:T(8,128)S(1)}, f32[64,1536]{1,0:T(8,128)}, u32[]{:S(2)}) copy-start(f32[64,1536]{1,0:T(8,128)} %copy-done.14) | copy-start | bytes 1179652
  668.0 19.9 %copy-start.39 = (f32[1536]{0:T(1024)S(1)}, f32[1536]{0:T(1024)}, u32[]{:S(2)}) copy-start(f32[1536]{0:T(1024)} %copy-done.37) | copy-start | bytes 18436
  668.0 19.9 %copy-start.51 = (f32[64]{0:T(128)S(1)}, f32[64]{0:T(128)}, u32[]{:S(2)}) copy-start(f32[64]{0:T(128)} %copy-done.49) | copy-start | bytes 772
  668.0 19.9 %copy-start.59 = (f32[64]{0:T(128)S(1)}, f32[64]{0:T(128)}, u32[]{:S(2)}) copy-start(f32[64]{0:T(128)} %copy-done.58) | copy-start | bytes 772
  689.9 81.6 %copy-start.61 = (bf16[64]{0:T(256)(128)(2,1)S(1)}, bf16[64]{0:T(256)(128)(2,1)}, u32[]{:S(2)}) copy-start(bf16[64]{0:T(256)(128)(2,1)} %get-tuple-element.347) | copy-start | bytes 388
  691.2 241.8 %all-to-all-start.3 = ((bf16[8,64,1536]{2,1,0:T(8,128)(2,1)}), bf16[8,64,1536]{2,1,0:T(8,128)(2,1)S(1)}, u32[]{:S(2)}, u32[]{:S(2)}) async-start(bf16[8,64,1536]{2,1,0:T(8,128)(2,1)} %broadcast_in_dim.42), calls=%async_computation.3 | async-start | bytes 3145728 | tf_op jit(solution)/shard_map/all_to_all | solution.py:30
  (71 other events, 263.3 us)
Sparse Core Ops, SparseCore 0:
  82.8 46.6 all-gather.5
  132.5 59.5 all-gather.7
  194.5 49.5 all-gather.9
  542.2 67.3 reduce-scatter.11
  613.2 76.9 reduce-scatter.17
  694.0 75.7 reduce-scatter.13
  773.6 66.4 reduce-scatter.15
  844.8 84.9 reduce-scatter.19
  931.5 39.2 all-gather.11
where the time goes:
time: 996 us; the launch traced here: 982 us
  waiting for transfers between devices  343 us (34%)
  matrix products  277 us (28%)
  blocking collectives  197 us (20%)
  local copies, waits for them, and re-layouts  67.7 us (7%)
  other arithmetic  60.1 us (6%)
  starting transfers between devices  20.5 us (2%)
  between operations  17.2 us (2%)
    unnamed x12, waiting for transfers between devices  90.9 us
    reduce_scatter x1, waiting for transfers between devices, body(): lax.psum_scatter(down_grad.astype(jnp.bfloat16), 'ctx', scatter_dimension...  72.1 us
    unnamed x2, blocking collectives  68.7 us
    reduce_scatter x1, waiting for transfers between devices, sent_together_2(): lax.psum_scatter(both, axis, scatter_dimension=dim, tiled=True)  55.2 us
    all_to_all x3, waiting for transfers between devices, sum_at_owner(): lax.all_to_all(blocks, axis, split_axis=0, concat_axis=0, tiled=True)  53.8 us
    dot_general x8, matrix products, back_step(): jnp.einsum('hrd,hkd->hrk', queries, key_part, preferred_element_type=jnp....  40.9 us
    all_gather x1, waiting for transfers between devices, body(): lax.all_gather(input_rows.astype(jnp.bfloat16), 'tp', axis=0, tiled=True)  37.7 us
    dot_general x8, matrix products, block_step(): jnp.einsum('hrd,hkd->hrk', queries, key_part, preferred_element_type=jnp....  37.2 us
  transfers between devices with their start and end apart: 14, of which 10 were waited for; matrix products, arithmetic and copies ran while one was open for 20% of the time, Pallas kernels for 0%

commit v1 on v0

v1 whole, which is shorter than its diff:
```python
import functools
import math

import jax
import jax.numpy as jnp
from jax import lax
from jax.experimental import pallas as pl
from jax.experimental.pallas import tpu as pltpu
from jax.sharding import PartitionSpec as P

HD = 64
EPS = 1e-05
THETA = 1000000.0
LOG2E = math.log2(math.e)
LN2 = math.log(2.0)
BF = jnp.bfloat16
F32 = jnp.float32
MESH = pl.DeviceIdType.MESH
VM = pl.BlockSpec(memory_space=pltpu.VMEM)
SM = pl.BlockSpec(memory_space=pltpu.SMEM)
HB = pl.BlockSpec(memory_space=pl.ANY)
DMA = pltpu.SemaphoreType.DMA


class Place:
    def __init__(self):
        self.c = lax.axis_index("ctx")
        self.t = lax.axis_index("tp")
        self.core = lax.rem(self.c, 2)
        self.x = lax.rem(self.c // 2, 4)
        self.zh = self.c // 8
        self.y = lax.rem(self.t, 4)
        self.zl = self.t // 4

    def ctx(self, dz, dx, other=0):
        core = self.core if not other else 1 - self.core
        zh = self.zh if not dz else 1 - self.zh
        return (zh * 4 + lax.rem(self.x + dx, 4)) * 2 + core

    def tp(self, dz, dy):
        zl = self.zl if not dz else 1 - self.zl
        return zl * 4 + lax.rem(self.y + dy, 4)


def greet(peers):
    barrier = pltpu.get_barrier_semaphore()
    for peer in peers:
        pl.semaphore_signal(barrier, inc=1, device_id=peer, device_id_type=MESH)
    pl.semaphore_wait(barrier, len(peers))


class Gather:
    def __init__(self, buf, rows, block, pair, right, left, sibling, send, recv, own=None):
        self.buf, self.rows, self.block = buf, rows, block
        self.to = {"z": pair, "r": right, "l": left, "s": sibling}
        self.send, self.recv, self.own = send, recv, own
        self.plan = {
            0: ((0, 0), 0, "z"),
            1: ((0, 0), 0, "r"),
            2: ((0, 0), 0, "l"),
            3: ((0, 3), 1, "r"),
            4: ((0, 1), 2, "l"),
            5: ((1, 0), 0, "r"),
            6: ((1, 0), 0, "l"),
            7: ((1, 3), 1, "r"),
            8: ((1, 1), 2, "l"),
            9: ((0, 0), 0, "s"),
            10: ((1, 0), 0, "s"),
            11: ((0, 3), 0, "s"),
            12: ((0, 1), 0, "s"),
            13: ((0, 2), 0, "s"),
            14: ((1, 3), 0, "s"),
            15: ((1, 1), 0, "s"),
            16: ((1, 2), 0, "s"),
        }
        self.count = 17 if sibling is not None else 9

    def copy(self, k):
        where, part, to = self.plan[k]
        rows = self.rows if part == 0 else self.rows // 2
        start = pl.multiple_of(self.block(*where) * self.rows, self.rows)
        if part == 2:
            start = pl.multiple_of(start + rows, rows)
        there = self.buf.at[pl.ds(start, rows)]
        here = there
        if where == (0, 0) and self.own is not None:
            here = self.own
        return pltpu.make_async_remote_copy(
            src_ref=here,
            dst_ref=there,
            send_sem=self.send.at[k],
            recv_sem=self.recv.at[k],
            device_id=self.to[to],
            device_id_type=MESH,
        )

    def go(self, *which):
        for k in which:
            if k < self.count:
                self.copy(k).start()

    def got(self, *which):
        for k in which:
            if k < self.count:
                self.copy(k).wait_recv()

    def begin(self):
        self.go(0, 1, 2, 9)

    def near(self):
        self.got(1)
        self.go(3, 11)
        self.got(2)
        self.go(4, 12)

    def pair(self):
        self.got(0)
        self.go(5, 6, 10)

    def far(self):
        self.got(5)
        self.go(7, 14)
        self.got(6)
        self.go(8, 15)
        self.got(3, 4)
        self.go(13)

    def last(self):
        self.got(7, 8)
        self.go(16)

    def sent(self):
        for k in range(self.count):
            self.copy(k).wait_send()

    def end(self):
        self.got(*range(9, 17))
        self.sent()


def ctx_neighbours(me):
    return (
        (me.ctx(1, 0), me.t),
        (me.ctx(0, 1), me.t),
        (me.ctx(0, 3), me.t),
        (me.ctx(0, 0, 1), me.t),
    )


def tp_neighbours(me):
    return (me.c, me.tp(1, 0)), (me.c, me.tp(0, 1)), (me.c, me.tp(0, 3))


def rms_inverse(value):
    return lax.rsqrt(jnp.mean(value * value, axis=-1, keepdims=True) + EPS)


def column_inverse(value):
    return lax.rsqrt(jnp.mean(value * value, axis=0, keepdims=True) + EPS)


def gain_columns(wq):
    total = wq[0:64, 256:384].astype(F32)
    for k in range(1, 16):
        total += wq[96 * k : 96 * k + 64, 256:384].astype(F32)
    return total[:, 64:65], total[:, 65:66]


def dot(a, b):
    return jnp.dot(a, b, preferred_element_type=F32)


def dot_nt(a, b):
    return lax.dot_general(a, b, (((1,), (1,)), ((), ())), preferred_element_type=F32)


def dot_tn(a, b):
    return lax.dot_general(a, b, (((0,), (0,)), ((), ())), preferred_element_type=F32)


PAIRS = ((0, 0), (0, 3), (0, 1), (1, 0), (0, 2), (1, 3), (1, 1), (1, 2))


def pair_of(me, step):
    dz = sum(jnp.where(step == k, p[0], 0) for k, p in enumerate(PAIRS) if p[0])
    dx = sum(jnp.where(step == k, p[1], 0) for k, p in enumerate(PAIRS) if p[1])
    zh = lax.rem(me.zh + dz, 2)
    return (zh * 4 + lax.rem(me.x + dx, 4)) * 2


def forward_kernel(
    kb, x_ref, wq_s, wf_s, cos_ref, sin_ref,
    wq, wf, wo, kv, qt, raw, att, sums, normed,
    acc, s_w, r_w, s_f, r_f, s_o, r_o, s_k, r_k, s_a, r_a, s_l,
):
    me = Place()
    ctx_z, ctx_r, ctx_l, ctx_s = ctx_neighbours(me)
    tp_z, tp_r, tp_l = tp_neighbours(me)
    tokens = x_ref.shape[0]
    greet([ctx_z, ctx_r, ctx_l, ctx_s, tp_z, tp_r, tp_l])
    weights = Gather(wq, 96, me.ctx, ctx_z, ctx_r, ctx_l, ctx_s, s_w, r_w, own=wq_s)
    feed = Gather(wf, 96, me.ctx, ctx_z, ctx_r, ctx_l, ctx_s, s_f, r_f, own=wf_s)
    keys = Gather(kv, tokens, me.ctx, ctx_z, ctx_r, ctx_l, ctx_s, s_k, r_k)
    outw = Gather(
        wo, 96, lambda dz, dy: me.tp(dz, dy) * 2 + me.core, tp_z, tp_r, tp_l, ctx_s, s_o, r_o
    )
    share = Gather(att, 192, me.tp, tp_z, tp_r, tp_l, None, s_a, r_a)

    weights.begin()
    mine = pl.multiple_of(me.c * 96, 96)
    keep = [
        pltpu.make_async_copy(wq_s, wq.at[pl.ds(mine, 96)], s_l.at[0]),
        pltpu.make_async_copy(wf_s, wf.at[pl.ds(mine, 96)], s_l.at[1]),
    ]
    for k in keep:
        k.start()

    def norm_rows(i, carry):
        rows = pl.ds(pl.multiple_of(i * 64, 64), 64)
        value = x_ref[rows].astype(F32)
        normed[rows] = (value * rms_inverse(value)).astype(BF)
        return carry

    lax.fori_loop(0, tokens // 64, norm_rows, 0)
    weights.near()
    weights.pair()
    weights.far()
    weights.last()
    keep[0].wait()
    weights.end()

    def project(i, carry):
        cols = pl.ds(pl.multiple_of(i * 256, 256), 256)
        raw[:, cols] = dot(normed[cols], wq[:, 0:384]).T
        return carry

    lax.fori_loop(0, tokens // 256, project, 0)
    query_gain, key_gain = gain_columns(wq)
    cosine, sine = cos_ref[...], sin_ref[...]

    def turned(value, gain):
        hat = value * column_inverse(value) * gain
        a, b = hat[:32], hat[32:]
        return jnp.concatenate([a * cosine - b * sine, b * cosine + a * sine], axis=0)

    both = jnp.concatenate([turned(raw[192:256], key_gain), raw[256:320]], axis=0)
    kv[pl.ds(pl.multiple_of(me.c * tokens, tokens), tokens)] = both.T.astype(BF)
    keys.begin()
    qt[64:128] = jnp.zeros((64, 3 * tokens), BF)
    for h in range(3):
        rows = raw[64 * h : 64 * h + 64]
        qt[0:64, h * tokens : (h + 1) * tokens] = (
            turned(rows, query_gain) * (LOG2E / 8.0)
        ).astype(BF)
    heads = wq[:, 384:640].T
    wo[pl.ds(pl.multiple_of(me.t * 192 + me.core * 96, 96), 96)] = jnp.where(
        me.core == 0, heads[0:96], heads[96:192]
    )
    outw.begin()
    feed.begin()
    acc[...] = jnp.zeros_like(acc)
    ones = jnp.concatenate([jnp.ones((1, 1024), BF), jnp.zeros((15, 1024), BF)], axis=0)
    apart = lax.broadcasted_iota(jnp.int32, (256, 256), 0) - lax.broadcasted_iota(
        jnp.int32, (256, 256), 1
    )

    def key_step(step, carry):
        @pl.when(step == 0)
        def _():
            keys.got(9)

        @pl.when(step == 1)
        def _():
            keys.near()
            keys.got(11)

        @pl.when(step == 2)
        def _():
            keys.pair()
            keys.got(12)

        @pl.when(step == 3)
        def _():
            keys.got(10)
            outw.near()

        @pl.when(step == 4)
        def _():
            keys.far()
            outw.pair()
            keys.got(13)

        @pl.when(step == 5)
        def _():
            keys.got(14)

        @pl.when(step == 6)
        def _():
            keys.last()
            outw.far()
            keys.got(15)

        @pl.when(step == 7)
        def _():
            keys.got(16)

        first = pair_of(me, step)
        rows = kv[pl.ds(pl.multiple_of(first * tokens, 1024), 1024), :]
        scores = dot(rows, qt[...])
        parts = []
        for a in range(4):
            line = []
            for b in range(6):
                sub = scores[a * 256 : a * 256 + 256, b * 256 : b * 256 + 256]
                seen = apart <= kb[me.c * 2 + b % 2] - kb[first * 2 + a]
                line.append(jnp.where(seen, jnp.exp2(sub), 0.0).astype(BF))
            parts.append(jnp.concatenate(line, axis=1))
        weight = jnp.concatenate(parts, axis=0)
        left = jnp.concatenate([rows.T[64:128], ones], axis=0)
        acc[...] += dot(left, weight)
        return carry

    lax.fori_loop(0, 8, key_step, 0)
    total = acc[64:65, :]
    sums[...] = jnp.broadcast_to(total, sums.shape)
    own = pl.multiple_of(me.t * 192, 192)
    for h in range(3):
        cols = slice(h * tokens, (h + 1) * tokens)
        att[pl.ds(own + 64 * h, 64)] = (acc[0:64, cols] / total[:, cols]).astype(BF)
    share.begin()
    outw.last()
    feed.near()
    share.near()
    share.pair()
    feed.pair()
    share.far()
    share.last()
    feed.far()
    keys.sent()
    share.sent()
    outw.end()
    feed.last()
    keep[1].wait()
    feed.end()


def forward_part(kb, block_input, wq_s, wf_s, cosine, sine):
    tokens = block_input.shape[0]
    shapes = [
        jax.ShapeDtypeStruct((1536, 640), BF),
        jax.ShapeDtypeStruct((1536, wf_s.shape[1]), BF),
        jax.ShapeDtypeStruct((1536, 1536), BF),
        jax.ShapeDtypeStruct((16 * tokens, 128), BF),
        jax.ShapeDtypeStruct((128, 3 * tokens), BF),
        jax.ShapeDtypeStruct((384, tokens), F32),
        jax.ShapeDtypeStruct((1536, tokens), BF),
        jax.ShapeDtypeStruct((8, 3 * tokens), F32),
        jax.ShapeDtypeStruct((tokens, 1536), BF),
    ]
    return pl.pallas_call(
        forward_kernel,
        out_shape=shapes,
        in_specs=[SM, VM, VM, HB, VM, VM],
        out_specs=[VM, HB, VM, VM, VM, VM, VM, VM, VM],
        scratch_shapes=[pltpu.VMEM((80, 3 * tokens), F32)]
        + [DMA((17,))] * 8
        + [DMA((9,))] * 2
        + [DMA((2,))],
        name="forward_part",
        compiler_params=pltpu.CompilerParams(
            collective_id=0, has_side_effects=True, vmem_limit_bytes=58 << 20
        ),
    )(kb, block_input, wq_s, wf_s, cosine, sine)


def backward_keys(kb, qt_ref, gt_ref, drift_ref, kv_ref, dq_ref, out_ref):
    me = Place()
    apart = lax.broadcasted_iota(jnp.int32, (256, 256), 0) - lax.broadcasted_iota(
        jnp.int32, (256, 256), 1
    )
    dq_ref[...] = jnp.zeros_like(dq_ref)

    def key_step(j, carry):
        rows = kv_ref[pl.ds(pl.multiple_of(j * 1024, 1024), 1024), :]
        scores = dot(rows, qt_ref[...])
        slopes = dot(rows, gt_ref[...])
        parts, grads = [], []
        for a in range(4):
            line, grad_line = [], []
            for b in range(6):
                at = (slice(a * 256, a * 256 + 256), slice(b * 256, b * 256 + 256))
                seen = apart <= kb[me.c * 2 + b % 2] - kb[j * 4 + a]
                weight = jnp.where(seen, jnp.exp2(scores[at]), 0.0)
                line.append(weight.astype(BF))
                grad_line.append((weight * (slopes[at] - drift_ref[0:1, at[1]])).astype(BF))
            parts.append(jnp.concatenate(line, axis=1))
            grads.append(jnp.concatenate(grad_line, axis=1))
        weight = jnp.concatenate(parts, axis=0)
        grad = jnp.concatenate(grads, axis=0)
        dq_ref[...] += dot(rows.T[0:64], grad)
        key_grad = dot_nt(qt_ref[0:64], grad) * LN2
        value_grad = dot_nt(gt_ref[64:128], weight)
        both = jnp.concatenate([key_grad, value_grad], axis=0).astype(BF)
        out_ref[2 * j] = both[:, 0:512]
        out_ref[2 * j + 1] = both[:, 512:1024]
        return carry

    lax.fori_loop(0, 8, key_step, 0)


def backward_part(kb, qt, gt, drift, kv):
    return pl.pallas_call(
        backward_keys,
        out_shape=[
            jax.ShapeDtypeStruct((64, 1536), F32),
            jax.ShapeDtypeStruct((16, 128, 512), BF),
        ],
        in_specs=[SM, VM, VM, VM, VM],
        out_specs=[VM, VM],
        name="backward_keys",
        compiler_params=pltpu.CompilerParams(vmem_limit_bytes=58 << 20),
    )(kb, qt, gt, drift, kv)


def rotary_tables(places, width):
    half_width = width // 2
    freq_table = THETA ** (-(jnp.arange(half_width, dtype=F32) * 2.0 / width))
    angles = freq_table[:, None] * places.astype(F32)[None, :]
    return jnp.cos(angles), jnp.sin(angles)


def cut_along(shard, dim, devices):
    dims = shard.shape
    blocks = shard.reshape(*dims[:dim], devices, dims[dim] // devices, *dims[dim + 1 :])
    return jnp.moveaxis(blocks, dim, 0)


def row_reduce(partial):
    blocks = cut_along(partial.astype(BF), 0, lax.axis_size("tp"))
    arrived = lax.all_to_all(blocks, "tp", split_axis=0, concat_axis=0, tiled=True)
    return arrived.astype(F32).sum(axis=0)


def row_collect(rows):
    return lax.all_gather(rows, "tp", axis=0, tiled=True)


def body(
    block_input, positions, attn_gain, query_weight, key_weight, value_weight, query_gain,
    key_gain, output_weight, ffn_gain, gate_weight, up_weight, down_weight, out_cotangent,
):
    tokens = block_input.shape[0]
    c, t = lax.axis_index("ctx"), lax.axis_index("tp")
    gain_one = attn_gain.astype(F32)[:, None]
    gain_two = ffn_gain.astype(F32)[:, None]
    kb = positions.reshape(32, 256)[:, 0]
    own_pos = lax.dynamic_slice_in_dim(positions, c * tokens, tokens, 0)
    cosine, sine = rotary_tables(own_pos, HD)
    spot = (jnp.arange(96)[:, None] == 4 * c + jnp.arange(4)[None, :]).astype(F32)
    head_gains = jnp.stack(
        [spot @ query_gain.astype(F32), spot @ key_gain.astype(F32)], axis=1
    ).astype(BF)

    def lifted(weight, gain):
        return (weight.astype(F32) * gain).astype(BF)

    def padded(weight, width):
        return jnp.pad(weight, ((0, 0), (0, width - weight.shape[1])))

    wq_s = jnp.concatenate(
        [
            lifted(query_weight, gain_one),
            lifted(key_weight, gain_one),
            lifted(value_weight, gain_one),
            padded(head_gains, 64),
            output_weight.T,
            jnp.zeros((96, 64), BF),
        ],
        axis=1,
    )
    wf_s = jnp.concatenate(
        [
            padded(lifted(gate_weight, gain_two), 896),
            padded(lifted(up_weight, gain_two), 896),
            padded(down_weight.T, 896),
        ],
        axis=1,
    )
    wq, wf, wo, kv, qt, raw, att, sums, normed = forward_part(
        kb, block_input, wq_s, wf_s, cosine, sine
    )
    x = block_input.astype(F32)
    mid = x + dot_tn(att, wo)
    inv_two = rms_inverse(mid)
    normed_two = mid * inv_two
    low_two = normed_two.astype(BF)
    gate_full, up_full, down_full = wf[:, 0:896], wf[:, 896:1792], wf[:, 1792:2688]
    gate = dot(low_two, gate_full)
    up = dot(low_two, up_full)
    sig = jax.nn.sigmoid(gate)
    act = (gate * sig * up).astype(BF)
    ffn_part = dot_nt(act, down_full)
    grad_act = dot(out_cotangent, down_full)
    grad_gate = (grad_act * up * sig * (1.0 + gate * (1.0 - sig))).astype(BF)
    grad_up = (grad_act * gate * sig).astype(BF)
    down_grad = dot_tn(out_cotangent, act)
    gate_grad = dot_tn(low_two, grad_gate)
    up_grad = dot_tn(low_two, grad_up)
    back_two = dot_nt(grad_gate, gate_full) + dot_nt(grad_up, up_full)
    gain_two_part = jnp.sum(back_two * normed_two, axis=0)
    pull = jnp.mean(back_two * normed_two, axis=-1, keepdims=True)
    share_mid = (
        out_cotangent.astype(F32) * 0.125 + inv_two * (back_two - normed_two * pull)
    ).astype(BF)
    grad_att = row_reduce(dot_nt(wo, share_mid))
    rows = tokens // 8

    def own_rows(a):
        return lax.dynamic_slice_in_dim(a, t * rows, rows, 0)

    block_output = row_collect((own_rows(mid) + row_reduce(ffn_part)).astype(BF))
    grad_mid = row_reduce(share_mid)
    grad_branch = row_collect(grad_mid.astype(BF))
    own_att = lax.dynamic_slice_in_dim(att, t * 192, 192, 0)
    out_grad = lax.dot_general(
        grad_branch, own_att, (((0,), (1,)), ((), ())), preferred_element_type=F32
    )
    total = sums[0].reshape(3, 1, tokens)
    heads = grad_att.reshape(3, HD, tokens)
    drift = jnp.sum(heads * own_att.reshape(3, HD, tokens).astype(F32), axis=1, keepdims=True) / total
    scaled = (heads / total).astype(BF).transpose(1, 0, 2).reshape(HD, 3 * tokens)
    gt = jnp.concatenate([jnp.zeros_like(scaled), scaled], axis=0)
    drift8 = jnp.broadcast_to(drift.reshape(1, 3 * tokens), (8, 3 * tokens))
    grad_q, grad_kv = backward_part(kb, qt, gt, drift8, kv)
    own_kv = lax.psum_scatter(
        grad_kv.reshape(16 * 128, 512), "ctx", scatter_dimension=0, tiled=True
    ).astype(F32)
    gains = wq.reshape(16, 96, 640)[:, :64, 320:322].astype(F32).sum(axis=0)

    def unturn(grad, value, gain):
        hat_inv = column_inverse(value)
        hat = value * hat_inv
        a, b = grad[:32], grad[32:]
        plain = jnp.concatenate([a * cosine + b * sine, b * cosine - a * sine], axis=0)
        gain_grad = jnp.sum(plain * hat, axis=1)
        pulled = plain * gain
        return gain_grad, (
            hat_inv * (pulled - hat * jnp.mean(pulled * hat, axis=0, keepdims=True))
        ).astype(BF)

    parts, qg_grad = [], 0.0
    for h in range(3):
        g, back = unturn(
            grad_q[:, h * tokens : (h + 1) * tokens] * 0.125, raw[64 * h : 64 * h + 64], gains[:, 0:1]
        )
        qg_grad += g
        parts.append(back)
    kg_grad, key_back = unturn(own_kv[0:64], raw[192:256], gains[:, 1:2])
    pre = jnp.concatenate(parts + [key_back, own_kv[64:128].astype(BF)], axis=0)
    qkv_grad = lax.dot_general(normed, pre, (((0,), (1,)), ((), ())), preferred_element_type=F32)
    back_part = lax.dot_general(
        pre, wq[:, 0:320], (((0,), (1,)), ((), ())), preferred_element_type=F32
    )
    inv_one = rms_inverse(x)
    normed_one = x * inv_one
    gain_one_part = jnp.sum(back_part * normed_one, axis=0)
    back_one = row_reduce(back_part)
    own_normed = own_rows(normed_one)
    grad_rows = grad_mid + own_rows(inv_one) * (
        back_one - own_normed * jnp.mean(back_one * own_normed, axis=-1, keepdims=True)
    )
    grad_input = row_collect(grad_rows.astype(BF)).astype(F32)
    vectors = jnp.concatenate([gain_one_part, gain_two_part, qg_grad, kg_grad])
    vectors = lax.psum(vectors, ("ctx", "tp"))
    weight_grads = jnp.concatenate([qkv_grad, out_grad, gate_grad, up_grad, down_grad], axis=1)
    own = lax.psum_scatter(
        weight_grads.astype(BF), "ctx", scatter_dimension=0, tiled=True
    ).astype(F32)

    def mine(a, width):
        return lax.dynamic_slice_in_dim(a, c * width, width, 0)

    return (
        block_output,
        grad_input,
        mine(vectors[0:1536], 96) / gain_one[:, 0],
        own[:, 0:192] * gain_one,
        own[:, 192:256] * gain_one,
        own[:, 256:320] * gain_one,
        mine(vectors[3072:3136], 4),
        mine(vectors[3136:3200], 4),
        own[:, 320:512].T,
        mine(vectors[1536:3072], 96) / gain_two[:, 0],
        own[:, 512 : 512 + 864] * gain_two,
        own[:, 1408 : 1408 + 864] * gain_two,
        own[:, 2304 : 2304 + 864].T,
    )


def solution(mesh):
    in_specs = (
        P("ctx", None),
        P(),
        P("ctx"),
        P("ctx", "tp"),
        P("ctx", "tp"),
        P("ctx", "tp"),
        P("ctx"),
        P("ctx"),
        P("tp", "ctx"),
        P("ctx"),
        P("ctx", "tp"),
        P("ctx", "tp"),
        P("tp", "ctx"),
        P("ctx", None),
    )
    out_specs = (
        P("ctx", None),
        P("ctx", None),
        P("ctx"),
        P("ctx", "tp"),
        P("ctx", "tp"),
        P("ctx", "tp"),
        P("ctx"),
        P("ctx"),
        P("tp", "ctx"),
        P("ctx"),
        P("ctx", "tp"),
        P("ctx", "tp"),
        P("tp", "ctx"),
    )
    return jax.shard_map(body, mesh=mesh, in_specs=in_specs, out_specs=out_specs, check_vma=False)
```

time: 996 us -> 573 us (0.58); the launches traced: 982 us -> 571 us
  matrix products: 277 us -> 45.9 us
  waiting for transfers between devices: 343 us -> 203 us
  Pallas kernels: 0 us -> 127 us
  blocking collectives: 197 us -> 96.7 us
  local copies, waits for them, and re-layouts: 67.7 us -> 32.7 us
  other arithmetic: 60.1 us -> 36 us
    dot_general x77 -> x16, matrix products: 277 us -> 45.9 us  [the longest x4 18.4 us: dot_tn(): lax.dot_general(a, b, (((0,), (0,)), ((), ())), preferred_element_type=F32)]
    pallas_call x0 -> x2, Pallas kernels: none -> 127 us  [the longest x1 89.3 us: forward_part(): pl.pallas_call(forward_kernel, out_shape=shapes, in_specs=[SM, VM, VM, HB...]
    unnamed x12 -> x5, waiting for transfers between devices: 90.9 us -> 0.59 us
    all_gather x3 -> x0, blocking collectives: 78.7 us -> none  [the longest x1 28.5 us: sent_together(): whole = lax.all_gather(both, axis, axis=dim, tiled=True)]
    unnamed x2 -> x0, blocking collectives: 68.7 us -> none
    psum x0 -> x1, blocking collectives: none -> 63.9 us  [body(): vectors = lax.psum(vectors, ('ctx', 'tp'))]
    all_to_all x5 -> x3, waiting for transfers between devices: 71.6 us -> 37.4 us  [row_reduce(): lax.all_to_all(blocks, 'tp', split_axis=0, concat_axis=0, tiled=True)]
    all_gather x4 -> x3, waiting for transfers between devices: 52.9 us -> 20 us  [row_collect(): return lax.all_gather(rows, 'tp', axis=0, tiled=True)]
  transfers between devices with their start and end apart: 14 -> 8, of which waited for: 10 -> 5; matrix products, arithmetic and copies ran while one was open for 20% -> 11% of each run, Pallas kernels for 0% -> 0%
where the time goes in v1:
time: 573 us; the launch traced here: 571 us
  waiting for transfers between devices  203 us (35%)
  Pallas kernels  127 us (22%)
  blocking collectives  96.7 us (17%)
  matrix products  45.9 us (8%)
  other arithmetic  36 us (6%)
  local copies, waits for them, and re-layouts  32.7 us (6%)
  starting transfers between devices  14.9 us (3%)
  between operations  14.4 us (3%)
    pallas_call x1, Pallas kernels, forward_part(): pl.pallas_call(forward_kernel, out_shape=shapes, in_specs=[SM, VM, VM, HB...  89.3 us
    reduce_scatter x1, waiting for transfers between devices, body(): lax.psum_scatter(weight_grads.astype(BF), 'ctx', scatter_dimension=0, til...  83.9 us
    psum x1, blocking collectives, body(): vectors = lax.psum(vectors, ('ctx', 'tp'))  63.9 us
    reduce_scatter x1, waiting for transfers between devices, body(): lax.psum_scatter(grad_kv.reshape(16 * 128, 512), 'ctx', scatter_dimension...  60.9 us
    pallas_call x1, Pallas kernels, backward_part(): pl.pallas_call(backward_keys, out_shape=[jax.ShapeDtypeStruct((64, 1536),...  38.1 us
    all_to_all x3, waiting for transfers between devices, row_reduce(): lax.all_to_all(blocks, 'tp', split_axis=0, concat_axis=0, tiled=True)  37.4 us
    all_to_all x1, blocking collectives, row_reduce(): lax.all_to_all(blocks, 'tp', split_axis=0, concat_axis=0, tiled=True)  32.7 us
    all_gather x3, waiting for transfers between devices, row_collect(): return lax.all_gather(rows, 'tp', axis=0, tiled=True)  20 us
  transfers between devices with their start and end apart: 8, of which 5 were waited for; matrix products, arithmetic and copies ran while one was open for 11% of the time, Pallas kernels for 0%

profile of v1, /device:TPU:0, one launch (start us, length us, event | category | flops | bytes accessed | tf_op | source)
XLA Modules:
  0.0 570.7 jit_solution(4089321792572773015)
XLA Ops:
  15.9 1.0 multiply_sine_fusion
  16.9 1.1 multiply_convert_fusion.3
  18.0 1.7 fusion.28.wf_s
  20.5 89.3 %forward_part.1 = (bf16[1536,640]{1,0:T(8,128)(2,1)}, bf16[1536,2688]{1,0:T(8,128)(2,1)}, bf16[1536,1536]{1,0:T(8,128)(2,1)}, bf16[8192,128]{1,0:T(8,128)(2,1)},...) custom-call(s32[32]{0:T(128)} %slice_reduce_fusion.2.kb, ...), custom_call_target="tpu_custom_call" | custom-call | tf_op jit(solution)/shard_map/forward_part/pallas_call | solution.py:360
  109.9 6.4 %multiply_reduce_fusion.1 = (f32[512]{0:T(512)S(1)}, f32[512,1536]{1,0:T(8,128)S(1)}) fusion(bf16[1536,512]{1,0:T(8,128)(2,1)} %get-tuple-element.24, bf16[1536,1536]{1,0:T(8,128)(2,1)} %get-tuple-element.25, bf16[512,1536]{1,0:T(8,128)(2,1)} %x_ref.1), kind=kOutput, calls=%fused_computation.14 | convolution fusion | flops 2419064320 | bytes 11012096 | tf_op jit(solution)/shard_map/dot_general | solution.py:178
  116.6 1.8 fusion.6
  118.6 1.8 fusion.2
  120.4 3.5 fusion.16
  123.9 1.8 fusion.8
  125.8 2.6 fusion.29
  128.4 0.9 add_convert_fusion
  129.4 3.8 convolution_convert_fusion.3
  133.2 4.7 all-to-all-start.2
  138.0 1.6 constant_dynamic-slice_fusion
  139.6 20.3 %all-to-all-done.2 = bf16[8,192,512]{2,1,0:T(8,128)(2,1)} async-done(((bf16[8,192,512]{2,1,0:T(8,128)(2,1)}), bf16[8,192,512]{2,1,0:T(8,128)(2,1)}, u32[]{:S(2)}, u32[]{:S(2)}) %all-to-all-start.2) | async-done | bytes 1572896 | tf_op jit(solution)/shard_map/all_to_all | solution.py:440
  160.0 1.7 convert_reduce_fusion.1
  161.8 1.4 divide_reduce_fusion
  164.8 1.3 broadcast_in_dim.8.drift_ref
  166.1 38.1 %backward_keys.1 = (f32[64,1536]{1,0:T(8,128)}, bf16[16,128,512]{2,1,0:T(8,128)(2,1)}) custom-call(s32[32]{0:T(128)} %slice_reduce_fusion.2.kb, bf16[128,1536]{1,0:T(8,128)(2,1)} %get-tuple-element.28.qt_ref, bf16[128,1536]{1,0:T(8,128)(2,1)} %concatenate.33.gt_ref, f32[8,1536]{1,0:T(8,128)} %broadcast_in_dim.8.drift_ref, ...), custom_call_target="tpu_custom_call" | custom-call | tf_op jit(solution)/shard_map/backward_keys/pallas_call | solution.py:412
  204.2 5.2 all-to-all-start.1
  209.5 1.2 convert_reduce_fusion.4
  211.3 1.0 multiply_reduce_fusion.8
  212.3 1.8 fusion
  214.8 60.9 %reduce-scatter.3.cloned.1.call-done = bf16[128,512]{1,0:T(8,128)(2,1)} async-done(((bf16[2048,512]{1,0:T(8,128)(2,1)}), bf16[128,512]{1,0:T(8,128)(2,1)}) %reduce-scatter.3.cloned.1.call-update) | async-done | bytes 131088 | tf_op jit(solution)/shard_map/reduce_scatter | solution.py:535
  275.7 1.0 convert_element_type.168
  276.7 1.1 fusion.53
  277.8 1.8 multiply_reduce_fusion.3
  281.5 4.7 multiply_reduce_fusion
  286.2 4.5 all-to-all-start.3
  291.5 1.7 convert_reduce_fusion.2
  293.2 17.1 %all-to-all-done.3 = bf16[8,64,1536]{2,1,0:T(8,128)(2,1)} async-done(((bf16[8,64,1536]{2,1,0:T(8,128)(2,1)}), bf16[8,64,1536]{2,1,0:T(8,128)(2,1)}, u32[]{:S(2)}, u32[]{:S(2)}) %all-to-all-start.3) | async-done | bytes 1572896 | tf_op jit(solution)/shard_map/all_to_all | solution.py:440
  310.2 1.7 convert_reduce_fusion
  311.9 1.1 multiply_reduce_fusion.2
  313.0 1.8 fusion.65
  314.9 3.9 convolution_convert_fusion.4
  318.8 32.7 %all_to_all.20 = bf16[8,64,1536]{2,1,0:T(8,128)(2,1)S(1)} all-to-all(bf16[8,64,1536]{2,1,0:T(8,128)(2,1)S(1)} %bitcast.87), channel_id=1, replica_groups=mesh['ctx'=16,'tp'=8] {'tp'}, dimensions={0} | all-to-all | bytes 3145728 | tf_op jit(solution)/shard_map/all_to_all | solution.py:440
  353.4 5.2 convolution_convert_fusion.1
  358.6 3.4 convolution_convert_fusion.2
  362.0 3.4 fusion.1
  367.0 1.9 convolution_convert_fusion.6
  369.2 14.6 %concatenate.40 = bf16[1536,3200]{1,0:T(8,128)(2,1)} concatenate(bf16[1536,320]{1,0:T(8,128)(2,1)S(1)} %copy.109, bf16[1536,192]{1,0:T(8,128)(2,1)S(1)} %copy.110, bf16[1536,896]{1,0:T(8,128)(2,1)} %convolution_convert_fusion.2, bf16[1536,896]{1,0:T(8,128)(2,1)} %convolution_convert_fusion.1, bf16[1536,896]{1,0:T(8,128)(2,1)} %fusion.1), dimensions={1} | concatenate | bytes 19660800 | tf_op jit(solution)/shard_map/concatenate | solution.py:575
  383.9 19.9 %all-gather.4.cloned.1.call-done = bf16[512,1536]{1,0:T(8,128)(2,1)} async-done(((bf16[64,1536]{1,0:T(8,128)(2,1)}), bf16[512,1536]{1,0:T(8,128)(2,1)}) %all-gather.4.cloned.1.call-update) | async-done | bytes 1572880 | tf_op jit(solution)/shard_map/all_gather | solution.py:445
  403.9 63.9 %psum.7 = f32[3200]{0:T(1024)S(1)} all-reduce(f32[3200]{0:T(1024)S(1)} %concatenate.39), channel_id=1, replica_groups=mesh['ctx'=16,'tp'=8] {'ctx','tp'}, use_global_device_ids=true, to_apply=%region_25.26 | all-reduce | flops 3200 | bytes 25600 | tf_op jit(solution)/shard_map/psum | solution.py:574
  470.3 3.7 convert_element_type.173
  473.9 83.9 %reduce-scatter.5.cloned.1.call-done = bf16[96,3200]{1,0:T(8,128)(2,1)} async-done(((bf16[1536,3200]{1,0:T(8,128)(2,1)}), bf16[96,3200]{1,0:T(8,128)(2,1)}) %reduce-scatter.5.cloned.1.call-update) | async-done | bytes 614416 | tf_op jit(solution)/shard_map/reduce_scatter | solution.py:576
  557.8 1.2 convert_element_type.175
  559.0 1.1 slice_multiply_fusion
  563.0 1.1 copy.125
  (152 shorter events, 24.7 us)
Async XLA Ops:
  7.2 0.7 copy-start
  7.2 102.7 %copy-start.25 = (f32[32]{0:T(128)}, f32[32]{0:T(128)S(1)}, u32[]{:S(2)}) copy-start(f32[32]{0:T(128)S(1)} %negate_power_fusion) | copy-start | bytes 388
  9.6 100.3 %copy-start.19 = (f32[96]{0:T(128)}, f32[96]{0:T(128)S(1)}, u32[]{:S(2)}) copy-start(f32[96]{0:T(128)S(1)} %convert_element_type.137) | copy-start | bytes 1156
  14.3 2.6 copy-start.23
  109.9 6.7 %copy-start.12 = (bf16[1536,2688]{1,0:T(8,128)(2,1)S(1)}, bf16[1536,2688]{1,0:T(8,128)(2,1)}, u32[]{:S(2)}) copy-start(bf16[1536,2688]{1,0:T(8,128)(2,1)} %get-tuple-element.26) | copy-start | bytes 24772612
  116.6 3.8 copy-start.8
  116.6 2.0 copy-start.10
  123.9 1.8 copy-start.32
  123.9 1.8 copy-start.13
  123.9 5.4 slice-start
  125.7 3.6 slice-start.1
  129.4 3.9 copy-start.3
  133.2 26.7 %all-to-all-start.2 = ((bf16[8,192,512]{2,1,0:T(8,128)(2,1)}), bf16[8,192,512]{2,1,0:T(8,128)(2,1)}, u32[]{:S(2)}, u32[]{:S(2)}) async-start(bf16[8,192,512]{2,1,0:T(8,128)(2,1)} %bitcast.86), calls=%async_computation.2 | async-start | bytes 3145728 | tf_op jit(solution)/shard_map/all_to_all | solution.py:440
  137.9 137.7 %reduce-scatter.3.cloned.1.call-start = ((), (), s32[]{:S(2)}) async-start(), calls=%async_computation.7 | async-start | bytes 2228224 | tf_op jit(solution)/shard_map/reduce_scatter | solution.py:535
  160.0 1.7 copy-start.5
  204.2 81.9 %all-to-all-start.1 = ((bf16[8,64,1536]{2,1,0:T(8,128)(2,1)}), bf16[8,64,1536]{2,1,0:T(8,128)(2,1)}, u32[]{:S(2)}, u32[]{:S(2)}) async-start(bf16[8,64,1536]{2,1,0:T(8,128)(2,1)} %bitcast.81), calls=%async_computation.1 | async-start | bytes 3145728 | tf_op jit(solution)/shard_map/all_to_all | solution.py:440
  209.5 5.3 copy-start.16
  275.6 4.0 copy-start.4
  275.6 5.0 copy-start.22
  276.7 4.1 copy-start.17
  276.7 4.8 copy-start.2
  276.7 4.8 copy-start.21
  280.8 0.7 copy-start.14
  286.2 24.0 %all-to-all-start.3 = ((bf16[8,64,1536]{2,1,0:T(8,128)(2,1)}), bf16[8,64,1536]{2,1,0:T(8,128)(2,1)}, u32[]{:S(2)}, u32[]{:S(2)}) async-start(bf16[8,64,1536]{2,1,0:T(8,128)(2,1)} %bitcast.80), calls=%async_computation.4 | async-start | bytes 3145728 | tf_op jit(solution)/shard_map/all_to_all | solution.py:440
  290.7 76.2 %all-gather.8.cloned.1.call-start = ((), (), s32[]{:S(2)}) async-start(), calls=%async_computation.9 | async-start | bytes 1769472 | tf_op jit(solution)/shard_map/all_gather | solution.py:445
  314.9 88.9 %all-gather.4.cloned.1.call-start = ((), (), s32[]{:S(2)}) async-start(), calls=%async_computation.6 | async-start | bytes 1769472 | tf_op jit(solution)/shard_map/all_gather | solution.py:445
  352.5 117.7 %all-gather.6.cloned.1.call-start = ((), (), s32[]{:S(2)}) async-start(), calls=%async_computation.8 | async-start | bytes 1769472 | tf_op jit(solution)/shard_map/all_gather | solution.py:445
  353.1 5.5 copy-start.9
  353.1 5.5 copy-start.33
  353.1 204.7 %reduce-scatter.5.cloned.1.call-start = ((), (), s32[]{:S(2)}) async-start(), calls=%async_computation.10 | async-start | bytes 10444800 | tf_op jit(solution)/shard_map/reduce_scatter | solution.py:576
  358.6 3.4 copy-start.11
  358.6 3.4 copy-start.34
  362.0 3.4 copy-start.15
  362.0 3.4 copy-start.31
  366.1 0.9 copy-start.6
  383.8 20.0 %copy-start.26 = (f32[64]{0:T(128)S(1)}, f32[64]{0:T(128)}, u32[]{:S(2)}) copy-start(f32[64]{0:T(128)} %get-tuple-element.126) | copy-start | bytes 772
  383.8 20.0 %copy-start.27 = (f32[64]{0:T(128)S(1)}, f32[64]{0:T(128)}, u32[]{:S(2)}) copy-start(f32[64]{0:T(128)} %get-tuple-element.121) | copy-start | bytes 772
  383.8 20.0 %copy-start.28 = (f32[64]{0:T(128)S(1)}, f32[64]{0:T(128)}, u32[]{:S(2)}) copy-start(f32[64]{0:T(128)} %get-tuple-element.124) | copy-start | bytes 772
  383.8 20.0 %copy-start.18 = (f32[1536]{0:T(1024)S(1)}, f32[1536]{0:T(1024)}, u32[]{:S(2)}) copy-start(f32[1536]{0:T(1024)} %get-tuple-element.113) | copy-start | bytes 18436
  383.8 85.3 %copy-start.29 = (bf16[96]{0:T(256)(128)(2,1)S(1)}, bf16[96]{0:T(256)(128)(2,1)}, u32[]{:S(2)}) copy-start(bf16[96]{0:T(256)(128)(2,1)} %param.23) | copy-start | bytes 580
  383.8 85.8 %copy-start.30 = (bf16[96]{0:T(256)(128)(2,1)S(1)}, bf16[96]{0:T(256)(128)(2,1)}, u32[]{:S(2)}) copy-start(bf16[96]{0:T(256)(128)(2,1)} %param.16) | copy-start | bytes 580
  470.3 88.7 %copy-start.24 = (f32[96]{0:T(128)S(1)}, f32[96]{0:T(128)}, u32[]{:S(2)}) copy-start(f32[96]{0:T(128)} %copy-done.23) | copy-start | bytes 1156
  473.9 86.2 %copy-start.20 = (f32[96]{0:T(128)S(1)}, f32[96]{0:T(128)}, u32[]{:S(2)}) copy-start(f32[96]{0:T(128)} %copy-done.19) | copy-start | bytes 1156
  559.0 4.1 copy-start.7
  559.0 5.2 copy-start.1
Sparse Core Ops, SparseCore 0:
  204.4 71.2 reduce-scatter.2
  315.0 46.6 all-gather.7
  363.9 39.8 all-gather.3
  405.3 39.8 all-gather.5
  449.5 108.3 reduce-scatter.4

commit v2 on v1

--- a/solution.py
+++ b/solution.py
@@ -373,53 +373,514 @@
     )(kb, block_input, wq_s, wf_s, cosine, sine)
 
 
-def backward_keys(kb, qt_ref, gt_ref, drift_ref, kv_ref, dq_ref, out_ref):
+SLOTS = ((0, 2), (1, 2), (1, 1), (1, 3), (0, 1), (0, 3), (1, 0), (0, 0))
+
+
+def slot_chip(me, step):
+    dz = sum(jnp.where(step == k, p[0], 0) for k, p in enumerate(SLOTS) if p[0])
+    dx = sum(jnp.where(step == k, p[1], 0) for k, p in enumerate(SLOTS) if p[1])
+    return lax.rem(me.zh + dz, 2) * 4 + lax.rem(me.x + dx, 4)
+
+
+def add_into(out, *terms):
+    total = terms[0][...].astype(F32)
+    for term in terms[1:]:
+        total += term[...].astype(F32)
+    out[...] = total.astype(out.dtype)
+
+
+class RingSum:
+    def __init__(self, src, half, stage, rel_l, rel_r, col_l, col_r, from_z, pair, right, left, send, recv):
+        self.src, self.half = src, half
+        at_stage = {2: (0, 0), 3: (0, 1), 4: (1, 0), 5: (1, 1)}
+
+        def put(k, part):
+            if stage is None:
+                return src(k, part)
+            rows = pl.ds(part * half, half)
+            return stage.at[2 if k == 6 else at_stage[k][0], rows]
+
+        self.put = put
+        self.rel_l, self.rel_r, self.col_l, self.col_r, self.from_z = rel_l, rel_r, col_l, col_r, from_z
+        self.to = {"z": pair, "r": right, "l": left}
+        self.send, self.recv = send, recv
+        low, high = pl.ds(0, half), pl.ds(half, half)
+        self.low, self.high = low, high
+        self.plan = [
+            (src(1, 0), rel_l.at[1], "r"),
+            (src(1, 1), rel_r.at[1], "l"),
+            (src(0, 0), rel_l.at[0], "r"),
+            (src(0, 1), rel_r.at[0], "l"),
+            (src(2, 1), col_l.at[1, high], "r"),
+            (src(3, 0), col_r.at[1, low], "l"),
+            (src(4, 1), col_l.at[0, high], "r"),
+            (src(5, 0), col_r.at[0, low], "l"),
+            (put(2, 0), col_l.at[1, low], "r"),
+            (put(3, 1), col_r.at[1, high], "l"),
+            (put(4, 0), col_l.at[0, low], "r"),
+            (put(5, 1), col_r.at[0, high], "l"),
+            (put(6, 0), from_z.at[low], "z"),
+            (put(6, 1), from_z.at[high], "z"),
+        ]
+
+    def copy(self, k):
+        here, there, to = self.plan[k]
+        return pltpu.make_async_remote_copy(
+            src_ref=here,
+            dst_ref=there,
+            send_sem=self.send.at[k],
+            recv_sem=self.recv.at[k],
+            device_id=self.to[to],
+            device_id_type=MESH,
+        )
+
+    def go(self, *which):
+        for k in which:
+            self.copy(k).start()
+
+    def got(self, *which):
+        for k in which:
+            self.copy(k).wait_recv()
+
+    def begin(self):
+        self.go(*range(8))
+
+    def relay_right(self, plane):
+        k = 2 if plane else 4
+        self.got(0 if plane else 2)
+        add_into(self.put(k, 0), self.src(k, 0), self.rel_l.at[plane])
+        self.go(8 if plane else 10)
+
+    def relay_left(self, plane):
+        k = 3 if plane else 5
+        self.got(1 if plane else 3)
+        add_into(self.put(k, 1), self.src(k, 1), self.rel_r.at[plane])
+        self.go(9 if plane else 11)
+
+    def relay(self):
+        for plane in (1, 0):
+            self.relay_right(plane)
+            self.relay_left(plane)
+
+    def column(self):
+        self.got(4, 8, 5, 9)
+        for part, rows in enumerate((self.low, self.high)):
+            add_into(
+                self.put(6, part),
+                self.src(6, part),
+                self.col_l.at[1, rows],
+                self.col_r.at[1, rows],
+            )
+            self.go(12 + part)
+
+    def finish(self, part):
+        if part == 0:
+            self.got(6, 10, 7, 11, 12, 13)
+        rows = self.low if part == 0 else self.high
+        total = self.src(7, part)[...].astype(F32)
+        for term in (self.col_l.at[0, rows], self.col_r.at[0, rows], self.from_z.at[rows]):
+            total += term[...].astype(F32)
+        return total
+
+    def sent(self):
+        for k in range(14):
+            self.copy(k).wait_send()
+
+
+def ring_scratch(half, width, stage=False):
+    return [
+        pltpu.VMEM((3, 2 * half, width) if stage else (1, 16, 128), BF),
+        pltpu.VMEM((2, half, width), BF),
+        pltpu.VMEM((2, half, width), BF),
+        pltpu.VMEM((2, 2 * half, width), BF),
+        pltpu.VMEM((2, 2 * half, width), BF),
+        pltpu.VMEM((2 * half, width), BF),
+        DMA((14,)),
+        DMA((14,)),
+    ]
+
+
+def ring(src, half, scratch, neighbours, stage=False):
+    room, rel_l, rel_r, col_l, col_r, from_z, send, recv = scratch
+    return RingSum(
+        src, half, room if stage else None, rel_l, rel_r, col_l, col_r, from_z, *neighbours[:3],
+        send, recv,
+    )
+
+
+def backward_kernel(
+    kb, u_ref, ffn_ref, share_ref, mid_ref, gate_g, up_g, down_g, gain_two,
+    x_ref, normed, wq, raw, att_own, sums, qt, kv, cos_ref, sin_ref,
+    two, gin, own_q, own_w, gains,
+    mid_rows, gt, drift, dq, gk, gk_sib, part_w, sib_w, pw, sib_p, back, pre, extra,
+    s_two, r_two, s_in, r_in, s_ex, r_ex, s_sib, r_sib, s_loc,
+    *rest,
+):
     me = Place()
+    cn = ctx_neighbours(me)
+    tn = tp_neighbours(me)
+    sib = cn[3]
+    tokens = normed.shape[0]
+    scratch = [rest[8 * k : 8 * k + 8] for k in range(8)]
+    greet([*cn, *tn])
+
+    def tp_block(k):
+        return me.tp(*SLOTS[k])
+
+    def chip(k):
+        dz, dx = SLOTS[k]
+        return me.ctx(dz, dx) // 2
+
+    def rows_of(ref, size):
+        def src(k, part):
+            start = pl.multiple_of(tp_block(k) * size, size) + part * (size // 2)
+            return ref.at[pl.ds(pl.multiple_of(start, size // 2), size // 2)]
+
+        return src
+
+    def two_rows(k, part):
+        ref = share_ref if part else ffn_ref
+        return ref.at[pl.ds(pl.multiple_of(tp_block(k) * 64, 64), 64)]
+
+    sum_u = ring(rows_of(u_ref, 192), 96, scratch[0], tn, True)
+    sum_two = ring(two_rows, 64, scratch[1], tn, True)
+    sum_b = ring(rows_of(back, 64), 32, scratch[2], tn)
+    sum_kv = ring(
+        lambda k, part: gk.at[k, me.core, pl.ds(64 * part, 64)], 64, scratch[3], cn
+    )
+    sum_w = [
+        ring(
+            lambda k, part, p=p: part_w.at[p, chip(k), pl.ds(48 * part, 48)],
+            48,
+            scratch[4 + p],
+            cn,
+        )
+        for p in range(3)
+    ]
+    sum_q = ring(
+        lambda k, part: pw.at[chip(k), me.core, pl.ds(48 * part, 48)], 48, scratch[7], cn
+    )
+    put_two = Gather(two, 128, me.tp, *tn, None, s_two, r_two)
+    put_in = Gather(gin, 64, me.tp, *tn, None, s_in, r_in)
+    put_ex = Gather(extra, 96, me.tp, *tn, None, s_ex, r_ex)
+
+    def to_sibling(k, here, there):
+        return pltpu.make_async_remote_copy(
+            src_ref=here,
+            dst_ref=there,
+            send_sem=s_sib.at[k],
+            recv_sem=r_sib.at[k],
+            device_id=sib,
+            device_id_type=MESH,
+        )
+
+    def key_swap(k):
+        return to_sibling(k, gk.at[k, 1 - me.core], gk_sib.at[k])
+
+    swap_w = [
+        to_sibling(8 + p, g.at[:, 1 - me.core], sib_w.at[p])
+        for p, g in enumerate((gate_g, up_g, down_g))
+    ]
+    swap_p = to_sibling(11, pw.at[:, 1 - me.core], sib_p)
+    keep_w = [
+        pltpu.make_async_copy(g.at[:, me.core], part_w.at[p], s_loc.at[p])
+        for p, g in enumerate((gate_g, up_g, down_g))
+    ]
+
+    sum_u.begin()
+    for p in range(3):
+        swap_w[p].start()
+        keep_w[p].start()
+
+    def join_w(p):
+        keep_w[p].wait()
+        swap_w[p].wait_recv()
+
+        def one(j, carry):
+            add_into(part_w.at[p, j], part_w.at[p, j], sib_w.at[p, j])
+            return carry
+
+        lax.fori_loop(0, 8, one, 0)
+
+    sum_u.relay()
+    join_w(0)
+    sum_w[0].begin()
+    sum_u.column()
+    join_w(1)
+    join_w(2)
+    halves = [sum_u.finish(0), sum_u.finish(1)]
+    grad_att = jnp.concatenate(halves, axis=0)
+    sum_two.begin()
+    gt[0:64] = jnp.zeros((64, 3 * tokens), BF)
+    for h in range(3):
+        cols = slice(h * tokens, (h + 1) * tokens)
+        grad = grad_att[64 * h : 64 * h + 64]
+        inverse = 1.0 / sums[0:1, cols]
+        gt[64:128, cols] = (grad * inverse).astype(BF)
+        drift[0:1, cols] = (
+            jnp.sum(grad * att_own[64 * h : 64 * h + 64].astype(F32), axis=0, keepdims=True)
+            * inverse
+        )
+    dq[...] = jnp.zeros_like(dq)
+    sum_w[0].relay()
+    sum_w[1].begin()
     apart = lax.broadcasted_iota(jnp.int32, (256, 256), 0) - lax.broadcasted_iota(
         jnp.int32, (256, 256), 1
     )
-    dq_ref[...] = jnp.zeros_like(dq_ref)
-
-    def key_step(j, carry):
-        rows = kv_ref[pl.ds(pl.multiple_of(j * 1024, 1024), 1024), :]
-        scores = dot(rows, qt_ref[...])
-        slopes = dot(rows, gt_ref[...])
-        parts, grads = [], []
-        for a in range(4):
-            line, grad_line = [], []
-            for b in range(6):
-                at = (slice(a * 256, a * 256 + 256), slice(b * 256, b * 256 + 256))
-                seen = apart <= kb[me.c * 2 + b % 2] - kb[j * 4 + a]
-                weight = jnp.where(seen, jnp.exp2(scores[at]), 0.0)
-                line.append(weight.astype(BF))
-                grad_line.append((weight * (slopes[at] - drift_ref[0:1, at[1]])).astype(BF))
-            parts.append(jnp.concatenate(line, axis=1))
-            grads.append(jnp.concatenate(grad_line, axis=1))
-        weight = jnp.concatenate(parts, axis=0)
-        grad = jnp.concatenate(grads, axis=0)
-        dq_ref[...] += dot(rows.T[0:64], grad)
-        key_grad = dot_nt(qt_ref[0:64], grad) * LN2
-        value_grad = dot_nt(gt_ref[64:128], weight)
-        both = jnp.concatenate([key_grad, value_grad], axis=0).astype(BF)
-        out_ref[2 * j] = both[:, 0:512]
-        out_ref[2 * j + 1] = both[:, 512:1024]
+
+    def join_keys(k):
+        key_swap(k).wait_recv()
+        add_into(gk.at[k, me.core], gk.at[k, me.core], gk_sib.at[k])
+
+    def key_step(step, carry):
+        @pl.when(step == 1)
+        def _():
+            join_keys(0)
+            sum_kv.go(2, 3)
+            sum_w[0].column()
+            sum_w[1].relay()
+            sum_w[2].begin()
+
+        @pl.when(step == 2)
+        def _():
+            join_keys(1)
+            sum_kv.go(0, 1)
+            sum_two.relay()
+
+        @pl.when(step == 3)
+        def _():
+            join_keys(2)
+            sum_kv.go(4)
+            sum_kv.relay_right(1)
+            sum_w[2].relay()
+            sum_w[1].column()
+
+        @pl.when(step == 4)
+        def _():
+            join_keys(3)
+            sum_kv.go(5)
+            sum_kv.relay_left(1)
+            sum_two.column()
+
+        @pl.when(step == 5)
+        def _():
+            join_keys(4)
+            sum_kv.go(6)
+            sum_kv.relay_right(0)
+            sum_w[2].column()
+
+        @pl.when(step == 6)
+        def _():
+            join_keys(5)
+            sum_kv.go(7)
+            sum_kv.relay_left(0)
+            own = pl.multiple_of(me.t * 128, 128)
+            two[pl.ds(own, 64)] = (mid_ref[...] + sum_two.finish(0)).astype(BF)
+            branch = sum_two.finish(1)
+            mid_rows[...] = branch
+            two[pl.ds(own + 64, 64)] = branch.astype(BF)
+            put_two.begin()
+
+        @pl.when(step == 7)
+        def _():
+            join_keys(6)
+            sum_kv.column()
+            for p in range(3):
+                for half in range(2):
+                    own_w[p, 48 * half : 48 * half + 48] = sum_w[p].finish(half)
+
+        place = slot_chip(me, step)
+        rows = kv[pl.ds(pl.multiple_of(place * 1024, 1024), 1024), :]
+        key_t = rows.T[0:64]
+        key_grad = value_grad = 0.0
+        for h in range(3):
+            cols = slice(h * tokens, (h + 1) * tokens)
+            scores = dot(rows, qt[:, cols])
+            slopes = dot(rows, gt[:, cols])
+            parts, grads = [], []
+            for a in range(4):
+                line, grad_line = [], []
+                for b in range(2):
+                    at = (slice(a * 256, a * 256 + 256), slice(b * 256, b * 256 + 256))
+                    seen = apart <= kb[me.c * 2 + b] - kb[place * 4 + a]
+                    weight = jnp.where(seen, jnp.exp2(scores[at]), 0.0)
+                    line.append(weight.astype(BF))
+                    lean = drift[0:1, h * tokens + b * 256 : h * tokens + b * 256 + 256]
+                    grad_line.append((weight * (slopes[at] - lean)).astype(BF))
+                parts.append(jnp.concatenate(line, axis=1))
+                grads.append(jnp.concatenate(grad_line, axis=1))
+            weight = jnp.concatenate(parts, axis=0)
+            grad = jnp.concatenate(grads, axis=0)
+            dq[:, cols] += dot(key_t, grad)
+            key_grad += dot_nt(qt[0:64, cols], grad)
+            value_grad += dot_nt(gt[64:128, cols], weight)
+        both = jnp.concatenate([key_grad * LN2, value_grad], axis=0).astype(BF)
+        gk[step, 0] = both[:, 0:512]
+        gk[step, 1] = both[:, 512:1024]
+        key_swap(step).start()
         return carry
 
     lax.fori_loop(0, 8, key_step, 0)
-
-
-def backward_part(kb, qt, gt, drift, kv):
+    query_gain, key_gain = gain_columns(wq)
+    cosine, sine = cos_ref[...], sin_ref[...]
+
+    def unturn(grad, value, gain):
+        inverse = column_inverse(value)
+        hat = value * inverse
+        a, b = grad[:32], grad[32:]
+        plain = jnp.concatenate([a * cosine + b * sine, b * cosine - a * sine], axis=0)
+        gain_grad = jnp.sum(plain * hat, axis=1, keepdims=True)
+        pulled = plain * gain
+        back_grad = inverse * (pulled - hat * jnp.mean(pulled * hat, axis=0, keepdims=True))
+        return gain_grad, back_grad
+
+    query_gain_grad = 0.0
+    for h in range(3):
+        part, grad = unturn(
+            dq[:, h * tokens : (h + 1) * tokens] * 0.125, raw[64 * h : 64 * h + 64], query_gain
+        )
+        query_gain_grad += part
+        pre[64 * h : 64 * h + 64] = grad
+    put_two.near()
+    put_two.pair()
+    join_keys(7)
+    key_grad, value_grad = sum_kv.finish(0), sum_kv.finish(1)
+    key_gain_grad, grad = unturn(key_grad, raw[192:256], key_gain)
+    pre[192:256] = grad
+    pre[256:320] = value_grad
+    pre[320:384] = jnp.zeros((64, tokens), F32)
+    pre_n = pre[...].T.astype(BF)
+    gain_one = 0.0
+    for i in range(2):
+        rows = slice(256 * i, 256 * i + 256)
+        part = dot_nt(pre_n[rows], wq[:, 0:384])
+        back[rows] = part.astype(BF)
+        gain_one += jnp.sum(part * normed[rows].astype(F32), axis=0, keepdims=True)
+    sum_b.begin()
+    lane = lax.broadcasted_iota(jnp.int32, (64, 1536), 1)
+    unit = lax.broadcasted_iota(jnp.int32, (64, 1536), 0)
+    spot = lane == (unit // 4) * 96 + lax.rem(unit, 4)
+
+    def spread(column):
+        return jnp.sum(jnp.where(spot, column, 0.0), axis=0, keepdims=True)
+
+    lines = jnp.concatenate(
+        [
+            jnp.zeros((64, 1536), F32),
+            gain_one,
+            gain_two[...],
+            spread(query_gain_grad),
+            spread(key_gain_grad),
+            jnp.zeros((60, 1536), F32),
+        ],
+        axis=0,
+    )
+    sides = lines.T
+    put_two.far()
+    put_two.last()
+    sum_b.relay()
+    att_n = jnp.concatenate([att_own[...].astype(F32), jnp.zeros((64, tokens), F32)], axis=0).T.astype(BF)
+    for i in range(4):
+        at = slice(384 * i, 384 * i + 384)
+        part = dot(normed[:, at].T, pre_n)
+        part = jnp.concatenate([part[:, 0:256], part[:, 256:384] + sides[at]], axis=1)
+        branch = jnp.concatenate(
+            [two[128 * b + 64 : 128 * b + 128, at] for b in range(8)], axis=0
+        )
+        whole = jnp.concatenate([part, dot(branch.T, att_n)], axis=1).astype(BF)
+        for q in range(4):
+            pw[2 * i + q // 2, q % 2] = whole[96 * q : 96 * q + 96]
+    swap_p.start()
+    sum_b.column()
+    swap_p.wait_recv()
+
+    def join_p(j, carry):
+        add_into(pw.at[j, me.core], pw.at[j, me.core], sib_p.at[j])
+        return carry
+
+    lax.fori_loop(0, 8, join_p, 0)
+    sum_q.begin()
+    own = pl.multiple_of(me.t * 64, 64)
+    value = x_ref[...].astype(F32)
+    inverse = rms_inverse(value)
+    hat = value * inverse
+    back_one = jnp.concatenate([sum_b.finish(0), sum_b.finish(1)], axis=0)
+    gin[pl.ds(own, 64)] = (
+        mid_rows[...]
+        + inverse * (back_one - hat * jnp.mean(back_one * hat, axis=-1, keepdims=True))
+    ).astype(BF)
+    put_in.begin()
+    sum_q.relay()
+    put_in.near()
+    put_in.pair()
+    sum_q.column()
+    put_in.far()
+    for half in range(2):
+        own_q[48 * half : 48 * half + 48] = sum_q.finish(half)
+    extra[pl.ds(pl.multiple_of(me.t * 96, 96), 96)] = own_q[:, 256:384]
+    put_ex.begin()
+    put_in.last()
+    put_ex.near()
+    put_ex.pair()
+    put_ex.far()
+    put_ex.last()
+    total = extra[0:96]
+    for b in range(1, 8):
+        total += extra[96 * b : 96 * b + 96]
+    gains[...] = total
+    for s in [sum_u, sum_two, sum_b, sum_kv, sum_q, *sum_w, put_two, put_in, put_ex, ]:
+        s.sent()
+    for k in range(8):
+        key_swap(k).wait_send()
+    for s in [*swap_w, swap_p]:
+        s.wait_send()
+
+
+def backward_part(*operands):
+    tokens = 512
+    shapes = [
+        jax.ShapeDtypeStruct((1024, 1536), BF),
+        jax.ShapeDtypeStruct((512, 1536), BF),
+        jax.ShapeDtypeStruct((96, 640), F32),
+        jax.ShapeDtypeStruct((3, 96, 896), F32),
+        jax.ShapeDtypeStruct((96, 128), F32),
+    ]
+    scratch = [
+        pltpu.VMEM((64, 1536), F32),
+        pltpu.VMEM((128, 3 * tokens), BF),
+        pltpu.VMEM((8, 3 * tokens), F32),
+        pltpu.VMEM((64, 3 * tokens), F32),
+        pltpu.VMEM((8, 2, 128, 512), BF),
+        pltpu.VMEM((8, 128, 512), BF),
+        pltpu.VMEM((3, 8, 96, 896), BF),
+        pltpu.VMEM((3, 8, 96, 896), BF),
+        pltpu.VMEM((8, 2, 96, 640), BF),
+        pltpu.VMEM((8, 96, 640), BF),
+        pltpu.VMEM((tokens, 1536), BF),
+        pltpu.VMEM((384, tokens), F32),
+        pltpu.VMEM((768, 128), F32),
+        *[DMA((9,))] * 6,
+        DMA((12,)),
+        DMA((12,)),
+        DMA((3,)),
+        *ring_scratch(96, 512, True),
+        *ring_scratch(64, 1536, True),
+        *ring_scratch(32, 1536),
+        *ring_scratch(64, 512),
+        *ring_scratch(48, 896) * 3,
+        *ring_scratch(48, 640),
+    ]
     return pl.pallas_call(
-        backward_keys,
-        out_shape=[
-            jax.ShapeDtypeStruct((64, 1536), F32),
-            jax.ShapeDtypeStruct((16, 128, 512), BF),
-        ],
-        in_specs=[SM, VM, VM, VM, VM],
-        out_specs=[VM, VM],
-        name="backward_keys",
-        compiler_params=pltpu.CompilerParams(vmem_limit_bytes=58 << 20),
-    )(kb, qt, gt, drift, kv)
+        backward_kernel,
+        out_shape=shapes,
+        in_specs=[SM, VM, VM, VM, VM, HB, HB, HB] + [VM] * 11,
+        out_specs=[VM] * 5,
+        scratch_shapes=scratch,
+        name="backward_part",
+        compiler_params=pltpu.CompilerParams(
+            collective_id=1, has_side_effects=True, vmem_limit_bytes=58 << 20
+        ),
+    )(*operands)
 
 
 def rotary_tables(places, width):
@@ -427,22 +888,6 @@
     freq_table = THETA ** (-(jnp.arange(half_width, dtype=F32) * 2.0 / width))
     angles = freq_table[:, None] * places.astype(F32)[None, :]
     return jnp.cos(angles), jnp.sin(angles)
-
-
-def cut_along(shard, dim, devices):
-    dims = shard.shape
-    blocks = shard.reshape(*dims[:dim], devices, dims[dim] // devices, *dims[dim + 1 :])
-    return jnp.moveaxis(blocks, dim, 0)
-
-
-def row_reduce(partial):
-    blocks = cut_along(partial.astype(BF), 0, lax.axis_size("tp"))
-    arrived = lax.all_to_all(blocks, "tp", split_axis=0, concat_axis=0, tiled=True)
-    return arrived.astype(F32).sum(axis=0)
-
-
-def row_collect(rows):
-    return lax.all_gather(rows, "tp", axis=0, tiled=True)
 
 
 def body(
@@ -499,101 +944,44 @@
     up = dot(low_two, up_full)
     sig = jax.nn.sigmoid(gate)
     act = (gate * sig * up).astype(BF)
-    ffn_part = dot_nt(act, down_full)
+    ffn_part = dot_nt(act, down_full).astype(BF)
     grad_act = dot(out_cotangent, down_full)
     grad_gate = (grad_act * up * sig * (1.0 + gate * (1.0 - sig))).astype(BF)
     grad_up = (grad_act * gate * sig).astype(BF)
-    down_grad = dot_tn(out_cotangent, act)
-    gate_grad = dot_tn(low_two, grad_gate)
-    up_grad = dot_tn(low_two, grad_up)
+
+    def blocks(grad):
+        return grad.astype(BF).reshape(8, 2, 96, 896)
+
+    down_grad = blocks(dot_tn(out_cotangent, act))
+    gate_grad = blocks(dot_tn(low_two, grad_gate))
+    up_grad = blocks(dot_tn(low_two, grad_up))
     back_two = dot_nt(grad_gate, gate_full) + dot_nt(grad_up, up_full)
-    gain_two_part = jnp.sum(back_two * normed_two, axis=0)
+    gain_two_part = jnp.sum(back_two * normed_two, axis=0, keepdims=True)
     pull = jnp.mean(back_two * normed_two, axis=-1, keepdims=True)
     share_mid = (
         out_cotangent.astype(F32) * 0.125 + inv_two * (back_two - normed_two * pull)
     ).astype(BF)
-    grad_att = row_reduce(dot_nt(wo, share_mid))
-    rows = tokens // 8
-
-    def own_rows(a):
-        return lax.dynamic_slice_in_dim(a, t * rows, rows, 0)
-
-    block_output = row_collect((own_rows(mid) + row_reduce(ffn_part)).astype(BF))
-    grad_mid = row_reduce(share_mid)
-    grad_branch = row_collect(grad_mid.astype(BF))
-    own_att = lax.dynamic_slice_in_dim(att, t * 192, 192, 0)
-    out_grad = lax.dot_general(
-        grad_branch, own_att, (((0,), (1,)), ((), ())), preferred_element_type=F32
-    )
-    total = sums[0].reshape(3, 1, tokens)
-    heads = grad_att.reshape(3, HD, tokens)
-    drift = jnp.sum(heads * own_att.reshape(3, HD, tokens).astype(F32), axis=1, keepdims=True) / total
-    scaled = (heads / total).astype(BF).transpose(1, 0, 2).reshape(HD, 3 * tokens)
-    gt = jnp.concatenate([jnp.zeros_like(scaled), scaled], axis=0)
-    drift8 = jnp.broadcast_to(drift.reshape(1, 3 * tokens), (8, 3 * tokens))
-    grad_q, grad_kv = backward_part(kb, qt, gt, drift8, kv)
-    own_kv = lax.psum_scatter(
-        grad_kv.reshape(16 * 128, 512), "ctx", scatter_dimension=0, tiled=True
-    ).astype(F32)
-    gains = wq.reshape(16, 96, 640)[:, :64, 320:322].astype(F32).sum(axis=0)
-
-    def unturn(grad, value, gain):
-        hat_inv = column_inverse(value)
-        hat = value * hat_inv
-        a, b = grad[:32], grad[32:]
-        plain = jnp.concatenate([a * cosine + b * sine, b * cosine - a * sine], axis=0)
-        gain_grad = jnp.sum(plain * hat, axis=1)
-        pulled = plain * gain
-        return gain_grad, (
-            hat_inv * (pulled - hat * jnp.mean(pulled * hat, axis=0, keepdims=True))
-        ).astype(BF)
-
-    parts, qg_grad = [], 0.0
-    for h in range(3):
-        g, back = unturn(
-            grad_q[:, h * tokens : (h + 1) * tokens] * 0.125, raw[64 * h : 64 * h + 64], gains[:, 0:1]
-        )
-        qg_grad += g
-        parts.append(back)
-    kg_grad, key_back = unturn(own_kv[0:64], raw[192:256], gains[:, 1:2])
-    pre = jnp.concatenate(parts + [key_back, own_kv[64:128].astype(BF)], axis=0)
-    qkv_grad = lax.dot_general(normed, pre, (((0,), (1,)), ((), ())), preferred_element_type=F32)
-    back_part = lax.dot_general(
-        pre, wq[:, 0:320], (((0,), (1,)), ((), ())), preferred_element_type=F32
-    )
-    inv_one = rms_inverse(x)
-    normed_one = x * inv_one
-    gain_one_part = jnp.sum(back_part * normed_one, axis=0)
-    back_one = row_reduce(back_part)
-    own_normed = own_rows(normed_one)
-    grad_rows = grad_mid + own_rows(inv_one) * (
-        back_one - own_normed * jnp.mean(back_one * own_normed, axis=-1, keepdims=True)
-    )
-    grad_input = row_collect(grad_rows.astype(BF)).astype(F32)
-    vectors = jnp.concatenate([gain_one_part, gain_two_part, qg_grad, kg_grad])
-    vectors = lax.psum(vectors, ("ctx", "tp"))
-    weight_grads = jnp.concatenate([qkv_grad, out_grad, gate_grad, up_grad, down_grad], axis=1)
-    own = lax.psum_scatter(
-        weight_grads.astype(BF), "ctx", scatter_dimension=0, tiled=True
-    ).astype(F32)
-
-    def mine(a, width):
-        return lax.dynamic_slice_in_dim(a, c * width, width, 0)
-
+    grad_att = dot_nt(wo, share_mid).astype(BF)
+    mid_rows = lax.dynamic_slice_in_dim(mid, t * 64, 64, 0)
+    att_own = lax.dynamic_slice_in_dim(att, t * 192, 192, 0)
+    two, gin, own_q, own_w, gains = backward_part(
+        kb, grad_att, ffn_part, share_mid, mid_rows, gate_grad, up_grad, down_grad, gain_two_part,
+        lax.dynamic_slice_in_dim(block_input, t * 64, 64, 0), normed, wq, raw, att_own, sums, qt, kv, cosine, sine,
+    )
     return (
-        block_output,
-        grad_input,
-        mine(vectors[0:1536], 96) / gain_one[:, 0],
-        own[:, 0:192] * gain_one,
-        own[:, 192:256] * gain_one,
-        own[:, 256:320] * gain_one,
-        mine(vectors[3072:3136], 4),
-        mine(vectors[3136:3200], 4),
-        own[:, 320:512].T,
-        mine(vectors[1536:3072], 96) / gain_two[:, 0],
-        own[:, 512 : 512 + 864] * gain_two,
-        own[:, 1408 : 1408 + 864] * gain_two,
-        own[:, 2304 : 2304 + 864].T,
+        two.reshape(8, 2, 64, 1536)[:, 0].reshape(tokens, 1536),
+        gin.astype(F32),
+        gains[:, 64] / gain_one[:, 0],
+        own_q[:, 0:192] * gain_one,
+        own_q[:, 192:256] * gain_one,
+        own_q[:, 256:320] * gain_one,
+        gains[0:4, 66],
+        gains[0:4, 67],
+        own_q[:, 384:576].T,
+        gains[:, 65] / gain_two[:, 0],
+        own_w[0, :, 0:864] * gain_two,
+        own_w[1, :, 0:864] * gain_two,
+        own_w[2, :, 0:864].T,
     )
 
 

time: 573 us -> 313 us (0.55)
  waiting for transfers between devices: 203 us -> 0 us
  Pallas kernels: 127 us -> 242 us
  blocking collectives: 96.7 us -> 0 us
  other arithmetic: 36 us -> 12.6 us
  starting transfers between devices: 14.9 us -> 0 us
  local copies, waits for them, and re-layouts: 32.7 us -> 19.2 us
  between operations: 14.4 us -> 1.48 us
  matrix products: 45.9 us -> 34.1 us
    reduce_scatter x2 -> x0, waiting for transfers between devices: 145 us -> none  [the longest x1 83.9 us: body(): lax.psum_scatter(weight_grads.astype(BF), 'ctx', scatter_dimension=0, til...]
    pallas_call x1, Pallas kernels: 38.1 us -> 153 us  [backward_part(): pl.pallas_call(backward_kernel, out_shape=shapes, in_specs=[SM, VM, VM, V...]
    psum x1 -> x0, blocking collectives: 63.9 us -> none  [body(): vectors = lax.psum(vectors, ('ctx', 'tp'))]
    all_to_all x3 -> x0, waiting for transfers between devices: 37.4 us -> none  [row_reduce(): lax.all_to_all(blocks, 'tp', split_axis=0, concat_axis=0, tiled=True)]
    all_to_all x1 -> x0, blocking collectives: 32.7 us -> none  [row_reduce(): lax.all_to_all(blocks, 'tp', split_axis=0, concat_axis=0, tiled=True)]
    all_gather x3 -> x0, waiting for transfers between devices: 20 us -> none  [row_collect(): return lax.all_gather(rows, 'tp', axis=0, tiled=True)]
    concatenate x4 -> x0, local copies, waits for them, and re-layouts: 15.5 us -> none  [the longest x1 14.6 us: body(): jnp.concatenate([qkv_grad, out_grad, gate_grad, up_grad, down_grad], axis=1)]
    all_to_all x3 -> x0, starting transfers between devices: 14.4 us -> none  [row_reduce(): lax.all_to_all(blocks, 'tp', split_axis=0, concat_axis=0, tiled=True)]
  transfers between devices with their start and end apart: 8 -> 0, of which waited for: 5 -> 0; matrix products, arithmetic and copies ran while one was open for 11% -> 0% of each run, Pallas kernels for 0% -> 0%
where the time goes in v2:
time: 313 us; the launch traced here: 309 us
  Pallas kernels  242 us (77%)
  matrix products  34.1 us (11%)
  local copies, waits for them, and re-layouts  19.2 us (6%)
  other arithmetic  12.6 us (4%)
    pallas_call x1, Pallas kernels, backward_part(): pl.pallas_call(backward_kernel, out_shape=shapes, in_specs=[SM, VM, VM, V...  153 us
    pallas_call x1, Pallas kernels, forward_part(): pl.pallas_call(forward_kernel, out_shape=shapes, in_specs=[SM, VM, VM, HB...  89.2 us
    dot_general x4, matrix products, dot_tn(): lax.dot_general(a, b, (((0,), (0,)), ((), ())), preferred_element_type=F32)  16.6 us
    dot_general x4, matrix products, dot_nt(): lax.dot_general(a, b, (((1,), (1,)), ((), ())), preferred_element_type=F32)  10.9 us

profile of v2, /device:TPU:0, one launch (start us, length us, event | category | flops | bytes accessed | tf_op | source)
XLA Modules:
  0.0 309.2 jit_solution(7238171418185245972)
XLA Ops:
  0.7 0.8 reshape.67
  1.4 0.6 slice_reduce_fusion.2.kb
  2.1 0.7 convert_element_type.92
  2.7 0.9 multiply_convert_fusion.4
  3.6 0.8 copy.87
  4.4 0.8 copy.86
  5.3 0.1 fusion.19
  5.5 0.8 fusion.17
  6.3 0.1 copy.88
  6.4 0.9 copy.89
  7.4 0.8 concatenate.6.wq_s
  8.1 0.7 convert_element_type.99
  8.8 1.1 multiply_convert_fusion.3
  9.9 1.7 fusion.25.wf_s
  11.7 0.8 dynamic-slice_convert_fusion
  12.4 1.0 multiply_sine_fusion
  13.4 89.2 %forward_part.1 = (bf16[1536,640]{1,0:T(8,128)(2,1)}, bf16[1536,2688]{1,0:T(8,128)(2,1)}, bf16[1536,1536]{1,0:T(8,128)(2,1)}, bf16[8192,128]{1,0:T(8,128)(2,1)},...) custom-call(s32[32]{0:T(128)} %slice_reduce_fusion.2.kb, ...), custom_call_target="tpu_custom_call" | custom-call | tf_op jit(solution)/shard_map/forward_part/pallas_call | solution.py:360
  102.6 6.4 %multiply_reduce_fusion = (f32[512]{0:T(512)S(1)}, f32[512,1536]{1,0:T(8,128)S(1)}) fusion(bf16[1536,512]{1,0:T(8,128)(2,1)} %get-tuple-element.28, bf16[1536,1536]{1,0:T(8,128)(2,1)} %get-tuple-element.27, bf16[512,1536]{1,0:T(8,128)(2,1)} %x_ref.1), kind=kOutput, calls=%fused_computation.6 | convolution fusion | flops 2419064320 | bytes 11012096 | tf_op jit(solution)/shard_map/dot_general | solution.py:178
  109.1 0.2 multiply_convert_fusion
  109.4 1.6 fusion.3
  111.0 0.3 copy-done.6
  111.3 1.6 fusion.9
  113.0 2.4 multiply_convert_fusion.1
  115.4 1.8 fusion.1
  117.3 2.2 fusion.26
  119.5 1.1 add_convert_fusion.share_ref
  120.6 3.8 %convolution_convert_fusion.4.u_ref = bf16[1536,512]{1,0:T(8,128)(2,1)} fusion(bf16[1536,1536]{1,0:T(8,128)(2,1)S(1)} %bitcast.80, bf16[512,1536]{1,0:T(8,128)(2,1)S(1)} %add_convert_fusion.share_ref), kind=kOutput, calls=%fused_computation.9 | convolution fusion | flops 2416705536 | bytes 7864320 | tf_op jit(solution)/shard_map/dot_general | solution.py:174
  124.4 3.1 %convolution_convert_fusion.3.ffn_ref = bf16[512,1536]{1,0:T(8,128)(2,1)} fusion(bf16[512,896]{0,1:T(8,128)(2,1)S(1)} %get-tuple-element.112, bf16[1536,2688]{1,0:T(8,128)(2,1)S(1)} %bitcast.75), kind=kOutput, calls=%fused_computation.8 | convolution fusion | flops 1410072576 | bytes 5242880 | tf_op jit(solution)/shard_map/dot_general | solution.py:174
  127.5 0.8 constant_dynamic-slice_fusion.2.mid_ref
  128.3 5.2 %convolution_convert_fusion.2 = bf16[1536,896]{1,0:T(8,128)(2,1)} fusion(bf16[512,1536]{1,0:T(8,128)(2,1)} %copy-done.3, bf16[512,896]{0,1:T(8,128)(2,1)} %copy-done.15), kind=kOutput, calls=%fused_computation.2 | convolution fusion | flops 1410662400 | bytes 5242880 | tf_op jit(solution)/shard_map/dot_general | solution.py:178
  133.5 3.4 %convolution_convert_fusion.1 = bf16[1536,896]{1,0:T(8,128)(2,1)} fusion(bf16[512,1536]{1,0:T(8,128)(2,1)S(1)} %copy-done.4, bf16[512,896]{0,1:T(8,128)(2,1)S(1)} %copy-done.10), kind=kOutput, calls=%fused_computation.1 | convolution fusion | flops 1410662400 | bytes 5242880 | tf_op jit(solution)/shard_map/dot_general | solution.py:178
  136.9 1.6 fusion
  138.5 2.8 copy.96
  141.3 0.6 broadcast_in_dim.5.gain_two
  141.9 1.6 constant_dynamic-slice_fusion.1.x_ref
  143.5 1.6 constant_dynamic-slice_fusion.att_own
  145.1 152.6 %backward_part.1 = (bf16[1024,1536]{1,0:T(8,128)(2,1)}, bf16[512,1536]{1,0:T(8,128)(2,1)}, f32[96,640]{1,0:T(8,128)}, f32[3,96,896]{2,1,0:T(8,128)}, f32[96,128]{1,0:T(8,128)}) custom-call(s32[32]{0:T(128)} %slice_reduce_fusion.2.kb, bf16[1536,512]{1,0:T(8,128)(2,1)} %convolution_convert_fusion.4.u_ref, bf16[512,1536]{1,0:T(8,128)(2,1)} %convolution_convert_fusion.3.ffn_ref, ...), custom_call_target="tpu_custom_call" | custom-call | tf_op jit(solution)/shard_map/backward_part/pallas_call | solution.py:873
  297.8 2.8 slice.65
  300.6 2.1 convert_element_type.117
  302.7 0.2 slice_reduce_fusion
  302.9 0.5 convert_divide_fusion
  303.4 0.7 slice_bitcast_fusion.1
  304.2 0.7 copy.97
  304.9 0.7 copy.98
  305.6 0.7 slice_reduce_fusion.3
  306.3 0.7 copy.99
  307.1 1.0 bitcast_multiply_fusion.2
  308.0 0.8 slice_bitcast_fusion
  (54 shorter events, 0.3 us)
Async XLA Ops:
  0.6 4.7 %copy-start = (bf16[4]{0:T(256)(128)(2,1)S(1)}, bf16[4]{0:T(256)(128)(2,1)}, u32[]{:S(2)}) copy-start(bf16[4]{0:T(256)(128)(2,1)} %param.21) | copy-start | bytes 28
  102.6 6.7 %slice-start = ((s8[8257536]{0:T(1024)(128)(4,1)}), s8[4194304]{0:T(1024)(128)(4,1)S(1)}, s32[]{:S(2)}) async-start(s8[8257536]{0:T(1024)(128)(4,1)} %bitcast.74), calls=%async_computation | async-start | bytes 8388608
  102.6 6.7 %slice-start.1 = ((s8[8257536]{0:T(1024)(128)(4,1)}), s8[4063232]{0:T(1024)(128)(4,1)S(1)}, s32[]{:S(2)}) async-start(s8[8257536]{0:T(1024)(128)(4,1)} %bitcast.74), calls=%async_computation.1 | async-start | bytes 8126464
  109.3 3.6 %copy-start.3 = (bf16[512,1536]{1,0:T(8,128)(2,1)}, bf16[512,1536]{1,0:T(8,128)(2,1)S(1)}, u32[]{:S(2)}) copy-start(bf16[512,1536]{1,0:T(8,128)(2,1)S(1)} %multiply_convert_fusion) | copy-start | bytes 4718596
  109.4 2.0 copy-start.6
  115.3 1.9 copy-start.15
  115.4 1.9 copy-start.9
  115.4 9.0 %copy-start.16 = (bf16[512,896]{0,1:T(8,128)(2,1)}, bf16[512,896]{0,1:T(8,128)(2,1)S(1)}, u32[]{:S(2)}) copy-start(bf16[512,896]{0,1:T(8,128)(2,1)S(1)} %get-tuple-element.112) | copy-start | bytes 2752516
  115.4 5.2 %slice-start.2 = ((s8[4718592]{0:T(1024)(128)(4,1)}), s8[4194304]{0:T(1024)(128)(4,1)S(1)}, s32[]{:S(2)}) async-start(s8[4718592]{0:T(1024)(128)(4,1)} %bitcast.79), calls=%async_computation.2 | async-start | bytes 8388608
  117.2 3.4 %slice-start.3 = ((s8[4718592]{0:T(1024)(128)(4,1)}), s8[524288]{0:T(1024)(128)(4,1)S(1)}, s32[]{:S(2)}) async-start(s8[4718592]{0:T(1024)(128)(4,1)} %bitcast.79), calls=%async_computation.3 | async-start | bytes 1048576
  120.6 3.8 %copy-start.2 = (bf16[512,1536]{1,0:T(8,128)(2,1)}, bf16[512,1536]{1,0:T(8,128)(2,1)S(1)}, u32[]{:S(2)}) copy-start(bf16[512,1536]{1,0:T(8,128)(2,1)S(1)} %add_convert_fusion.share_ref) | copy-start | bytes 4718596
  128.3 5.2 %copy-start.4 = (bf16[512,1536]{1,0:T(8,128)(2,1)S(1)}, bf16[512,1536]{1,0:T(8,128)(2,1)}, u32[]{:S(2)}) copy-start(bf16[512,1536]{1,0:T(8,128)(2,1)} %copy-done.3) | copy-start | bytes 4718596
  128.3 5.2 %copy-start.10 = (bf16[512,896]{0,1:T(8,128)(2,1)S(1)}, bf16[512,896]{0,1:T(8,128)(2,1)}, u32[]{:S(2)}) copy-start(bf16[512,896]{0,1:T(8,128)(2,1)} %copy-done.9) | copy-start | bytes 2752516
  133.5 3.4 %copy-start.7 = (bf16[512,1536]{1,0:T(8,128)(2,1)S(1)}, bf16[512,1536]{1,0:T(8,128)(2,1)}, u32[]{:S(2)}) copy-start(bf16[512,1536]{1,0:T(8,128)(2,1)} %param.27) | copy-start | bytes 4718596
  133.5 3.4 %copy-start.17 = (bf16[512,896]{0,1:T(8,128)(2,1)S(1)}, bf16[512,896]{0,1:T(8,128)(2,1)}, u32[]{:S(2)}) copy-start(bf16[512,896]{0,1:T(8,128)(2,1)} %copy-done.16) | copy-start | bytes 2752516
  297.8 2.8 copy-start.5
  300.5 2.1 copy-start.12
  300.5 2.3 copy-start.13
  300.5 2.3 copy-start.14
  300.5 2.8 copy-start.11
  300.6 6.5 %copy-start.8 = (f32[3,96,896]{2,1,0:T(8,128)S(1)}, f32[3,96,896]{2,1,0:T(8,128)}, u32[]{:S(2)}) copy-start(f32[3,96,896]{2,1,0:T(8,128)} %get-tuple-element.40) | copy-start | bytes 3096580
  300.6 8.2 %copy-start.1 = (bf16[4]{0:T(256)(128)(2,1)S(1)}, bf16[4]{0:T(256)(128)(2,1)}, u32[]{:S(2)}) copy-start(bf16[4]{0:T(256)(128)(2,1)} %param.21) | copy-start | bytes 28

commit v3 on v2

--- a/solution.py
+++ b/solution.py
@@ -181,205 +181,13 @@
 PAIRS = ((0, 0), (0, 3), (0, 1), (1, 0), (0, 2), (1, 3), (1, 1), (1, 2))
 
 
-def pair_of(me, step):
-    dz = sum(jnp.where(step == k, p[0], 0) for k, p in enumerate(PAIRS) if p[0])
-    dx = sum(jnp.where(step == k, p[1], 0) for k, p in enumerate(PAIRS) if p[1])
-    zh = lax.rem(me.zh + dz, 2)
-    return (zh * 4 + lax.rem(me.x + dx, 4)) * 2
-
-
-def forward_kernel(
-    kb, x_ref, wq_s, wf_s, cos_ref, sin_ref,
-    wq, wf, wo, kv, qt, raw, att, sums, normed,
-    acc, s_w, r_w, s_f, r_f, s_o, r_o, s_k, r_k, s_a, r_a, s_l,
-):
-    me = Place()
-    ctx_z, ctx_r, ctx_l, ctx_s = ctx_neighbours(me)
-    tp_z, tp_r, tp_l = tp_neighbours(me)
-    tokens = x_ref.shape[0]
-    greet([ctx_z, ctx_r, ctx_l, ctx_s, tp_z, tp_r, tp_l])
-    weights = Gather(wq, 96, me.ctx, ctx_z, ctx_r, ctx_l, ctx_s, s_w, r_w, own=wq_s)
-    feed = Gather(wf, 96, me.ctx, ctx_z, ctx_r, ctx_l, ctx_s, s_f, r_f, own=wf_s)
-    keys = Gather(kv, tokens, me.ctx, ctx_z, ctx_r, ctx_l, ctx_s, s_k, r_k)
-    outw = Gather(
-        wo, 96, lambda dz, dy: me.tp(dz, dy) * 2 + me.core, tp_z, tp_r, tp_l, ctx_s, s_o, r_o
-    )
-    share = Gather(att, 192, me.tp, tp_z, tp_r, tp_l, None, s_a, r_a)
-
-    weights.begin()
-    mine = pl.multiple_of(me.c * 96, 96)
-    keep = [
-        pltpu.make_async_copy(wq_s, wq.at[pl.ds(mine, 96)], s_l.at[0]),
-        pltpu.make_async_copy(wf_s, wf.at[pl.ds(mine, 96)], s_l.at[1]),
-    ]
-    for k in keep:
-        k.start()
-
-    def norm_rows(i, carry):
-        rows = pl.ds(pl.multiple_of(i * 64, 64), 64)
-        value = x_ref[rows].astype(F32)
-        normed[rows] = (value * rms_inverse(value)).astype(BF)
-        return carry
-
-    lax.fori_loop(0, tokens // 64, norm_rows, 0)
-    weights.near()
-    weights.pair()
-    weights.far()
-    weights.last()
-    keep[0].wait()
-    weights.end()
-
-    def project(i, carry):
-        cols = pl.ds(pl.multiple_of(i * 256, 256), 256)
-        raw[:, cols] = dot(normed[cols], wq[:, 0:384]).T
-        return carry
-
-    lax.fori_loop(0, tokens // 256, project, 0)
-    query_gain, key_gain = gain_columns(wq)
-    cosine, sine = cos_ref[...], sin_ref[...]
-
-    def turned(value, gain):
-        hat = value * column_inverse(value) * gain
-        a, b = hat[:32], hat[32:]
-        return jnp.concatenate([a * cosine - b * sine, b * cosine + a * sine], axis=0)
-
-    both = jnp.concatenate([turned(raw[192:256], key_gain), raw[256:320]], axis=0)
-    kv[pl.ds(pl.multiple_of(me.c * tokens, tokens), tokens)] = both.T.astype(BF)
-    keys.begin()
-    qt[64:128] = jnp.zeros((64, 3 * tokens), BF)
-    for h in range(3):
-        rows = raw[64 * h : 64 * h + 64]
-        qt[0:64, h * tokens : (h + 1) * tokens] = (
-            turned(rows, query_gain) * (LOG2E / 8.0)
-        ).astype(BF)
-    heads = wq[:, 384:640].T
-    wo[pl.ds(pl.multiple_of(me.t * 192 + me.core * 96, 96), 96)] = jnp.where(
-        me.core == 0, heads[0:96], heads[96:192]
-    )
-    outw.begin()
-    feed.begin()
-    acc[...] = jnp.zeros_like(acc)
-    ones = jnp.concatenate([jnp.ones((1, 1024), BF), jnp.zeros((15, 1024), BF)], axis=0)
-    apart = lax.broadcasted_iota(jnp.int32, (256, 256), 0) - lax.broadcasted_iota(
-        jnp.int32, (256, 256), 1
-    )
-
-    def key_step(step, carry):
-        @pl.when(step == 0)
-        def _():
-            keys.got(9)
-
-        @pl.when(step == 1)
-        def _():
-            keys.near()
-            keys.got(11)
-
-        @pl.when(step == 2)
-        def _():
-            keys.pair()
-            keys.got(12)
-
-        @pl.when(step == 3)
-        def _():
-            keys.got(10)
-            outw.near()
-
-        @pl.when(step == 4)
-        def _():
-            keys.far()
-            outw.pair()
-            keys.got(13)
-
-        @pl.when(step == 5)
-        def _():
-            keys.got(14)
-
-        @pl.when(step == 6)
-        def _():
-            keys.last()
-            outw.far()
-            keys.got(15)
-
-        @pl.when(step == 7)
-        def _():
-            keys.got(16)
-
-        first = pair_of(me, step)
-        rows = kv[pl.ds(pl.multiple_of(first * tokens, 1024), 1024), :]
-        scores = dot(rows, qt[...])
-        parts = []
-        for a in range(4):
-            line = []
-            for b in range(6):
-                sub = scores[a * 256 : a * 256 + 256, b * 256 : b * 256 + 256]
-                seen = apart <= kb[me.c * 2 + b % 2] - kb[first * 2 + a]
-                line.append(jnp.where(seen, jnp.exp2(sub), 0.0).astype(BF))
-            parts.append(jnp.concatenate(line, axis=1))
-        weight = jnp.concatenate(parts, axis=0)
-        left = jnp.concatenate([rows.T[64:128], ones], axis=0)
-        acc[...] += dot(left, weight)
-        return carry
-
-    lax.fori_loop(0, 8, key_step, 0)
-    total = acc[64:65, :]
-    sums[...] = jnp.broadcast_to(total, sums.shape)
-    own = pl.multiple_of(me.t * 192, 192)
-    for h in range(3):
-        cols = slice(h * tokens, (h + 1) * tokens)
-        att[pl.ds(own + 64 * h, 64)] = (acc[0:64, cols] / total[:, cols]).astype(BF)
-    share.begin()
-    outw.last()
-    feed.near()
-    share.near()
-    share.pair()
-    feed.pair()
-    share.far()
-    share.last()
-    feed.far()
-    keys.sent()
-    share.sent()
-    outw.end()
-    feed.last()
-    keep[1].wait()
-    feed.end()
-
-
-def forward_part(kb, block_input, wq_s, wf_s, cosine, sine):
-    tokens = block_input.shape[0]
-    shapes = [
-        jax.ShapeDtypeStruct((1536, 640), BF),
-        jax.ShapeDtypeStruct((1536, wf_s.shape[1]), BF),
-        jax.ShapeDtypeStruct((1536, 1536), BF),
-        jax.ShapeDtypeStruct((16 * tokens, 128), BF),
-        jax.ShapeDtypeStruct((128, 3 * tokens), BF),
-        jax.ShapeDtypeStruct((384, tokens), F32),
-        jax.ShapeDtypeStruct((1536, tokens), BF),
-        jax.ShapeDtypeStruct((8, 3 * tokens), F32),
-        jax.ShapeDtypeStruct((tokens, 1536), BF),
-    ]
-    return pl.pallas_call(
-        forward_kernel,
-        out_shape=shapes,
-        in_specs=[SM, VM, VM, HB, VM, VM],
-        out_specs=[VM, HB, VM, VM, VM, VM, VM, VM, VM],
-        scratch_shapes=[pltpu.VMEM((80, 3 * tokens), F32)]
-        + [DMA((17,))] * 8
-        + [DMA((9,))] * 2
-        + [DMA((2,))],
-        name="forward_part",
-        compiler_params=pltpu.CompilerParams(
-            collective_id=0, has_side_effects=True, vmem_limit_bytes=58 << 20
-        ),
-    )(kb, block_input, wq_s, wf_s, cosine, sine)
+def chip_of(me, step, order):
+    dz = sum(jnp.where(step == k, p[0], 0) for k, p in enumerate(order) if p[0])
+    dx = sum(jnp.where(step == k, p[1], 0) for k, p in enumerate(order) if p[1])
+    return lax.rem(me.zh + dz, 2) * 4 + lax.rem(me.x + dx, 4)
 
 
 SLOTS = ((0, 2), (1, 2), (1, 1), (1, 3), (0, 1), (0, 3), (1, 0), (0, 0))
-
-
-def slot_chip(me, step):
-    dz = sum(jnp.where(step == k, p[0], 0) for k, p in enumerate(SLOTS) if p[0])
-    dx = sum(jnp.where(step == k, p[1], 0) for k, p in enumerate(SLOTS) if p[1])
-    return lax.rem(me.zh + dz, 2) * 4 + lax.rem(me.x + dx, 4)
 
 
 def add_into(out, *terms):
@@ -508,12 +316,384 @@
     )
 
 
+def forward_kernel(
+    kb, x_ref, cot, wq_s, wo_s, wf_s, cos_ref, sin_ref,
+    wq, kv, qt, raw, sums, normed, att_own, u_ref, share_ref, block, gain_two, low, act, grad_g, grad_u, p_all,
+    wo_t, wf, wo, att, acc, pbuf, mid, inv, gate, up, ffn,
+    s_w, r_w, s_v, r_v, s_f, r_f, s_o, r_o, s_k, r_k, s_a, r_a, s_l, s_p,
+    *rest,
+):
+    me = Place()
+    cn = ctx_neighbours(me)
+    tn = tp_neighbours(me)
+    tokens = x_ref.shape[0]
+    greet([*cn, *tn])
+    weights = Gather(wq, 96, me.ctx, *cn, s_w, r_w, own=wq_s)
+    outs = Gather(wo_t, 96, me.ctx, *cn, s_v, r_v, own=wo_s)
+    feed = [
+        Gather(
+            wf.at[p], 96, me.ctx, *cn, s_f.at[p], r_f.at[p], own=wf_s.at[:, 896 * p : 896 * p + 896]
+        )
+        for p in range(3)
+    ]
+    keys = Gather(kv, tokens, me.ctx, *cn, s_k, r_k)
+    outw = Gather(
+        wo, 96, lambda dz, dy: me.tp(dz, dy) * 2 + me.core, *tn, cn[3], s_o, r_o
+    )
+    share = [
+        Gather(
+            att, 64, lambda dz, dy, h=h: me.tp(dz, dy) * 3 + h, *tn, None, s_a.at[h], r_a.at[h]
+        )
+        for h in range(3)
+    ]
+    sum_f = ring(
+        lambda k, part: ffn.at[
+            pl.ds(pl.multiple_of(me.tp(*SLOTS[k]) * 64 + 32 * part, 32), 32)
+        ],
+        32, rest, tn,
+    )
+
+    weights.begin()
+    outs.begin()
+    mine = pl.ds(pl.multiple_of(me.c * 96, 96), 96)
+    keep = [
+        pltpu.make_async_copy(wq_s, wq.at[mine], s_l.at[0]),
+        pltpu.make_async_copy(wo_s, wo_t.at[mine], s_l.at[1]),
+    ] + [
+        pltpu.make_async_copy(wf_s.at[:, 896 * p : 896 * p + 896], wf.at[p, mine], s_l.at[2 + p])
+        for p in range(3)
+    ]
+    for k in keep:
+        k.start()
+
+    def norm_rows(i, carry):
+        rows = pl.ds(pl.multiple_of(i * 64, 64), 64)
+        value = x_ref[rows].astype(F32)
+        normed[rows] = (value * rms_inverse(value)).astype(BF)
+        return carry
+
+    lax.fori_loop(0, tokens // 64, norm_rows, 0)
+    weights.near()
+    weights.pair()
+    outs.near()
+    outs.pair()
+    weights.far()
+    weights.last()
+    outs.far()
+    feed[0].begin()
+    keep[0].wait()
+    weights.end()
+
+    def project(i, carry):
+        cols = pl.ds(pl.multiple_of(i * 256, 256), 256)
+        raw[:, cols] = dot(normed[cols], wq[...]).T
+        return carry
+
+    lax.fori_loop(0, tokens // 256, project, 0)
+    query_gain, key_gain = gain_columns(wq)
+    cosine, sine = cos_ref[...], sin_ref[...]
+
+    def turned(value, gain):
+        hat = value * column_inverse(value) * gain
+        a, b = hat[:32], hat[32:]
+        return jnp.concatenate([a * cosine - b * sine, b * cosine + a * sine], axis=0)
+
+    both = jnp.concatenate([turned(raw[192:256], key_gain), raw[256:320]], axis=0)
+    kv[pl.ds(pl.multiple_of(me.c * tokens, tokens), tokens)] = both.T.astype(BF)
+    keys.begin()
+    qt[64:128] = jnp.zeros((64, 3 * tokens), BF)
+    for h in range(3):
+        qt[0:64, h * tokens : (h + 1) * tokens] = (
+            turned(raw[64 * h : 64 * h + 64], query_gain) * (LOG2E / 8.0)
+        ).astype(BF)
+    outs.last()
+    keep[1].wait()
+    outs.end()
+    heads = wo_t[...].T
+    wo[pl.ds(pl.multiple_of(me.t * 192 + me.core * 96, 96), 96)] = jnp.where(
+        me.core == 0, heads[0:96], heads[96:192]
+    )
+    outw.begin()
+    feed[1].begin()
+    acc[...] = jnp.zeros_like(acc)
+    ones = jnp.concatenate([jnp.ones((1, 1024), BF), jnp.zeros((15, 1024), BF)], axis=0)
+    apart = lax.broadcasted_iota(jnp.int32, (256, 256), 0) - lax.broadcasted_iota(
+        jnp.int32, (256, 256), 1
+    )
+
+    def attend(h, place, slot):
+        rows = kv[pl.ds(pl.multiple_of(place * 1024, 1024), 1024), :]
+        scores = dot(rows, qt[:, pl.ds(pl.multiple_of(h * tokens, tokens), tokens)])
+        parts = []
+        for a in range(4):
+            line = []
+            for b in range(2):
+                sub = scores[a * 256 : a * 256 + 256, b * 256 : b * 256 + 256]
+                seen = apart <= kb[me.c * 2 + b] - kb[place * 4 + a]
+                line.append(jnp.where(seen, jnp.exp2(sub), 0.0).astype(BF))
+            parts.append(jnp.concatenate(line, axis=1))
+        weight = jnp.concatenate(parts, axis=0)
+        pbuf[slot] = weight
+        left = jnp.concatenate([rows.T[64:128], ones], axis=0)
+        return dot(left, weight)
+
+    def store(h, place, slot):
+        return pltpu.make_async_copy(pbuf.at[slot], p_all.at[place, h], s_p.at[slot])
+
+    def close(h):
+        total = acc[h, 64:65]
+        sums[0:1, h * tokens : (h + 1) * tokens] = total
+        value = (acc[h, 0:64] / total).astype(BF)
+        att_own[64 * h : 64 * h + 64] = value
+        att[pl.ds(pl.multiple_of(me.t * 192 + 64 * h, 64), 64)] = value
+        share[h].begin()
+
+    def first_head(step, carry):
+        @pl.when(step == 0)
+        def _():
+            keys.got(9)
+
+        @pl.when(step == 1)
+        def _():
+            keys.near()
+            keys.got(11)
+
+        @pl.when(step == 2)
+        def _():
+            keys.pair()
+            keys.got(12)
+
+        @pl.when(step == 3)
+        def _():
+            keys.got(10)
+            feed[0].near()
+
+        @pl.when(step == 4)
+        def _():
+            keys.far()
+            keys.got(13)
+            outw.near()
+
+        @pl.when(step == 5)
+        def _():
+            keys.got(14)
+            feed[0].pair()
+            outw.pair()
+
+        @pl.when(step == 6)
+        def _():
+            keys.last()
+            keys.got(15)
+            feed[2].begin()
+
+        @pl.when(step == 7)
+        def _():
+            keys.got(16)
+
+        place = chip_of(me, step, PAIRS)
+        slot = lax.rem(step, 4)
+
+        @pl.when(step >= 4)
+        def _():
+            store(0, place, slot).wait()
+
+        acc[0] += attend(0, place, slot)
+        store(0, place, slot).start()
+        return carry
+
+    lax.fori_loop(0, 8, first_head, 0)
+    close(0)
+
+    def more_heads(i, carry):
+        @pl.when(i == 0)
+        def _():
+            feed[1].near()
+            outw.far()
+
+        @pl.when(i == 1)
+        def _():
+            feed[0].far()
+            feed[1].pair()
+
+        @pl.when(i == 2)
+        def _():
+            share[0].near()
+            share[0].pair()
+            outw.last()
+
+        @pl.when(i == 3)
+        def _():
+            feed[0].last()
+            share[0].far()
+
+        @pl.when(i == 4)
+        def _():
+            close(1)
+            share[0].last()
+            feed[2].near()
+
+        @pl.when(i == 5)
+        def _():
+            feed[1].far()
+            feed[2].pair()
+
+        @pl.when(i == 6)
+        def _():
+            share[1].near()
+            share[1].pair()
+
+        @pl.when(i == 7)
+        def _():
+            feed[1].last()
+            share[1].far()
+
+        h = 1 + i // 4
+        for half in range(2):
+            place = chip_of(me, 2 * lax.rem(i, 4) + half, PAIRS)
+            slot = 2 * lax.rem(i, 2) + half
+            store(h, place, slot).wait()
+            acc[h] += attend(h, place, slot)
+            store(h, place, slot).start()
+        return carry
+
+    lax.fori_loop(0, 8, more_heads, 0)
+    close(2)
+    share[1].last()
+    share[2].near()
+    share[2].pair()
+    feed[2].far()
+    share[2].far()
+    share[2].last()
+    feed[2].last()
+    outw.end()
+    keep[2].wait()
+    keep[3].wait()
+    feed[0].end()
+    feed[1].end()
+
+    def forward_rows(i, carry):
+        rows = pl.ds(pl.multiple_of(i * 256, 256), 256)
+        value = x_ref[rows].astype(F32) + dot(att[:, rows].T, wo[...])
+        inverse = rms_inverse(value)
+        mid[rows] = value
+        inv[rows] = jnp.broadcast_to(inverse, (256, 128))
+        hidden = (value * inverse).astype(BF)
+        low[rows] = hidden
+        g = dot(hidden, wf[0])
+        u = dot(hidden, wf[1])
+        gate[rows] = g
+        up[rows] = u
+        a = (g * jax.nn.sigmoid(g) * u).astype(BF)
+        act[rows] = a
+
+        @pl.when(i == 0)
+        def _():
+            keep[4].wait()
+            feed[2].end()
+
+        ffn[rows] = dot_nt(a, wf[2]).astype(BF)
+        return carry
+
+    lax.fori_loop(0, 2, forward_rows, 0)
+    sum_f.begin()
+    gain_two[...] = jnp.zeros_like(gain_two)
+
+    def backward_rows(i, carry):
+        @pl.when(i == 1)
+        def _():
+            sum_f.relay()
+
+        rows = pl.ds(pl.multiple_of(i * 256, 256), 256)
+        ct = cot[rows]
+        g, u = gate[rows], up[rows]
+        sig = jax.nn.sigmoid(g)
+        grad_act = dot(ct, wf[2])
+        gg = (grad_act * u * sig * (1.0 + g * (1.0 - sig))).astype(BF)
+        gu = (grad_act * g * sig).astype(BF)
+        grad_g[rows] = gg
+        grad_u[rows] = gu
+        back = dot_nt(gg, wf[0]) + dot_nt(gu, wf[1])
+        hat = low[rows].astype(F32)
+        both = back * hat
+        gain_two[...] += jnp.sum(both, axis=0, keepdims=True)
+        pull = jnp.mean(both, axis=-1, keepdims=True)
+        part = (ct.astype(F32) * 0.125 + inv[rows][:, 0:1] * (back - hat * pull)).astype(BF)
+        share_ref[rows] = part
+        u_ref[:, rows] = dot_nt(wo[...], part).astype(BF)
+        return carry
+
+    lax.fori_loop(0, 2, backward_rows, 0)
+    sum_f.column()
+    own = pl.multiple_of(me.t * 64, 64)
+    block[0:32] = (mid[pl.ds(own, 32)] + sum_f.finish(0)).astype(BF)
+    block[32:64] = (mid[pl.ds(pl.multiple_of(own + 32, 32), 32)] + sum_f.finish(1)).astype(BF)
+    keys.sent()
+    sum_f.sent()
+    for s in share:
+        s.sent()
+    for slot in range(4):
+        store(0, 0, slot).wait()
+
+
+def forward_part(*operands):
+    tokens = 512
+    shapes = [
+        jax.ShapeDtypeStruct((1536, 384), BF),
+        jax.ShapeDtypeStruct((16 * tokens, 128), BF),
+        jax.ShapeDtypeStruct((128, 3 * tokens), BF),
+        jax.ShapeDtypeStruct((384, tokens), F32),
+        jax.ShapeDtypeStruct((8, 3 * tokens), F32),
+        jax.ShapeDtypeStruct((tokens, 1536), BF),
+        jax.ShapeDtypeStruct((192, tokens), BF),
+        jax.ShapeDtypeStruct((1536, tokens), BF),
+        jax.ShapeDtypeStruct((tokens, 1536), BF),
+        jax.ShapeDtypeStruct((64, 1536), BF),
+        jax.ShapeDtypeStruct((1, 1536), F32),
+        jax.ShapeDtypeStruct((tokens, 1536), BF),
+        jax.ShapeDtypeStruct((tokens, 896), BF),
+        jax.ShapeDtypeStruct((tokens, 896), BF),
+        jax.ShapeDtypeStruct((tokens, 896), BF),
+        jax.ShapeDtypeStruct((8, 3, 1024, tokens), BF),
+    ]
+    scratch = [
+        pltpu.VMEM((1536, 256), BF),
+        pltpu.VMEM((3, 1536, 896), BF),
+        pltpu.VMEM((1536, 1536), BF),
+        pltpu.VMEM((1536, tokens), BF),
+        pltpu.VMEM((3, 80, tokens), F32),
+        pltpu.VMEM((4, 1024, tokens), BF),
+        pltpu.VMEM((tokens, 1536), F32),
+        pltpu.VMEM((tokens, 128), F32),
+        pltpu.VMEM((tokens, 896), F32),
+        pltpu.VMEM((tokens, 896), F32),
+        pltpu.VMEM((tokens, 1536), BF),
+        *[DMA((17,))] * 4,
+        *[DMA((3, 17))] * 2,
+        *[DMA((17,))] * 4,
+        *[DMA((3, 9))] * 2,
+        DMA((5,)),
+        DMA((4,)),
+        *ring_scratch(32, 1536),
+    ]
+    return pl.pallas_call(
+        forward_kernel,
+        out_shape=shapes,
+        in_specs=[SM] + [VM] * 7,
+        out_specs=[VM] * 15 + [HB],
+        scratch_shapes=scratch,
+        name="forward_part",
+        compiler_params=pltpu.CompilerParams(
+            collective_id=0, has_side_effects=True, vmem_limit_bytes=59 << 20
+        ),
+    )(*operands)
+
+
 def backward_kernel(
-    kb, u_ref, ffn_ref, share_ref, mid_ref, gate_g, up_g, down_g, gain_two,
-    x_ref, normed, wq, raw, att_own, sums, qt, kv, cos_ref, sin_ref,
+    kb, u_ref, share_ref, block, cot, low, act, grad_g, grad_u, gain_two,
+    x_ref, normed, wq, raw, att_own, sums, qt, kv, cos_ref, sin_ref, p_all,
     two, gin, own_q, own_w, gains,
-    mid_rows, gt, drift, dq, gk, gk_sib, part_w, sib_w, pw, sib_p, back, pre, extra,
-    s_two, r_two, s_in, r_in, s_ex, r_ex, s_sib, r_sib, s_loc,
+    mid_rows, own_two, branch, gt, drift, dq, gk, gk_sib, wg, sib_w, pw, sib_p, back, pre, extra,
+    s_two, r_two, s_in, r_in, s_ex, r_ex, s_sib, r_sib, s_loc, s_p,
     *rest,
 ):
     me = Place()
@@ -538,19 +718,15 @@
 
         return src
 
-    def two_rows(k, part):
-        ref = share_ref if part else ffn_ref
-        return ref.at[pl.ds(pl.multiple_of(tp_block(k) * 64, 64), 64)]
-
     sum_u = ring(rows_of(u_ref, 192), 96, scratch[0], tn, True)
-    sum_two = ring(two_rows, 64, scratch[1], tn, True)
+    sum_two = ring(rows_of(share_ref, 64), 32, scratch[1], tn, True)
     sum_b = ring(rows_of(back, 64), 32, scratch[2], tn)
     sum_kv = ring(
         lambda k, part: gk.at[k, me.core, pl.ds(64 * part, 64)], 64, scratch[3], cn
     )
     sum_w = [
         ring(
-            lambda k, part, p=p: part_w.at[p, chip(k), pl.ds(48 * part, 48)],
+            lambda k, part, p=p: wg.at[p, chip(k), me.core, pl.ds(48 * part, 48)],
             48,
             scratch[4 + p],
             cn,
@@ -560,7 +736,7 @@
     sum_q = ring(
         lambda k, part: pw.at[chip(k), me.core, pl.ds(48 * part, 48)], 48, scratch[7], cn
     )
-    put_two = Gather(two, 128, me.tp, *tn, None, s_two, r_two)
+    put_two = Gather(two, 128, me.tp, *tn, None, s_two, r_two, own=own_two)
     put_in = Gather(gin, 64, me.tp, *tn, None, s_in, r_in)
     put_ex = Gather(extra, 96, me.tp, *tn, None, s_ex, r_ex)
 
@@ -577,39 +753,61 @@
     def key_swap(k):
         return to_sibling(k, gk.at[k, 1 - me.core], gk_sib.at[k])
 
-    swap_w = [
-        to_sibling(8 + p, g.at[:, 1 - me.core], sib_w.at[p])
-        for p, g in enumerate((gate_g, up_g, down_g))
-    ]
+    swap_w = [to_sibling(8 + p, wg.at[p, :, 1 - me.core], sib_w.at[p]) for p in range(3)]
     swap_p = to_sibling(11, pw.at[:, 1 - me.core], sib_p)
-    keep_w = [
-        pltpu.make_async_copy(g.at[:, me.core], part_w.at[p], s_loc.at[p])
-        for p, g in enumerate((gate_g, up_g, down_g))
-    ]
 
     sum_u.begin()
-    for p in range(3):
-        swap_w[p].start()
-        keep_w[p].start()
+
+    def weight_grads(b_low, b_cot, b_act, b_g, b_u):
+        loads = [
+            pltpu.make_async_copy(h, v, s_loc.at[k])
+            for k, (h, v) in enumerate(
+                [(low, b_low), (grad_g, b_g), (grad_u, b_u), (cot, b_cot), (act, b_act)]
+            )
+        ]
+        for k in loads:
+            k.start()
+        loads[0].wait()
+        for p, (left, right) in enumerate([(b_low, b_g), (b_low, b_u), (b_cot, b_act)]):
+            loads[1 + p].wait()
+            if p == 2:
+                loads[4].wait()
+
+            def chunk(i, carry, p=p, left=left, right=right):
+                at = pl.ds(pl.multiple_of(384 * i, 384), 384)
+                whole = dot(left[:, at].T, right[...]).astype(BF)
+                for q in range(4):
+                    wg[p, 2 * i + q // 2, q % 2] = whole[96 * q : 96 * q + 96]
+                return carry
+
+            lax.fori_loop(0, 4, chunk, 0)
+            swap_w[p].start()
+            if p == 0:
+                sum_u.relay()
+            if p == 1:
+                sum_u.column()
+
+    pl.run_scoped(
+        weight_grads,
+        pltpu.VMEM((tokens, 1536), BF),
+        pltpu.VMEM((tokens, 1536), BF),
+        pltpu.VMEM((tokens, 896), BF),
+        pltpu.VMEM((tokens, 896), BF),
+        pltpu.VMEM((tokens, 896), BF),
+    )
 
     def join_w(p):
-        keep_w[p].wait()
         swap_w[p].wait_recv()
 
         def one(j, carry):
-            add_into(part_w.at[p, j], part_w.at[p, j], sib_w.at[p, j])
+            add_into(wg.at[p, j, me.core], wg.at[p, j, me.core], sib_w.at[p, j])
             return carry
 
         lax.fori_loop(0, 8, one, 0)
 
-    sum_u.relay()
     join_w(0)
     sum_w[0].begin()
-    sum_u.column()
-    join_w(1)
-    join_w(2)
-    halves = [sum_u.finish(0), sum_u.finish(1)]
-    grad_att = jnp.concatenate(halves, axis=0)
+    grad_att = jnp.concatenate([sum_u.finish(0), sum_u.finish(1)], axis=0)
     sum_two.begin()
     gt[0:64] = jnp.zeros((64, 3 * tokens), BF)
     for h in range(3):
@@ -622,105 +820,117 @@
             * inverse
         )
     dq[...] = jnp.zeros_like(dq)
-    sum_w[0].relay()
-    sum_w[1].begin()
-    apart = lax.broadcasted_iota(jnp.int32, (256, 256), 0) - lax.broadcasted_iota(
-        jnp.int32, (256, 256), 1
-    )
 
     def join_keys(k):
         key_swap(k).wait_recv()
         add_into(gk.at[k, me.core], gk.at[k, me.core], gk_sib.at[k])
 
-    def key_step(step, carry):
-        @pl.when(step == 1)
-        def _():
-            join_keys(0)
-            sum_kv.go(2, 3)
-            sum_w[0].column()
-            sum_w[1].relay()
-            sum_w[2].begin()
-
-        @pl.when(step == 2)
-        def _():
-            join_keys(1)
-            sum_kv.go(0, 1)
-            sum_two.relay()
-
-        @pl.when(step == 3)
-        def _():
-            join_keys(2)
-            sum_kv.go(4)
-            sum_kv.relay_right(1)
-            sum_w[2].relay()
-            sum_w[1].column()
-
-        @pl.when(step == 4)
-        def _():
-            join_keys(3)
-            sum_kv.go(5)
-            sum_kv.relay_left(1)
-            sum_two.column()
-
-        @pl.when(step == 5)
-        def _():
-            join_keys(4)
-            sum_kv.go(6)
-            sum_kv.relay_right(0)
-            sum_w[2].column()
-
-        @pl.when(step == 6)
-        def _():
-            join_keys(5)
-            sum_kv.go(7)
-            sum_kv.relay_left(0)
-            own = pl.multiple_of(me.t * 128, 128)
-            two[pl.ds(own, 64)] = (mid_ref[...] + sum_two.finish(0)).astype(BF)
-            branch = sum_two.finish(1)
-            mid_rows[...] = branch
-            two[pl.ds(own + 64, 64)] = branch.astype(BF)
-            put_two.begin()
-
-        @pl.when(step == 7)
-        def _():
-            join_keys(6)
-            sum_kv.column()
-            for p in range(3):
+    def key_loop(pbuf):
+        def load(step, slot):
+            return pltpu.make_async_copy(
+                p_all.at[chip_of(me, step, SLOTS)], pbuf.at[slot], s_p.at[slot]
+            )
+
+        load(0, 0).start()
+
+        def key_step(step, carry):
+            slot = lax.rem(step, 2)
+
+            @pl.when(step < 7)
+            def _():
+                load(step + 1, 1 - slot).start()
+
+            @pl.when(step == 0)
+            def _():
+                sum_w[0].relay()
+                join_w(1)
+                sum_w[1].begin()
+
+            @pl.when(step == 1)
+            def _():
+                join_keys(0)
+                sum_kv.go(2, 3)
+                sum_w[0].column()
+
+            @pl.when(step == 2)
+            def _():
+                join_keys(1)
+                sum_kv.go(0, 1)
+                sum_two.relay()
+                sum_w[1].relay()
+                join_w(2)
+                sum_w[2].begin()
+
+            @pl.when(step == 3)
+            def _():
+                join_keys(2)
+                sum_kv.go(4)
+                sum_kv.relay_right(1)
+                sum_w[1].column()
+                sum_two.column()
+
+            @pl.when(step == 4)
+            def _():
+                join_keys(3)
+                sum_kv.go(5)
+                sum_kv.relay_left(1)
+                sum_w[2].relay()
+                branch_rows = jnp.concatenate([sum_two.finish(0), sum_two.finish(1)], axis=0)
+                mid_rows[...] = branch_rows
+                own_two[0:64] = block[...]
+                own_two[64:128] = branch_rows.astype(BF)
+                put_two.begin()
+                keep_two.start()
+
+            @pl.when(step == 5)
+            def _():
+                join_keys(4)
+                sum_kv.go(6)
+                sum_kv.relay_right(0)
                 for half in range(2):
-                    own_w[p, 48 * half : 48 * half + 48] = sum_w[p].finish(half)
-
-        place = slot_chip(me, step)
-        rows = kv[pl.ds(pl.multiple_of(place * 1024, 1024), 1024), :]
-        key_t = rows.T[0:64]
-        key_grad = value_grad = 0.0
-        for h in range(3):
-            cols = slice(h * tokens, (h + 1) * tokens)
-            scores = dot(rows, qt[:, cols])
-            slopes = dot(rows, gt[:, cols])
-            parts, grads = [], []
-            for a in range(4):
-                line, grad_line = [], []
-                for b in range(2):
-                    at = (slice(a * 256, a * 256 + 256), slice(b * 256, b * 256 + 256))
-                    seen = apart <= kb[me.c * 2 + b] - kb[place * 4 + a]
-                    weight = jnp.where(seen, jnp.exp2(scores[at]), 0.0)
-                    line.append(weight.astype(BF))
-                    lean = drift[0:1, h * tokens + b * 256 : h * tokens + b * 256 + 256]
-                    grad_line.append((weight * (slopes[at] - lean)).astype(BF))
-                parts.append(jnp.concatenate(line, axis=1))
-                grads.append(jnp.concatenate(grad_line, axis=1))
-            weight = jnp.concatenate(parts, axis=0)
-            grad = jnp.concatenate(grads, axis=0)
-            dq[:, cols] += dot(key_t, grad)
-            key_grad += dot_nt(qt[0:64, cols], grad)
-            value_grad += dot_nt(gt[64:128, cols], weight)
-        both = jnp.concatenate([key_grad * LN2, value_grad], axis=0).astype(BF)
-        gk[step, 0] = both[:, 0:512]
-        gk[step, 1] = both[:, 512:1024]
-        key_swap(step).start()
-        return carry
-
-    lax.fori_loop(0, 8, key_step, 0)
+                    own_w[0, 48 * half : 48 * half + 48] = sum_w[0].finish(half)
+
+            @pl.when(step == 6)
+            def _():
+                join_keys(5)
+                sum_kv.go(7)
+                sum_kv.relay_left(0)
+                put_two.near()
+                sum_w[2].column()
+
+            @pl.when(step == 7)
+            def _():
+                join_keys(6)
+                sum_kv.column()
+                put_two.pair()
+                for half in range(2):
+                    own_w[1, 48 * half : 48 * half + 48] = sum_w[1].finish(half)
+
+            place = chip_of(me, step, SLOTS)
+            load(step, slot).wait()
+            rows = kv[pl.ds(pl.multiple_of(place * 1024, 1024), 1024), :]
+            key_t = rows.T[0:64]
+            key_grad = value_grad = 0.0
+            for h in range(3):
+                cols = slice(h * tokens, (h + 1) * tokens)
+                slopes = dot(rows, gt[:, cols])
+                weight = pbuf[slot, h]
+                grad = (weight.astype(F32) * (slopes - drift[0:1, cols])).astype(BF)
+                dq[:, cols] += dot(key_t, grad)
+                key_grad += dot_nt(qt[0:64, cols], grad)
+                value_grad += dot_nt(gt[64:128, cols], weight)
+            both = jnp.concatenate([key_grad * LN2, value_grad], axis=0).astype(BF)
+            gk[step, 0] = both[:, 0:512]
+            gk[step, 1] = both[:, 512:1024]
+            key_swap(step).start()
+            return carry
+
+        lax.fori_loop(0, 8, key_step, 0)
+
+    keep_two = pltpu.make_async_copy(
+        own_two, two.at[pl.ds(pl.multiple_of(me.t * 128, 128), 128)], s_loc.at[5]
+    )
+    pl.run_scoped(key_loop, pltpu.VMEM((2, 3, 1024, tokens), BF))
     query_gain, key_gain = gain_columns(wq)
     cosine, sine = cos_ref[...], sin_ref[...]
 
@@ -741,8 +951,7 @@
         )
         query_gain_grad += part
         pre[64 * h : 64 * h + 64] = grad
-    put_two.near()
-    put_two.pair()
+    put_two.far()
     join_keys(7)
     key_grad, value_grad = sum_kv.finish(0), sum_kv.finish(1)
     key_gain_grad, grad = unturn(key_grad, raw[192:256], key_gain)
@@ -753,10 +962,22 @@
     gain_one = 0.0
     for i in range(2):
         rows = slice(256 * i, 256 * i + 256)
-        part = dot_nt(pre_n[rows], wq[:, 0:384])
+        part = dot_nt(pre_n[rows], wq[...])
         back[rows] = part.astype(BF)
         gain_one += jnp.sum(part * normed[rows].astype(F32), axis=0, keepdims=True)
     sum_b.begin()
+    put_two.last()
+    keep_two.wait()
+    fetch = [
+        pltpu.make_async_copy(
+            two.at[pl.ds(128 * b + 64, 64)], branch.at[pl.ds(64 * b, 64)], s_loc.at[6 + b]
+        )
+        for b in range(8)
+    ]
+    for f in fetch:
+        f.start()
+    for half in range(2):
+        own_w[2, 48 * half : 48 * half + 48] = sum_w[2].finish(half)
     lane = lax.broadcasted_iota(jnp.int32, (64, 1536), 1)
     unit = lax.broadcasted_iota(jnp.int32, (64, 1536), 0)
     spot = lane == (unit // 4) * 96 + lax.rem(unit, 4)
@@ -776,18 +997,15 @@
         axis=0,
     )
     sides = lines.T
-    put_two.far()
-    put_two.last()
     sum_b.relay()
     att_n = jnp.concatenate([att_own[...].astype(F32), jnp.zeros((64, tokens), F32)], axis=0).T.astype(BF)
+    for f in fetch:
+        f.wait()
     for i in range(4):
         at = slice(384 * i, 384 * i + 384)
         part = dot(normed[:, at].T, pre_n)
         part = jnp.concatenate([part[:, 0:256], part[:, 256:384] + sides[at]], axis=1)
-        branch = jnp.concatenate(
-            [two[128 * b + 64 : 128 * b + 128, at] for b in range(8)], axis=0
-        )
-        whole = jnp.concatenate([part, dot(branch.T, att_n)], axis=1).astype(BF)
+        whole = jnp.concatenate([part, dot(branch[:, at].T, att_n)], axis=1).astype(BF)
         for q in range(4):
             pw[2 * i + q // 2, q % 2] = whole[96 * q : 96 * q + 96]
     swap_p.start()
@@ -828,7 +1046,7 @@
     for b in range(1, 8):
         total += extra[96 * b : 96 * b + 96]
     gains[...] = total
-    for s in [sum_u, sum_two, sum_b, sum_kv, sum_q, *sum_w, put_two, put_in, put_ex, ]:
+    for s in [sum_u, sum_two, sum_b, sum_kv, sum_q, *sum_w, put_two, put_in, put_ex]:
         s.sent()
     for k in range(8):
         key_swap(k).wait_send()
@@ -847,12 +1065,14 @@
     ]
     scratch = [
         pltpu.VMEM((64, 1536), F32),
+        pltpu.VMEM((128, 1536), BF),
+        pltpu.VMEM((tokens, 1536), BF),
         pltpu.VMEM((128, 3 * tokens), BF),
         pltpu.VMEM((8, 3 * tokens), F32),
         pltpu.VMEM((64, 3 * tokens), F32),
         pltpu.VMEM((8, 2, 128, 512), BF),
         pltpu.VMEM((8, 128, 512), BF),
-        pltpu.VMEM((3, 8, 96, 896), BF),
+        pltpu.VMEM((3, 8, 2, 96, 896), BF),
         pltpu.VMEM((3, 8, 96, 896), BF),
         pltpu.VMEM((8, 2, 96, 640), BF),
         pltpu.VMEM((8, 96, 640), BF),
@@ -862,9 +1082,10 @@
         *[DMA((9,))] * 6,
         DMA((12,)),
         DMA((12,)),
-        DMA((3,)),
+        DMA((14,)),
+        DMA((2,)),
         *ring_scratch(96, 512, True),
-        *ring_scratch(64, 1536, True),
+        *ring_scratch(32, 1536, True),
         *ring_scratch(32, 1536),
         *ring_scratch(64, 512),
         *ring_scratch(48, 896) * 3,
@@ -873,12 +1094,12 @@
     return pl.pallas_call(
         backward_kernel,
         out_shape=shapes,
-        in_specs=[SM, VM, VM, VM, VM, HB, HB, HB] + [VM] * 11,
-        out_specs=[VM] * 5,
+        in_specs=[SM, VM, VM, VM, HB, HB, HB, HB, HB] + [VM] * 11 + [HB],
+        out_specs=[HB] + [VM] * 4,
         scratch_shapes=scratch,
         name="backward_part",
         compiler_params=pltpu.CompilerParams(
-            collective_id=1, has_side_effects=True, vmem_limit_bytes=58 << 20
+            collective_id=1, has_side_effects=True, vmem_limit_bytes=59 << 20
         ),
     )(*operands)
 
@@ -918,11 +1139,10 @@
             lifted(key_weight, gain_one),
             lifted(value_weight, gain_one),
             padded(head_gains, 64),
-            output_weight.T,
-            jnp.zeros((96, 64), BF),
         ],
         axis=1,
     )
+    wo_s = padded(output_weight.T, 256)
     wf_s = jnp.concatenate(
         [
             padded(lifted(gate_weight, gain_two), 896),
@@ -931,42 +1151,14 @@
         ],
         axis=1,
     )
-    wq, wf, wo, kv, qt, raw, att, sums, normed = forward_part(
-        kb, block_input, wq_s, wf_s, cosine, sine
-    )
-    x = block_input.astype(F32)
-    mid = x + dot_tn(att, wo)
-    inv_two = rms_inverse(mid)
-    normed_two = mid * inv_two
-    low_two = normed_two.astype(BF)
-    gate_full, up_full, down_full = wf[:, 0:896], wf[:, 896:1792], wf[:, 1792:2688]
-    gate = dot(low_two, gate_full)
-    up = dot(low_two, up_full)
-    sig = jax.nn.sigmoid(gate)
-    act = (gate * sig * up).astype(BF)
-    ffn_part = dot_nt(act, down_full).astype(BF)
-    grad_act = dot(out_cotangent, down_full)
-    grad_gate = (grad_act * up * sig * (1.0 + gate * (1.0 - sig))).astype(BF)
-    grad_up = (grad_act * gate * sig).astype(BF)
-
-    def blocks(grad):
-        return grad.astype(BF).reshape(8, 2, 96, 896)
-
-    down_grad = blocks(dot_tn(out_cotangent, act))
-    gate_grad = blocks(dot_tn(low_two, grad_gate))
-    up_grad = blocks(dot_tn(low_two, grad_up))
-    back_two = dot_nt(grad_gate, gate_full) + dot_nt(grad_up, up_full)
-    gain_two_part = jnp.sum(back_two * normed_two, axis=0, keepdims=True)
-    pull = jnp.mean(back_two * normed_two, axis=-1, keepdims=True)
-    share_mid = (
-        out_cotangent.astype(F32) * 0.125 + inv_two * (back_two - normed_two * pull)
-    ).astype(BF)
-    grad_att = dot_nt(wo, share_mid).astype(BF)
-    mid_rows = lax.dynamic_slice_in_dim(mid, t * 64, 64, 0)
-    att_own = lax.dynamic_slice_in_dim(att, t * 192, 192, 0)
+    (
+        wq, kv, qt, raw, sums, normed, att_own, u, share, block, gain_two_part, low, act, grad_g,
+        grad_u, p_all,
+    ) = forward_part(kb, block_input, out_cotangent, wq_s, wo_s, wf_s, cosine, sine)
     two, gin, own_q, own_w, gains = backward_part(
-        kb, grad_att, ffn_part, share_mid, mid_rows, gate_grad, up_grad, down_grad, gain_two_part,
-        lax.dynamic_slice_in_dim(block_input, t * 64, 64, 0), normed, wq, raw, att_own, sums, qt, kv, cosine, sine,
+        kb, u, share, block, out_cotangent, low, act, grad_g, grad_u, gain_two_part,
+        lax.dynamic_slice_in_dim(block_input, t * 64, 64, 0),
+        normed, wq, raw, att_own, sums, qt, kv, cosine, sine, p_all,
     )
     return (
         two.reshape(8, 2, 64, 1536)[:, 0].reshape(tokens, 1536),

time: 313 us -> 274 us (0.88)
  matrix products: 34.1 us -> 0.93 us
  local copies, waits for them, and re-layouts: 19.2 us -> 12.9 us
  Pallas kernels: 242 us -> 248 us
    dot_general x11 -> x0, matrix products: 33.2 us -> none  [the longest x4 16.6 us: dot_tn(): lax.dot_general(a, b, (((0,), (0,)), ((), ())), preferred_element_type=F32)]
    pallas_call x1, Pallas kernels: 89.2 us -> 115 us  [forward_part(): pl.pallas_call(forward_kernel, out_shape=shapes, in_specs=[SM] + [VM] * 7...]
    pallas_call x1, Pallas kernels: 153 us -> 133 us  [backward_part(): pl.pallas_call(backward_kernel, out_shape=shapes, in_specs=[SM, VM, VM, V...]
where the time goes in v3:
time: 274 us; the launch traced here: 273 us
  Pallas kernels  248 us (91%)
  local copies, waits for them, and re-layouts  12.9 us (5%)
  other arithmetic  10.2 us (4%)
    pallas_call x1, Pallas kernels, backward_part(): pl.pallas_call(backward_kernel, out_shape=shapes, in_specs=[SM, VM, VM, V...  133 us
    pallas_call x1, Pallas kernels, forward_part(): pl.pallas_call(forward_kernel, out_shape=shapes, in_specs=[SM] + [VM] * 7...  115 us

profile of v3, /device:TPU:0, one launch (start us, length us, event | category | flops | bytes accessed | tf_op | source)
XLA Modules:
  0.0 272.7 jit_solution(3540792281858628912)
XLA Ops:
  0.6 0.0 copy-start
  0.7 0.0 copy-start.7
  0.7 0.0 copy-start.6
  0.7 0.0 copy-start.5
  0.7 0.7 convert_element_type.55
  1.4 0.7 convert_element_type.62
  2.1 0.0 copy-done
  2.1 0.1 fusion.1
  2.2 0.8 fusion.3
  3.1 0.8 dynamic-slice_convert_fusion
  3.8 0.1 copy.60
  4.0 0.8 reshape.46
  4.7 0.6 slice_reduce_fusion.2.kb
  5.4 0.9 multiply_convert_fusion.2
  6.2 0.8 copy.58
  7.1 0.8 copy.59
  7.9 0.1 multiply_convert_fusion.4
  8.0 0.7 fusion.11.wq_s
  8.7 0.9 copy.61
  9.6 0.6 pad.19.wo_s
  10.2 1.0 multiply_sine_fusion
  11.2 1.6 constant_dynamic-slice_fusion.x_ref
  12.8 0.0 copy-done.6
  12.8 0.0 copy-done.5
  12.8 0.1 multiply_convert_fusion.1
  12.9 0.0 copy-done.7
  12.9 0.8 fusion.9.wf_s
  13.8 115.4 %forward_part.1 = (bf16[1536,384]{1,0:T(8,128)(2,1)}, bf16[8192,128]{1,0:T(8,128)(2,1)}, bf16[128,1536]{1,0:T(8,128)(2,1)}, f32[384,512]{1,0:T(8,128)}, f32[8,15...) custom-call(s32[32]{0:T(128)} %slice_reduce_fusion.2.kb, ...), custom_call_target="tpu_custom_call" | custom-call | tf_op jit(solution)/shard_map/forward_part/pallas_call | solution.py:678
  129.1 132.5 %backward_part.1 = (bf16[1024,1536]{1,0:T(8,128)(2,1)}, bf16[512,1536]{1,0:T(8,128)(2,1)}, f32[96,640]{1,0:T(8,128)}, f32[3,96,896]{2,1,0:T(8,128)}, f32[96,128]{1,0:T(8,128)}) custom-call(s32[32]{0:T(128)} %slice_reduce_fusion.2.kb, bf16[1536,512]{1,0:T(8,128)(2,1)} %get-tuple-element.34.u_ref, bf16[512,1536]{1,0:T(8,128)(2,1)} %get-tuple-element.35.share_ref, ...), custom_call_target="tpu_custom_call" | custom-call | tf_op jit(solution)/shard_map/backward_part/pallas_call | solution.py:1094
  261.7 0.0 copy-start.4
  261.7 0.0 copy-start.8
  261.7 0.0 copy-start.9
  261.7 0.0 copy-start.3
  261.7 0.0 copy-start.2
  261.7 2.8 %slice.53 = bf16[8,1,64,1536]{3,2,1,0:T(8,128)(2,1)} slice(bf16[8,2,64,1536]{3,2,1,0:T(8,128)(2,1)} %bitcast.37), slice={[0:8], [0:1], [0:64], [0:1536]} | slice | bytes 3145728 | tf_op jit(solution)/shard_map/slice | solution.py:1164
  264.5 0.0 copy-done.4
  264.5 0.7 slice_reduce_fusion.3
  265.2 0.2 slice_reduce_fusion
  265.4 0.5 convert_divide_fusion
  265.9 0.1 slice_multiply_fusion.1
  266.0 0.7 slice_bitcast_fusion.1
  266.7 0.7 copy.64
  267.5 0.7 copy.63
  268.2 0.7 copy.62
  268.9 0.0 copy-done.2
  268.9 0.8 slice_bitcast_fusion
  269.6 1.0 bitcast_multiply_fusion
  270.6 2.1 convert_element_type.67
  (8 shorter events, 0.0 us)
Async XLA Ops:
  0.6 1.5 copy-start
  0.7 12.3 %copy-start.7 = (bf16[864,96]{0,1:T(8,128)(2,1)S(1)}, bf16[864,96]{0,1:T(8,128)(2,1)}, u32[]{:S(2)}) copy-start(bf16[864,96]{0,1:T(8,128)(2,1)} %param.26) | copy-start | bytes 497668
  0.7 12.1 %copy-start.6 = (bf16[96,864]{1,0:T(8,128)(2,1)S(1)}, bf16[96,864]{1,0:T(8,128)(2,1)}, u32[]{:S(2)}) copy-start(bf16[96,864]{1,0:T(8,128)(2,1)} %param.25) | copy-start | bytes 497668
  0.7 12.1 %copy-start.5 = (bf16[96,864]{1,0:T(8,128)(2,1)S(1)}, bf16[96,864]{1,0:T(8,128)(2,1)}, u32[]{:S(2)}) copy-start(bf16[96,864]{1,0:T(8,128)(2,1)} %param.24) | copy-start | bytes 497668
  261.7 2.8 %copy-start.4 = (f32[96,128]{1,0:T(8,128)S(1)}, f32[96,128]{1,0:T(8,128)}, u32[]{:S(2)}) copy-start(f32[96,128]{1,0:T(8,128)} %get-tuple-element.52) | copy-start | bytes 147460
  261.7 3.7 %copy-start.8 = (bf16[96]{0:T(256)(128)(2,1)S(1)}, bf16[96]{0:T(256)(128)(2,1)}, u32[]{:S(2)}) copy-start(bf16[96]{0:T(256)(128)(2,1)} %param.16) | copy-start | bytes 580
  261.7 3.7 %copy-start.9 = (bf16[96]{0:T(256)(128)(2,1)S(1)}, bf16[96]{0:T(256)(128)(2,1)}, u32[]{:S(2)}) copy-start(bf16[96]{0:T(256)(128)(2,1)} %param.23) | copy-start | bytes 580
  261.7 4.2 %copy-start.3 = (f32[96,640]{1,0:T(8,128)S(1)}, f32[96,640]{1,0:T(8,128)}, u32[]{:S(2)}) copy-start(f32[96,640]{1,0:T(8,128)} %get-tuple-element.53) | copy-start | bytes 737284
  261.7 7.2 %copy-start.2 = (f32[3,96,896]{2,1,0:T(8,128)S(1)}, f32[3,96,896]{2,1,0:T(8,128)}, u32[]{:S(2)}) copy-start(f32[3,96,896]{2,1,0:T(8,128)} %get-tuple-element.54) | copy-start | bytes 3096580
  264.5 6.1 %copy-start.1 = (bf16[512,1536]{1,0:T(8,128)(2,1)S(1)}, bf16[512,1536]{1,0:T(8,128)(2,1)}, u32[]{:S(2)}) copy-start(bf16[512,1536]{1,0:T(8,128)(2,1)} %get-tuple-element.51) | copy-start | bytes 4718596

commit v4 on v3

--- a/solution.py
+++ b/solution.py
@@ -50,9 +50,12 @@
 
 
 class Gather:
-    def __init__(self, buf, rows, block, pair, right, left, sibling, send, recv, own=None):
+    def __init__(self, buf, rows, block, pair, right, left, sibling, send, recv, own=None, cross=(), over=False):
         self.buf, self.rows, self.block = buf, rows, block
         self.to = {"z": pair, "r": right, "l": left, "s": sibling}
+        self.cross = len(cross) > 0
+        if self.cross:
+            self.to["zr"], self.to["zl"] = cross
         self.send, self.recv, self.own = send, recv, own
         self.plan = {
             0: ((0, 0), 0, "z"),
@@ -73,6 +76,15 @@
             15: ((1, 1), 0, "s"),
             16: ((1, 2), 0, "s"),
         }
+        if self.cross:
+            self.plan[5] = ((0, 0), 0, "zr")
+            self.plan[6] = ((0, 0), 0, "zl")
+        self.over = over
+        if over:
+            self.plan[5] = ((0, 3), 0, "z")
+            self.plan[6] = ((0, 1), 0, "z")
+            self.plan[7] = ((0, 2), 1, "z")
+            self.plan[8] = ((0, 2), 2, "z")
         self.count = 17 if sibling is not None else 9
 
     def copy(self, k):
@@ -106,18 +118,33 @@
 
     def begin(self):
         self.go(0, 1, 2, 9)
+        if self.cross:
+            self.go(5, 6)
 
     def near(self):
         self.got(1)
         self.go(3, 11)
+        if self.over:
+            self.go(5)
         self.got(2)
         self.go(4, 12)
+        if self.over:
+            self.go(6)
 
     def pair(self):
         self.got(0)
-        self.go(5, 6, 10)
+        if not self.cross and not self.over:
+            self.go(5, 6)
+        self.go(10)
 
     def far(self):
+        if self.over:
+            self.got(3)
+            self.go(7)
+            self.got(4)
+            self.go(8)
+            self.got(5, 6)
+            return
         self.got(5)
         self.go(7, 14)
         self.got(6)
@@ -151,6 +178,10 @@
     return (me.c, me.tp(1, 0)), (me.c, me.tp(0, 1)), (me.c, me.tp(0, 3))
 
 
+def tp_cross(me):
+    return (me.c, me.tp(1, 1)), (me.c, me.tp(1, 3))
+
+
 def rms_inverse(value):
     return lax.rsqrt(jnp.mean(value * value, axis=-1, keepdims=True) + EPS)
 
@@ -187,7 +218,7 @@
     return lax.rem(me.zh + dz, 2) * 4 + lax.rem(me.x + dx, 4)
 
 
-SLOTS = ((0, 2), (1, 2), (1, 1), (1, 3), (0, 1), (0, 3), (1, 0), (0, 0))
+SLOTS = ((1, 2), (0, 2), (1, 1), (1, 3), (0, 1), (0, 3), (1, 0), (0, 0))
 
 
 def add_into(out, *terms):
@@ -198,7 +229,7 @@
 
 
 class RingSum:
-    def __init__(self, src, half, stage, rel_l, rel_r, col_l, col_r, from_z, pair, right, left, send, recv):
+    def __init__(self, src, half, stage, rel_l, rel_r, col_l, col_r, from_z, pair, right, left, send, recv, cross=()):
         self.src, self.half = src, half
         at_stage = {2: (0, 0), 3: (0, 1), 4: (1, 0), 5: (1, 1)}
 
@@ -210,25 +241,29 @@
 
         self.put = put
         self.rel_l, self.rel_r, self.col_l, self.col_r, self.from_z = rel_l, rel_r, col_l, col_r, from_z
-        self.to = {"z": pair, "r": right, "l": left}
+        self.to = {"z": pair, "r": right, "l": left, "zr": right, "zl": left}
+        self.cross = len(cross) > 0
+        if self.cross:
+            self.to["zr"], self.to["zl"] = cross
         self.send, self.recv = send, recv
         low, high = pl.ds(0, half), pl.ds(half, half)
         self.low, self.high = low, high
+        self.last = 14
         self.plan = [
-            (src(1, 0), rel_l.at[1], "r"),
-            (src(1, 1), rel_r.at[1], "l"),
-            (src(0, 0), rel_l.at[0], "r"),
-            (src(0, 1), rel_r.at[0], "l"),
-            (src(2, 1), col_l.at[1, high], "r"),
-            (src(3, 0), col_r.at[1, low], "l"),
+            (src(0, 0), rel_l.at[1], "r"),
+            (src(0, 1), rel_r.at[1], "l"),
+            (src(1, 0), rel_l.at[0], "r"),
+            (src(1, 1), rel_r.at[0], "l"),
+            (src(2, 1), col_l.at[1, high], "zr"),
+            (src(3, 0), col_r.at[1, low], "zl"),
             (src(4, 1), col_l.at[0, high], "r"),
             (src(5, 0), col_r.at[0, low], "l"),
-            (put(2, 0), col_l.at[1, low], "r"),
-            (put(3, 1), col_r.at[1, high], "l"),
+            (put(2, 0), col_l.at[1, low], "zr"),
+            (put(3, 1), col_r.at[1, high], "zl"),
             (put(4, 0), col_l.at[0, low], "r"),
             (put(5, 1), col_r.at[0, high], "l"),
-            (put(6, 0), from_z.at[low], "z"),
-            (put(6, 1), from_z.at[high], "z"),
+            ((src if self.cross else put)(6, 0), from_z.at[low], "z"),
+            ((src if self.cross else put)(6, 1), from_z.at[high], "z"),
         ]
 
     def copy(self, k):
@@ -252,6 +287,8 @@
 
     def begin(self):
         self.go(*range(8))
+        if self.cross:
+            self.go(12, 13)
 
     def relay_right(self, plane):
         k = 2 if plane else 4
@@ -281,17 +318,34 @@
             )
             self.go(12 + part)
 
+    def columns(self, out):
+        self.last = 12
+        self.got(4, 8, 5, 9, 6, 10, 7, 11)
+        for plane, k in ((0, 7), (1, 6)):
+            for part, rows in enumerate((self.low, self.high)):
+                add_into(
+                    out.at[plane, rows],
+                    self.src(k, part),
+                    self.col_l.at[plane, rows],
+                    self.col_r.at[plane, rows],
+                )
+
     def finish(self, part):
         if part == 0:
             self.got(6, 10, 7, 11, 12, 13)
+            if self.cross:
+                self.got(4, 8, 5, 9)
         rows = self.low if part == 0 else self.high
         total = self.src(7, part)[...].astype(F32)
-        for term in (self.col_l.at[0, rows], self.col_r.at[0, rows], self.from_z.at[rows]):
+        terms = [self.col_l.at[0, rows], self.col_r.at[0, rows], self.from_z.at[rows]]
+        if self.cross:
+            terms += [self.col_l.at[1, rows], self.col_r.at[1, rows]]
+        for term in terms:
             total += term[...].astype(F32)
         return total
 
     def sent(self):
-        for k in range(14):
+        for k in range(self.last):
             self.copy(k).wait_send()
 
 
@@ -308,19 +362,123 @@
     ]
 
 
-def ring(src, half, scratch, neighbours, stage=False):
+def ring(src, half, scratch, neighbours, stage=False, cross=()):
     room, rel_l, rel_r, col_l, col_r, from_z, send, recv = scratch
     return RingSum(
         src, half, room if stage else None, rel_l, rel_r, col_l, col_r, from_z, *neighbours[:3],
-        send, recv,
+        send, recv, cross,
     )
+
+
+def gain_lines(lines, refs):
+    lines[...] = jnp.zeros_like(lines)
+    for k, ref in enumerate(refs):
+        lines[k : k + 1, 0 : ref.shape[1]] = ref[...].astype(F32)
+    columns = lines[...].T
+    return columns[0:96, 0:1], columns[0:96, 1:2]
+
+
+def prepare_kernel(
+    places, attn_gain, ffn_gain, query_gain, key_gain, freq,
+    query, key_t, value_t, output, gate, up, down_t, wq_s, wo_s, wf_s, cosine, sine, lines,
+):
+    c = lax.axis_index("ctx")
+    gain_one, gain_two = gain_lines(lines, [attn_gain, ffn_gain, query_gain, key_gain])
+    row = lax.broadcasted_iota(jnp.int32, (96, 64), 0)
+    col = lax.broadcasted_iota(jnp.int32, (96, 64), 1)
+    sides = jnp.zeros((96, 64), F32)
+    for k in range(2):
+        for j in range(4):
+            at = (row == 4 * c + j) & (col == k)
+            sides = jnp.where(at, lines[2 + k : 3 + k, j : j + 1], sides)
+
+    def lifted(weight, gain):
+        return (weight.astype(F32) * gain).astype(BF)
+
+    both = jnp.concatenate([key_t[...].astype(F32), value_t[...].astype(F32)], axis=0).T
+    wq_s[:, 0:192] = lifted(query[...], gain_one)
+    wq_s[:, 192:320] = lifted(both, gain_one)
+    wq_s[:, 320:384] = sides.astype(BF)
+    wo_s[:, 192:256] = jnp.zeros((96, 64), BF)
+    wo_s[:, 0:192] = output[...].astype(F32).T.astype(BF)
+    for k in range(3):
+        wf_s[:, 896 * k + 768 : 896 * k + 896] = jnp.zeros((96, 128), BF)
+    wf_s[:, 0:864] = lifted(gate[...], gain_two)
+    wf_s[:, 896:1760] = lifted(up[...], gain_two)
+    wf_s[:, 1792:2656] = down_t[...]
+    place = places[0:1, pl.ds(pl.multiple_of(c * 512, 512), 512)]
+    angle = freq[:, 0:1] * place.astype(F32)
+    cosine[...] = jnp.cos(angle)
+    sine[...] = jnp.sin(angle)
+
+
+def prepare(*operands):
+    shapes = [
+        jax.ShapeDtypeStruct((96, 384), BF),
+        jax.ShapeDtypeStruct((96, 256), BF),
+        jax.ShapeDtypeStruct((96, 2688), BF),
+        jax.ShapeDtypeStruct((32, 512), F32),
+        jax.ShapeDtypeStruct((32, 512), F32),
+    ]
+    return pl.pallas_call(
+        prepare_kernel,
+        out_shape=shapes,
+        in_specs=[VM] * 13,
+        out_specs=[VM] * 5,
+        scratch_shapes=[pltpu.VMEM((8, 128), F32)],
+        name="prepare",
+        compiler_params=pltpu.CompilerParams(vmem_limit_bytes=59 << 20),
+    )(*operands)
+
+
+def conclude_kernel(
+    attn_gain, ffn_gain, block, gin, own_q, own_w, side,
+    block_output, grad_input, g_attn, g_query, g_key, g_value, g_qg, g_kg, g_out, g_ffn, g_gate, g_up, g_down,
+    lines,
+):
+    gain_one, gain_two = gain_lines(lines, [attn_gain, ffn_gain])
+    block_output[...] = block[...]
+    grad_input[...] = gin[...].astype(F32)
+    g_query[...] = own_q[:, 0:192] * gain_one
+    both = (own_q[:, 192:320] * gain_one).T
+    g_key[...] = both[0:64]
+    g_value[...] = both[64:128]
+    g_out[...] = own_q[:, 384:576].T
+    g_gate[...] = own_w[0, :, 0:864] * gain_two
+    g_up[...] = own_w[1, :, 0:864] * gain_two
+    g_down[...] = own_w[2, :, 0:864]
+    g_attn[...] = side[0:1, 0:96] / lines[0:1, 0:96]
+    g_ffn[...] = side[1:2, 0:96] / lines[1:2, 0:96]
+    g_qg[...] = side[2:3, 0:4]
+    g_kg[...] = side[3:4, 0:4]
+
+
+def conclude(*operands):
+    dims = [
+        ((512, 1536), BF), ((512, 1536), F32), ((1, 96), F32), ((96, 192), F32), ((64, 96), F32),
+        ((64, 96), F32), ((1, 4), F32), ((1, 4), F32), ((192, 96), F32), ((1, 96), F32),
+        ((96, 864), F32), ((96, 864), F32), ((96, 864), F32),
+    ]
+    results = pl.pallas_call(
+        conclude_kernel,
+        out_shape=[jax.ShapeDtypeStruct(*d) for d in dims],
+        in_specs=[VM] * 7,
+        out_specs=[VM] * 13,
+        scratch_shapes=[pltpu.VMEM((8, 128), F32)],
+        name="conclude",
+        compiler_params=pltpu.CompilerParams(vmem_limit_bytes=59 << 20),
+    )(*operands)
+    results = [r.T if k in (4, 5, 12) else r for k, r in enumerate(results)]
+    return tuple(r.reshape(-1) if r.shape[0] == 1 else r for r in results)
 
 
 def forward_kernel(
     kb, x_ref, cot, wq_s, wo_s, wf_s, cos_ref, sin_ref,
-    wq, kv, qt, raw, sums, normed, att_own, u_ref, share_ref, block, gain_two, low, act, grad_g, grad_u, p_all,
+    wq_out, kv_out, qt_out, raw_out, normed_out, low_out, act_out, g_out, u_out, share_out,
+    sums, att_own, u_ref, mid_own, col_sum, gain_two, p_all,
+    wq, kv, qt, raw, normed, low, act, grad_g, grad_u, share_ref,
     wo_t, wf, wo, att, acc, pbuf, mid, inv, gate, up, ffn,
-    s_w, r_w, s_v, r_v, s_f, r_f, s_o, r_o, s_k, r_k, s_a, r_a, s_l, s_p,
+    s_w, r_w, s_v, r_v, s_f, r_f, s_o, r_o, s_k, r_k, s_a, r_a, s_l, s_p, s_out,
     *rest,
 ):
     me = Place()
@@ -365,6 +523,23 @@
     ]
     for k in keep:
         k.start()
+    emits = [
+        pltpu.make_async_copy(v, h, s_out.at[k])
+        for k, (v, h) in enumerate(
+            [
+                (wq, wq_out),
+                (kv, kv_out),
+                (qt, qt_out),
+                (raw, raw_out),
+                (normed, normed_out),
+                (low, low_out),
+                (act, act_out),
+                (grad_g, g_out),
+                (grad_u, u_out),
+                (share_ref, share_out),
+            ]
+        )
+    ]
 
     def norm_rows(i, carry):
         rows = pl.ds(pl.multiple_of(i * 64, 64), 64)
@@ -377,12 +552,22 @@
     weights.pair()
     outs.near()
     outs.pair()
+    emits[4].start()
     weights.far()
     weights.last()
     outs.far()
-    feed[0].begin()
+    outs.last()
+    keep[1].wait()
+    outs.end()
+    heads = wo_t[...].T
+    wo[pl.ds(pl.multiple_of(me.t * 192 + me.core * 96, 96), 96)] = jnp.where(
+        me.core == 0, heads[0:96], heads[96:192]
+    )
+    outw.begin()
     keep[0].wait()
     weights.end()
+    feed[0].begin()
+    emits[0].start()
 
     def project(i, carry):
         cols = pl.ds(pl.multiple_of(i * 256, 256), 256)
@@ -390,6 +575,7 @@
         return carry
 
     lax.fori_loop(0, tokens // 256, project, 0)
+    emits[3].start()
     query_gain, key_gain = gain_columns(wq)
     cosine, sine = cos_ref[...], sin_ref[...]
 
@@ -406,14 +592,8 @@
         qt[0:64, h * tokens : (h + 1) * tokens] = (
             turned(raw[64 * h : 64 * h + 64], query_gain) * (LOG2E / 8.0)
         ).astype(BF)
-    outs.last()
-    keep[1].wait()
-    outs.end()
-    heads = wo_t[...].T
-    wo[pl.ds(pl.multiple_of(me.t * 192 + me.core * 96, 96), 96)] = jnp.where(
-        me.core == 0, heads[0:96], heads[96:192]
-    )
-    outw.begin()
+    emits[2].start()
+    outw.near()
     feed[1].begin()
     acc[...] = jnp.zeros_like(acc)
     ones = jnp.concatenate([jnp.ones((1, 1024), BF), jnp.zeros((15, 1024), BF)], axis=0)
@@ -429,7 +609,7 @@
             line = []
             for b in range(2):
                 sub = scores[a * 256 : a * 256 + 256, b * 256 : b * 256 + 256]
-                seen = apart <= kb[me.c * 2 + b] - kb[place * 4 + a]
+                seen = apart <= kb[me.c * 512 + b * 256] - kb[place * 1024 + a * 256]
                 line.append(jnp.where(seen, jnp.exp2(sub), 0.0).astype(BF))
             parts.append(jnp.concatenate(line, axis=1))
         weight = jnp.concatenate(parts, axis=0)
@@ -456,6 +636,7 @@
         @pl.when(step == 1)
         def _():
             keys.near()
+            outw.pair()
             keys.got(11)
 
         @pl.when(step == 2)
@@ -471,14 +652,13 @@
         @pl.when(step == 4)
         def _():
             keys.far()
+            outw.far()
             keys.got(13)
-            outw.near()
 
         @pl.when(step == 5)
         def _():
             keys.got(14)
             feed[0].pair()
-            outw.pair()
 
         @pl.when(step == 6)
         def _():
@@ -489,6 +669,8 @@
         @pl.when(step == 7)
         def _():
             keys.got(16)
+            outw.last()
+            emits[1].start()
 
         place = chip_of(me, step, PAIRS)
         slot = lax.rem(step, 4)
@@ -508,7 +690,6 @@
         @pl.when(i == 0)
         def _():
             feed[1].near()
-            outw.far()
 
         @pl.when(i == 1)
         def _():
@@ -519,7 +700,6 @@
         def _():
             share[0].near()
             share[0].pair()
-            outw.last()
 
         @pl.when(i == 3)
         def _():
@@ -561,15 +741,9 @@
     share[1].last()
     share[2].near()
     share[2].pair()
-    feed[2].far()
     share[2].far()
     share[2].last()
-    feed[2].last()
     outw.end()
-    keep[2].wait()
-    keep[3].wait()
-    feed[0].end()
-    feed[1].end()
 
     def forward_rows(i, carry):
         rows = pl.ds(pl.multiple_of(i * 256, 256), 256)
@@ -579,22 +753,35 @@
         inv[rows] = jnp.broadcast_to(inverse, (256, 128))
         hidden = (value * inverse).astype(BF)
         low[rows] = hidden
+
+        @pl.when(i == 0)
+        def _():
+            keep[2].wait()
+            feed[0].end()
+            keep[3].wait()
+            feed[1].end()
+            feed[2].far()
+
         g = dot(hidden, wf[0])
         u = dot(hidden, wf[1])
         gate[rows] = g
         up[rows] = u
-        a = (g * jax.nn.sigmoid(g) * u).astype(BF)
-        act[rows] = a
-
-        @pl.when(i == 0)
-        def _():
-            keep[4].wait()
-            feed[2].end()
-
-        ffn[rows] = dot_nt(a, wf[2]).astype(BF)
+        act[rows] = (g * jax.nn.sigmoid(g) * u).astype(BF)
         return carry
 
     lax.fori_loop(0, 2, forward_rows, 0)
+    emits[5].start()
+    emits[6].start()
+    feed[2].last()
+    keep[4].wait()
+    feed[2].end()
+
+    def down_rows(i, carry):
+        rows = pl.ds(pl.multiple_of(i * 256, 256), 256)
+        ffn[rows] = dot_nt(act[rows], wf[2]).astype(BF)
+        return carry
+
+    lax.fori_loop(0, 2, down_rows, 0)
     sum_f.begin()
     gain_two[...] = jnp.zeros_like(gain_two)
 
@@ -623,10 +810,12 @@
         return carry
 
     lax.fori_loop(0, 2, backward_rows, 0)
-    sum_f.column()
-    own = pl.multiple_of(me.t * 64, 64)
-    block[0:32] = (mid[pl.ds(own, 32)] + sum_f.finish(0)).astype(BF)
-    block[32:64] = (mid[pl.ds(pl.multiple_of(own + 32, 32), 32)] + sum_f.finish(1)).astype(BF)
+    for k in range(7, 10):
+        emits[k].start()
+    mid_own[...] = mid[pl.ds(pl.multiple_of(me.t * 64, 64), 64)]
+    sum_f.columns(col_sum)
+    for k in range(10):
+        emits[k].wait()
     keys.sent()
     sum_f.sent()
     for s in share:
@@ -637,25 +826,29 @@
 
 def forward_part(*operands):
     tokens = 512
-    shapes = [
-        jax.ShapeDtypeStruct((1536, 384), BF),
-        jax.ShapeDtypeStruct((16 * tokens, 128), BF),
-        jax.ShapeDtypeStruct((128, 3 * tokens), BF),
-        jax.ShapeDtypeStruct((384, tokens), F32),
+    kept = [
+        ((1536, 384), BF),
+        ((16 * tokens, 128), BF),
+        ((128, 3 * tokens), BF),
+        ((384, tokens), F32),
+        ((tokens, 1536), BF),
+        ((tokens, 1536), BF),
+        ((tokens, 896), BF),
+        ((tokens, 896), BF),
+        ((tokens, 896), BF),
+        ((tokens, 1536), BF),
+    ]
+    shapes = [jax.ShapeDtypeStruct(*k) for k in kept] + [
         jax.ShapeDtypeStruct((8, 3 * tokens), F32),
-        jax.ShapeDtypeStruct((tokens, 1536), BF),
         jax.ShapeDtypeStruct((192, tokens), BF),
         jax.ShapeDtypeStruct((1536, tokens), BF),
-        jax.ShapeDtypeStruct((tokens, 1536), BF),
-        jax.ShapeDtypeStruct((64, 1536), BF),
+        jax.ShapeDtypeStruct((64, 1536), F32),
+        jax.ShapeDtypeStruct((2, 64, 1536), BF),
         jax.ShapeDtypeStruct((1, 1536), F32),
-        jax.ShapeDtypeStruct((tokens, 1536), BF),
-        jax.ShapeDtypeStruct((tokens, 896), BF),
-        jax.ShapeDtypeStruct((tokens, 896), BF),
-        jax.ShapeDtypeStruct((tokens, 896), BF),
         jax.ShapeDtypeStruct((8, 3, 1024, tokens), BF),
     ]
     scratch = [
+        *[pltpu.VMEM(*k) for k in kept],
         pltpu.VMEM((1536, 256), BF),
         pltpu.VMEM((3, 1536, 896), BF),
         pltpu.VMEM((1536, 1536), BF),
@@ -673,13 +866,14 @@
         *[DMA((3, 9))] * 2,
         DMA((5,)),
         DMA((4,)),
+        DMA((10,)),
         *ring_scratch(32, 1536),
     ]
     return pl.pallas_call(
         forward_kernel,
         out_shape=shapes,
         in_specs=[SM] + [VM] * 7,
-        out_specs=[VM] * 15 + [HB],
+        out_specs=[HB] * 10 + [VM] * 6 + [HB],
         scratch_shapes=scratch,
         name="forward_part",
         compiler_params=pltpu.CompilerParams(
@@ -689,20 +883,22 @@
 
 
 def backward_kernel(
-    kb, u_ref, share_ref, block, cot, low, act, grad_g, grad_u, gain_two,
-    x_ref, normed, wq, raw, att_own, sums, qt, kv, cos_ref, sin_ref, p_all,
-    two, gin, own_q, own_w, gains,
-    mid_rows, own_two, branch, gt, drift, dq, gk, gk_sib, wg, sib_w, pw, sib_p, back, pre, extra,
-    s_two, r_two, s_in, r_in, s_ex, r_ex, s_sib, r_sib, s_loc, s_p,
+    wq_in, kv_in, qt_in, raw_in, normed_in, low, act, grad_g, grad_u, share_in,
+    sums, att_own, u_ref, mid_own, col_sum, gain_two, p_all, cot, x_in, cos_ref, sin_ref,
+    blk, gin, own_q, own_w, gains,
+    wq, kv, qt, raw, share_ref, x_ref, col_z,
+    mid_rows, branch, gt, drift, dq, gk, gk_sib, wg, sib_w, pw, sib_p, back, pre, extra,
+    s_blk, r_blk, s_br, r_br, s_in, r_in, s_ex, r_ex, s_sib, r_sib, s_loc, s_p,
     *rest,
 ):
     me = Place()
     cn = ctx_neighbours(me)
     tn = tp_neighbours(me)
     sib = cn[3]
-    tokens = normed.shape[0]
+    tokens = 512
     scratch = [rest[8 * k : 8 * k + 8] for k in range(8)]
-    greet([*cn, *tn])
+    crossing = tp_cross(me)
+    greet([*cn, *tn, *crossing, (me.c, me.tp(0, 2)), (me.c, me.tp(1, 2))])
 
     def tp_block(k):
         return me.tp(*SLOTS[k])
@@ -718,9 +914,9 @@
 
         return src
 
-    sum_u = ring(rows_of(u_ref, 192), 96, scratch[0], tn, True)
-    sum_two = ring(rows_of(share_ref, 64), 32, scratch[1], tn, True)
-    sum_b = ring(rows_of(back, 64), 32, scratch[2], tn)
+    sum_u = ring(rows_of(u_ref, 192), 96, scratch[0], tn, True, crossing)
+    sum_two = ring(rows_of(share_ref, 64), 32, scratch[1], tn, True, crossing)
+    sum_b = ring(rows_of(back, 64), 32, scratch[2], tn, False, crossing)
     sum_kv = ring(
         lambda k, part: gk.at[k, me.core, pl.ds(64 * part, 64)], 64, scratch[3], cn
     )
@@ -736,9 +932,21 @@
     sum_q = ring(
         lambda k, part: pw.at[chip(k), me.core, pl.ds(48 * part, 48)], 48, scratch[7], cn
     )
-    put_two = Gather(two, 128, me.tp, *tn, None, s_two, r_two, own=own_two)
+    put_two = Gather(blk, 64, me.tp, *tn, None, s_blk, r_blk, over=True)
+    put_br = Gather(branch, 64, me.tp, *tn, None, s_br, r_br)
     put_in = Gather(gin, 64, me.tp, *tn, None, s_in, r_in)
-    put_ex = Gather(extra, 96, me.tp, *tn, None, s_ex, r_ex)
+    others = [(dz, dy) for dz in (0, 1) for dy in range(4) if (dz, dy) != (0, 0)]
+    put_ex = [
+        pltpu.make_async_remote_copy(
+            src_ref=extra.at[0],
+            dst_ref=extra.at[1 + k],
+            send_sem=s_ex.at[k],
+            recv_sem=r_ex.at[k],
+            device_id=(me.c, me.tp(*o)),
+            device_id_type=MESH,
+        )
+        for k, o in enumerate(others)
+    ]
 
     def to_sibling(k, here, there):
         return pltpu.make_async_remote_copy(
@@ -755,23 +963,44 @@
 
     swap_w = [to_sibling(8 + p, wg.at[p, :, 1 - me.core], sib_w.at[p]) for p in range(3)]
     swap_p = to_sibling(11, pw.at[:, 1 - me.core], sib_p)
+    cross = pltpu.make_async_remote_copy(
+        src_ref=col_sum.at[1],
+        dst_ref=col_z,
+        send_sem=s_sib.at[12],
+        recv_sem=r_sib.at[12],
+        device_id=tn[0],
+        device_id_type=MESH,
+    )
+    takes = [
+        pltpu.make_async_copy(h, v, s_loc.at[14 + k])
+        for k, (h, v) in enumerate(
+            [
+                (wq_in, wq),
+                (kv_in, kv),
+                (qt_in, qt),
+                (raw_in, raw),
+                (share_in, share_ref),
+                (x_in.at[pl.ds(pl.multiple_of(me.t * 64, 64), 64)], x_ref),
+            ]
+        )
+    ]
 
     sum_u.begin()
-
-    def weight_grads(b_low, b_cot, b_act, b_g, b_u):
-        loads = [
-            pltpu.make_async_copy(h, v, s_loc.at[k])
-            for k, (h, v) in enumerate(
-                [(low, b_low), (grad_g, b_g), (grad_u, b_u), (cot, b_cot), (act, b_act)]
-            )
-        ]
-        for k in loads:
+    cross.start()
+
+    def weight_grads(b_low, b_cot, b_one, b_two):
+        def load(k, here, there):
+            return pltpu.make_async_copy(here, there, s_loc.at[k])
+
+        loads = [load(0, low, b_low), load(1, grad_g, b_one), load(2, grad_u, b_two)]
+        loads += [load(3, cot, b_cot), load(4, act, b_one)]
+        for k in loads[0:4] + takes:
             k.start()
         loads[0].wait()
-        for p, (left, right) in enumerate([(b_low, b_g), (b_low, b_u), (b_cot, b_act)]):
-            loads[1 + p].wait()
+        for p, (left, right) in enumerate([(b_low, b_one), (b_low, b_two), (b_cot, b_one)]):
+            loads[(1, 2, 4)[p]].wait()
             if p == 2:
-                loads[4].wait()
+                loads[3].wait()
 
             def chunk(i, carry, p=p, left=left, right=right):
                 at = pl.ds(pl.multiple_of(384 * i, 384), 384)
@@ -783,9 +1012,8 @@
             lax.fori_loop(0, 4, chunk, 0)
             swap_w[p].start()
             if p == 0:
+                loads[4].start()
                 sum_u.relay()
-            if p == 1:
-                sum_u.column()
 
     pl.run_scoped(
         weight_grads,
@@ -793,7 +1021,6 @@
         pltpu.VMEM((tokens, 1536), BF),
         pltpu.VMEM((tokens, 896), BF),
         pltpu.VMEM((tokens, 896), BF),
-        pltpu.VMEM((tokens, 896), BF),
     )
 
     def join_w(p):
@@ -807,8 +1034,16 @@
 
     join_w(0)
     sum_w[0].begin()
+    for k in takes:
+        k.wait()
     grad_att = jnp.concatenate([sum_u.finish(0), sum_u.finish(1)], axis=0)
+    own = pl.multiple_of(me.t * 64, 64)
+    cross.wait_recv()
+    blk[pl.ds(own, 64)] = (
+        mid_own[...] + col_sum[0].astype(F32) + col_z[...].astype(F32)
+    ).astype(BF)
     sum_two.begin()
+    put_two.begin()
     gt[0:64] = jnp.zeros((64, 3 * tokens), BF)
     for h in range(3):
         cols = slice(h * tokens, (h + 1) * tokens)
@@ -826,99 +1061,94 @@
         add_into(gk.at[k, me.core], gk.at[k, me.core], gk_sib.at[k])
 
     def key_loop(pbuf):
-        def load(step, slot):
+        def load(step, h):
             return pltpu.make_async_copy(
-                p_all.at[chip_of(me, step, SLOTS)], pbuf.at[slot], s_p.at[slot]
+                p_all.at[chip_of(me, step, SLOTS), h], pbuf.at[h], s_p.at[h]
             )
 
-        load(0, 0).start()
+        for h in range(3):
+            load(0, h).start()
 
         def key_step(step, carry):
-            slot = lax.rem(step, 2)
-
-            @pl.when(step < 7)
+            @pl.when(step == 1)
             def _():
-                load(step + 1, 1 - slot).start()
-
-            @pl.when(step == 0)
-            def _():
+                join_keys(0)
+                sum_kv.go(0, 1)
+                sum_two.relay()
                 sum_w[0].relay()
                 join_w(1)
                 sum_w[1].begin()
 
-            @pl.when(step == 1)
-            def _():
-                join_keys(0)
-                sum_kv.go(2, 3)
-                sum_w[0].column()
-
             @pl.when(step == 2)
             def _():
                 join_keys(1)
-                sum_kv.go(0, 1)
-                sum_two.relay()
-                sum_w[1].relay()
-                join_w(2)
-                sum_w[2].begin()
+                sum_kv.go(2, 3)
+                put_two.near()
 
             @pl.when(step == 3)
             def _():
                 join_keys(2)
                 sum_kv.go(4)
                 sum_kv.relay_right(1)
-                sum_w[1].column()
-                sum_two.column()
+                branch_rows = jnp.concatenate([sum_two.finish(0), sum_two.finish(1)], axis=0)
+                mid_rows[...] = branch_rows
+                branch[pl.ds(own, 64)] = branch_rows.astype(BF)
+                put_br.begin()
+                sum_w[0].column()
+                sum_w[1].relay()
+                join_w(2)
+                sum_w[2].begin()
 
             @pl.when(step == 4)
             def _():
                 join_keys(3)
                 sum_kv.go(5)
                 sum_kv.relay_left(1)
-                sum_w[2].relay()
-                branch_rows = jnp.concatenate([sum_two.finish(0), sum_two.finish(1)], axis=0)
-                mid_rows[...] = branch_rows
-                own_two[0:64] = block[...]
-                own_two[64:128] = branch_rows.astype(BF)
-                put_two.begin()
-                keep_two.start()
+                put_two.far()
 
             @pl.when(step == 5)
             def _():
                 join_keys(4)
                 sum_kv.go(6)
                 sum_kv.relay_right(0)
-                for half in range(2):
-                    own_w[0, 48 * half : 48 * half + 48] = sum_w[0].finish(half)
+                sum_w[1].column()
+                put_two.pair()
+                put_br.near()
+                put_br.pair()
 
             @pl.when(step == 6)
             def _():
                 join_keys(5)
                 sum_kv.go(7)
                 sum_kv.relay_left(0)
-                put_two.near()
-                sum_w[2].column()
+                put_br.far()
+                put_two.last()
+                sum_w[2].relay()
 
             @pl.when(step == 7)
             def _():
                 join_keys(6)
                 sum_kv.column()
-                put_two.pair()
-                for half in range(2):
-                    own_w[1, 48 * half : 48 * half + 48] = sum_w[1].finish(half)
+                put_br.last()
 
             place = chip_of(me, step, SLOTS)
-            load(step, slot).wait()
             rows = kv[pl.ds(pl.multiple_of(place * 1024, 1024), 1024), :]
             key_t = rows.T[0:64]
             key_grad = value_grad = 0.0
             for h in range(3):
                 cols = slice(h * tokens, (h + 1) * tokens)
                 slopes = dot(rows, gt[:, cols])
-                weight = pbuf[slot, h]
+                load(step, h).wait()
+                weight = pbuf[h]
                 grad = (weight.astype(F32) * (slopes - drift[0:1, cols])).astype(BF)
                 dq[:, cols] += dot(key_t, grad)
                 key_grad += dot_nt(qt[0:64, cols], grad)
                 value_grad += dot_nt(gt[64:128, cols], weight)
+
+                @pl.when(step < 7)
+                def _(h=h):
+                    load(step + 1, h).start()
+
             both = jnp.concatenate([key_grad * LN2, value_grad], axis=0).astype(BF)
             gk[step, 0] = both[:, 0:512]
             gk[step, 1] = both[:, 512:1024]
@@ -927,145 +1157,143 @@
 
         lax.fori_loop(0, 8, key_step, 0)
 
-    keep_two = pltpu.make_async_copy(
-        own_two, two.at[pl.ds(pl.multiple_of(me.t * 128, 128), 128)], s_loc.at[5]
-    )
-    pl.run_scoped(key_loop, pltpu.VMEM((2, 3, 1024, tokens), BF))
-    query_gain, key_gain = gain_columns(wq)
-    cosine, sine = cos_ref[...], sin_ref[...]
-
-    def unturn(grad, value, gain):
-        inverse = column_inverse(value)
+    pl.run_scoped(key_loop, pltpu.VMEM((3, 1024, tokens), BF))
+    def finale(normed):
+        fetch = pltpu.make_async_copy(normed_in, normed, s_loc.at[5])
+        fetch.start()
+        query_gain, key_gain = gain_columns(wq)
+        cosine, sine = cos_ref[...], sin_ref[...]
+
+        def unturn(grad, value, gain):
+            inverse = column_inverse(value)
+            hat = value * inverse
+            a, b = grad[:32], grad[32:]
+            plain = jnp.concatenate([a * cosine + b * sine, b * cosine - a * sine], axis=0)
+            gain_grad = jnp.sum(plain * hat, axis=1, keepdims=True)
+            pulled = plain * gain
+            back_grad = inverse * (pulled - hat * jnp.mean(pulled * hat, axis=0, keepdims=True))
+            return gain_grad, back_grad
+
+        query_gain_grad = 0.0
+        for h in range(3):
+            part, grad = unturn(
+                dq[:, h * tokens : (h + 1) * tokens] * 0.125, raw[64 * h : 64 * h + 64], query_gain
+            )
+            query_gain_grad += part
+            pre[64 * h : 64 * h + 64] = grad
+        join_keys(7)
+        key_grad, value_grad = sum_kv.finish(0), sum_kv.finish(1)
+        key_gain_grad, grad = unturn(key_grad, raw[192:256], key_gain)
+        pre[192:256] = grad
+        pre[256:320] = value_grad
+        pre[320:384] = jnp.zeros((64, tokens), F32)
+        pre_n = pre[...].T.astype(BF)
+        for i in range(2):
+            rows = slice(256 * i, 256 * i + 256)
+            back[rows] = dot_nt(pre_n[rows], wq[...]).astype(BF)
+        sum_b.begin()
+        fetch.wait()
+        gain_one = 0.0
+        for i in range(4):
+            rows = slice(128 * i, 128 * i + 128)
+            gain_one += jnp.sum(
+                back[rows].astype(F32) * normed[rows].astype(F32), axis=0, keepdims=True
+            )
+        sum_w[2].column()
+        lane = lax.broadcasted_iota(jnp.int32, (64, 1536), 1)
+        unit = lax.broadcasted_iota(jnp.int32, (64, 1536), 0)
+        spot = lane == (unit // 4) * 96 + lax.rem(unit, 4)
+
+        def spread(column):
+            return jnp.sum(jnp.where(spot, column, 0.0), axis=0, keepdims=True)
+
+        lines = jnp.concatenate(
+            [
+                jnp.zeros((64, 1536), F32),
+                gain_one,
+                gain_two[...],
+                spread(query_gain_grad),
+                spread(key_gain_grad),
+                jnp.zeros((60, 1536), F32),
+            ],
+            axis=0,
+        )
+        sides = lines.T
+        sum_b.relay()
+        att_n = jnp.concatenate([att_own[...].astype(F32), jnp.zeros((64, tokens), F32)], axis=0).T.astype(BF)
+        for i in range(4):
+            at = slice(384 * i, 384 * i + 384)
+            part = dot(normed[:, at].T, pre_n)
+            part = jnp.concatenate([part[:, 0:256], part[:, 256:384] + sides[at]], axis=1)
+            whole = jnp.concatenate([part, dot(branch[:, at].T, att_n)], axis=1).astype(BF)
+            for q in range(4):
+                pw[2 * i + q // 2, q % 2] = whole[96 * q : 96 * q + 96]
+        swap_p.start()
+        swap_p.wait_recv()
+
+        def join_p(j, carry):
+            add_into(pw.at[j, me.core], pw.at[j, me.core], sib_p.at[j])
+            return carry
+
+        lax.fori_loop(0, 8, join_p, 0)
+        sum_q.begin()
+        value = x_ref[...].astype(F32)
+        inverse = rms_inverse(value)
         hat = value * inverse
-        a, b = grad[:32], grad[32:]
-        plain = jnp.concatenate([a * cosine + b * sine, b * cosine - a * sine], axis=0)
-        gain_grad = jnp.sum(plain * hat, axis=1, keepdims=True)
-        pulled = plain * gain
-        back_grad = inverse * (pulled - hat * jnp.mean(pulled * hat, axis=0, keepdims=True))
-        return gain_grad, back_grad
-
-    query_gain_grad = 0.0
-    for h in range(3):
-        part, grad = unturn(
-            dq[:, h * tokens : (h + 1) * tokens] * 0.125, raw[64 * h : 64 * h + 64], query_gain
-        )
-        query_gain_grad += part
-        pre[64 * h : 64 * h + 64] = grad
-    put_two.far()
-    join_keys(7)
-    key_grad, value_grad = sum_kv.finish(0), sum_kv.finish(1)
-    key_gain_grad, grad = unturn(key_grad, raw[192:256], key_gain)
-    pre[192:256] = grad
-    pre[256:320] = value_grad
-    pre[320:384] = jnp.zeros((64, tokens), F32)
-    pre_n = pre[...].T.astype(BF)
-    gain_one = 0.0
-    for i in range(2):
-        rows = slice(256 * i, 256 * i + 256)
-        part = dot_nt(pre_n[rows], wq[...])
-        back[rows] = part.astype(BF)
-        gain_one += jnp.sum(part * normed[rows].astype(F32), axis=0, keepdims=True)
-    sum_b.begin()
-    put_two.last()
-    keep_two.wait()
-    fetch = [
-        pltpu.make_async_copy(
-            two.at[pl.ds(128 * b + 64, 64)], branch.at[pl.ds(64 * b, 64)], s_loc.at[6 + b]
-        )
-        for b in range(8)
-    ]
-    for f in fetch:
-        f.start()
-    for half in range(2):
-        own_w[2, 48 * half : 48 * half + 48] = sum_w[2].finish(half)
-    lane = lax.broadcasted_iota(jnp.int32, (64, 1536), 1)
-    unit = lax.broadcasted_iota(jnp.int32, (64, 1536), 0)
-    spot = lane == (unit // 4) * 96 + lax.rem(unit, 4)
-
-    def spread(column):
-        return jnp.sum(jnp.where(spot, column, 0.0), axis=0, keepdims=True)
-
-    lines = jnp.concatenate(
-        [
-            jnp.zeros((64, 1536), F32),
-            gain_one,
-            gain_two[...],
-            spread(query_gain_grad),
-            spread(key_gain_grad),
-            jnp.zeros((60, 1536), F32),
-        ],
-        axis=0,
-    )
-    sides = lines.T
-    sum_b.relay()
-    att_n = jnp.concatenate([att_own[...].astype(F32), jnp.zeros((64, tokens), F32)], axis=0).T.astype(BF)
-    for f in fetch:
-        f.wait()
-    for i in range(4):
-        at = slice(384 * i, 384 * i + 384)
-        part = dot(normed[:, at].T, pre_n)
-        part = jnp.concatenate([part[:, 0:256], part[:, 256:384] + sides[at]], axis=1)
-        whole = jnp.concatenate([part, dot(branch[:, at].T, att_n)], axis=1).astype(BF)
-        for q in range(4):
-            pw[2 * i + q // 2, q % 2] = whole[96 * q : 96 * q + 96]
-    swap_p.start()
-    sum_b.column()
-    swap_p.wait_recv()
-
-    def join_p(j, carry):
-        add_into(pw.at[j, me.core], pw.at[j, me.core], sib_p.at[j])
-        return carry
-
-    lax.fori_loop(0, 8, join_p, 0)
-    sum_q.begin()
-    own = pl.multiple_of(me.t * 64, 64)
-    value = x_ref[...].astype(F32)
-    inverse = rms_inverse(value)
-    hat = value * inverse
-    back_one = jnp.concatenate([sum_b.finish(0), sum_b.finish(1)], axis=0)
-    gin[pl.ds(own, 64)] = (
-        mid_rows[...]
-        + inverse * (back_one - hat * jnp.mean(back_one * hat, axis=-1, keepdims=True))
-    ).astype(BF)
-    put_in.begin()
-    sum_q.relay()
-    put_in.near()
-    put_in.pair()
-    sum_q.column()
-    put_in.far()
-    for half in range(2):
-        own_q[48 * half : 48 * half + 48] = sum_q.finish(half)
-    extra[pl.ds(pl.multiple_of(me.t * 96, 96), 96)] = own_q[:, 256:384]
-    put_ex.begin()
-    put_in.last()
-    put_ex.near()
-    put_ex.pair()
-    put_ex.far()
-    put_ex.last()
-    total = extra[0:96]
-    for b in range(1, 8):
-        total += extra[96 * b : 96 * b + 96]
-    gains[...] = total
-    for s in [sum_u, sum_two, sum_b, sum_kv, sum_q, *sum_w, put_two, put_in, put_ex]:
-        s.sent()
-    for k in range(8):
-        key_swap(k).wait_send()
-    for s in [*swap_w, swap_p]:
-        s.wait_send()
+        back_one = jnp.concatenate([sum_b.finish(0), sum_b.finish(1)], axis=0)
+        gin[pl.ds(own, 64)] = (
+            mid_rows[...]
+            + inverse * (back_one - hat * jnp.mean(back_one * hat, axis=-1, keepdims=True))
+        ).astype(BF)
+        put_in.begin()
+        for p in range(3):
+            for half in range(2):
+                own_w[p, 48 * half : 48 * half + 48] = sum_w[p].finish(half)
+        put_in.near()
+        sum_q.relay()
+        put_in.pair()
+        sum_q.column()
+        put_in.far()
+        for half in range(2):
+            own_q[48 * half : 48 * half + 48] = sum_q.finish(half)
+        extra[0] = own_q[:, 256:384].T[64:72]
+        for p in put_ex:
+            p.start()
+        put_in.last()
+        for p in put_ex:
+            p.wait()
+        total = extra[0]
+        for b in range(1, 8):
+            total += extra[b]
+        gains[...] = total
+        for s in [sum_u, sum_two, sum_b, sum_kv, sum_q, *sum_w, put_two, put_br, put_in]:
+            s.sent()
+        for k in range(8):
+            key_swap(k).wait_send()
+        for s in [*swap_w, swap_p, cross]:
+            s.wait_send()
+
+    pl.run_scoped(finale, pltpu.VMEM((tokens, 1536), BF))
 
 
 def backward_part(*operands):
     tokens = 512
     shapes = [
-        jax.ShapeDtypeStruct((1024, 1536), BF),
+        jax.ShapeDtypeStruct((512, 1536), BF),
         jax.ShapeDtypeStruct((512, 1536), BF),
         jax.ShapeDtypeStruct((96, 640), F32),
         jax.ShapeDtypeStruct((3, 96, 896), F32),
-        jax.ShapeDtypeStruct((96, 128), F32),
+        jax.ShapeDtypeStruct((8, 96), F32),
     ]
     scratch = [
+        pltpu.VMEM((1536, 384), BF),
+        pltpu.VMEM((16 * tokens, 128), BF),
+        pltpu.VMEM((128, 3 * tokens), BF),
+        pltpu.VMEM((384, tokens), F32),
+        pltpu.VMEM((tokens, 1536), BF),
+        pltpu.VMEM((64, 1536), BF),
+        pltpu.VMEM((64, 1536), BF),
         pltpu.VMEM((64, 1536), F32),
-        pltpu.VMEM((128, 1536), BF),
         pltpu.VMEM((tokens, 1536), BF),
         pltpu.VMEM((128, 3 * tokens), BF),
         pltpu.VMEM((8, 3 * tokens), F32),
@@ -1078,12 +1306,12 @@
         pltpu.VMEM((8, 96, 640), BF),
         pltpu.VMEM((tokens, 1536), BF),
         pltpu.VMEM((384, tokens), F32),
-        pltpu.VMEM((768, 128), F32),
-        *[DMA((9,))] * 6,
-        DMA((12,)),
-        DMA((12,)),
-        DMA((14,)),
-        DMA((2,)),
+        pltpu.VMEM((8, 8, 96), F32),
+        *[DMA((9,))] * 8,
+        DMA((13,)),
+        DMA((13,)),
+        DMA((21,)),
+        DMA((3,)),
         *ring_scratch(96, 512, True),
         *ring_scratch(32, 1536, True),
         *ring_scratch(32, 1536),
@@ -1094,8 +1322,8 @@
     return pl.pallas_call(
         backward_kernel,
         out_shape=shapes,
-        in_specs=[SM, VM, VM, VM, HB, HB, HB, HB, HB] + [VM] * 11 + [HB],
-        out_specs=[HB] + [VM] * 4,
+        in_specs=[HB] * 10 + [VM] * 6 + [HB] * 3 + [VM] * 2,
+        out_specs=[VM] * 5,
         scratch_shapes=scratch,
         name="backward_part",
         compiler_params=pltpu.CompilerParams(
@@ -1104,77 +1332,24 @@
     )(*operands)
 
 
-def rotary_tables(places, width):
-    half_width = width // 2
-    freq_table = THETA ** (-(jnp.arange(half_width, dtype=F32) * 2.0 / width))
-    angles = freq_table[:, None] * places.astype(F32)[None, :]
-    return jnp.cos(angles), jnp.sin(angles)
+FREQ = [[THETA ** (-2.0 * i / HD)] * 128 for i in range(HD // 2)]
 
 
 def body(
     block_input, positions, attn_gain, query_weight, key_weight, value_weight, query_gain,
     key_gain, output_weight, ffn_gain, gate_weight, up_weight, down_weight, out_cotangent,
 ):
-    tokens = block_input.shape[0]
-    c, t = lax.axis_index("ctx"), lax.axis_index("tp")
-    gain_one = attn_gain.astype(F32)[:, None]
-    gain_two = ffn_gain.astype(F32)[:, None]
-    kb = positions.reshape(32, 256)[:, 0]
-    own_pos = lax.dynamic_slice_in_dim(positions, c * tokens, tokens, 0)
-    cosine, sine = rotary_tables(own_pos, HD)
-    spot = (jnp.arange(96)[:, None] == 4 * c + jnp.arange(4)[None, :]).astype(F32)
-    head_gains = jnp.stack(
-        [spot @ query_gain.astype(F32), spot @ key_gain.astype(F32)], axis=1
-    ).astype(BF)
-
-    def lifted(weight, gain):
-        return (weight.astype(F32) * gain).astype(BF)
-
-    def padded(weight, width):
-        return jnp.pad(weight, ((0, 0), (0, width - weight.shape[1])))
-
-    wq_s = jnp.concatenate(
-        [
-            lifted(query_weight, gain_one),
-            lifted(key_weight, gain_one),
-            lifted(value_weight, gain_one),
-            padded(head_gains, 64),
-        ],
-        axis=1,
+    def line(gain):
+        return gain.reshape(1, -1)
+
+    wq_s, wo_s, wf_s, cosine, sine = prepare(
+        line(positions), line(attn_gain), line(ffn_gain), line(query_gain), line(key_gain),
+        jnp.array(FREQ, F32), query_weight, key_weight.T, value_weight.T, output_weight,
+        gate_weight, up_weight, down_weight.T,
     )
-    wo_s = padded(output_weight.T, 256)
-    wf_s = jnp.concatenate(
-        [
-            padded(lifted(gate_weight, gain_two), 896),
-            padded(lifted(up_weight, gain_two), 896),
-            padded(down_weight.T, 896),
-        ],
-        axis=1,
-    )
-    (
-        wq, kv, qt, raw, sums, normed, att_own, u, share, block, gain_two_part, low, act, grad_g,
-        grad_u, p_all,
-    ) = forward_part(kb, block_input, out_cotangent, wq_s, wo_s, wf_s, cosine, sine)
-    two, gin, own_q, own_w, gains = backward_part(
-        kb, u, share, block, out_cotangent, low, act, grad_g, grad_u, gain_two_part,
-        lax.dynamic_slice_in_dim(block_input, t * 64, 64, 0),
-        normed, wq, raw, att_own, sums, qt, kv, cosine, sine, p_all,
-    )
-    return (
-        two.reshape(8, 2, 64, 1536)[:, 0].reshape(tokens, 1536),
-        gin.astype(F32),
-        gains[:, 64] / gain_one[:, 0],
-        own_q[:, 0:192] * gain_one,
-        own_q[:, 192:256] * gain_one,
-        own_q[:, 256:320] * gain_one,
-        gains[0:4, 66],
-        gains[0:4, 67],
-        own_q[:, 384:576].T,
-        gains[:, 65] / gain_two[:, 0],
-        own_w[0, :, 0:864] * gain_two,
-        own_w[1, :, 0:864] * gain_two,
-        own_w[2, :, 0:864].T,
-    )
+    results = forward_part(positions, block_input, out_cotangent, wq_s, wo_s, wf_s, cosine, sine)
+    results = backward_part(*results, out_cotangent, block_input, cosine, sine)
+    return conclude(line(attn_gain), line(ffn_gain), *results)
 
 
 def solution(mesh):

time: 274 us -> 243 us (0.89)
  local copies, waits for them, and re-layouts: 12.9 us -> 0 us
  other arithmetic: 10.2 us -> 0 us
  Pallas kernels: 248 us -> 242 us
    pallas_call x1 -> x3, Pallas kernels: 133 us -> 126 us  [the longest x1 118 us: backward_part(): pl.pallas_call(backward_kernel, out_shape=shapes, in_specs=[HB] * 10 + [V...]
    convert_element_type x7 -> x0, other arithmetic: 5.32 us -> none  [the longest x1 2.07 us: body(): gin.astype(F32)]
    slice x4 -> x0, local copies, waits for them, and re-layouts: 4.29 us -> none  [the longest x1 2.76 us: body(): two.reshape(8, 2, 64, 1536)[:, 0].reshape(tokens, 1536)]
    unnamed x24 -> x0, local copies, waits for them, and re-layouts: 3.07 us -> none
where the time goes in v4:
time: 243 us
  Pallas kernels  242 us (100%)
    pallas_call x1, Pallas kernels, backward_part(): pl.pallas_call(backward_kernel, out_shape=shapes, in_specs=[HB] * 10 + [V...  118 us
    pallas_call x1, Pallas kernels, forward_part(): pl.pallas_call(forward_kernel, out_shape=shapes, in_specs=[SM] + [VM] * 7...  116 us
    pallas_call x1, Pallas kernels, conclude(): pl.pallas_call(conclude_kernel, out_shape=[jax.ShapeDtypeStruct(*d) for d...  5.38 us

profile of v4, /device:TPU:0, one launch (start us, length us, event | category | flops | bytes accessed | tf_op | source)
XLA Modules:
  0.0 242.7 jit_solution(6459980237516768961)
XLA Ops:
  0.6 2.7 %prepare.1 = (bf16[96,384]{1,0:T(8,128)(2,1)}, bf16[96,256]{1,0:T(8,128)(2,1)}, bf16[96,2688]{1,0:T(8,128)(2,1)}, f32[32,512]{1,0:T(8,128)}, f32[32,512]{1,0:T(8,128)}) custom-call(s32[1,8192]{1,0:T(1,128)} %bitcast.16, bf16[1,96]{1,0:T(2,128)(2,1)} %bitcast.19, bf16[1,96]{1,0:T(2,128)(2,1)} %bitcast.21, bf16[1,4]{1,0:T(2,128)(2,1)} %bitcast.23, ...), custom_call_target="tpu_custom_call" | custom-call | tf_op jit(solution)/shard_map/prepare/pallas_call | solution.py:423
  3.3 115.8 %forward_part.1 = (bf16[1536,384]{1,0:T(8,128)(2,1)}, bf16[8192,128]{1,0:T(8,128)(2,1)}, bf16[128,1536]{1,0:T(8,128)(2,1)}, f32[384,512]{1,0:T(8,128)}, bf16[512...) custom-call(s32[8192]{0:T(1024)} %kb.1, ...), custom_call_target="tpu_custom_call" | custom-call | tf_op jit(solution)/shard_map/forward_part/pallas_call | solution.py:872
  119.1 118.1 %backward_part.1 = (bf16[512,1536]{1,0:T(8,128)(2,1)}, bf16[512,1536]{1,0:T(8,128)(2,1)}, f32[96,640]{1,0:T(8,128)}, f32[3,96,896]{2,1,0:T(8,128)}, f32[8,96]{1,0:T(8,128)}) custom-call(bf16[1536,384]{1,0:T(8,128)(2,1)} %get-tuple-element.58.wq_in, bf16[8192,128]{1,0:T(8,128)(2,1)} %get-tuple-element.59.kv_in, bf16[128,1536]{1,0:T(8,128)(2,1)} %get-tuple-element.60.qt_in, ...), custom_call_target="tpu_custom_call" | custom-call | tf_op jit(solution)/shard_map/backward_part/pallas_call | solution.py:1322
  237.2 5.4 %conclude.1 = (bf16[512,1536]{1,0:T(8,128)(2,1)}, f32[512,1536]{1,0:T(8,128)}, f32[1,96]{1,0:T(1,128)}, f32[96,192]{1,0:T(8,128)}, f32[64,96]{1,0:T(8,128)}, /*i...) custom-call(bf16[1,96]{1,0:T(2,128)(2,1)} %bitcast.20, ...), custom_call_target="tpu_custom_call" | custom-call | tf_op jit(solution)/shard_map/conclude/pallas_call | solution.py:462

commit v5 on v4

--- a/solution.py
+++ b/solution.py
@@ -484,8 +484,9 @@
     me = Place()
     cn = ctx_neighbours(me)
     tn = tp_neighbours(me)
+    cross = tp_cross(me)
     tokens = x_ref.shape[0]
-    greet([*cn, *tn])
+    greet([*cn, *tn, *cross])
     weights = Gather(wq, 96, me.ctx, *cn, s_w, r_w, own=wq_s)
     outs = Gather(wo_t, 96, me.ctx, *cn, s_v, r_v, own=wo_s)
     feed = [
@@ -500,7 +501,8 @@
     )
     share = [
         Gather(
-            att, 64, lambda dz, dy, h=h: me.tp(dz, dy) * 3 + h, *tn, None, s_a.at[h], r_a.at[h]
+            att, 64, lambda dz, dy, h=h: me.tp(dz, dy) * 3 + h, *tn, None, s_a.at[h], r_a.at[h],
+            cross=cross,
         )
         for h in range(3)
     ]
@@ -513,6 +515,7 @@
 
     weights.begin()
     outs.begin()
+    feed[0].go(1, 2, 9)
     mine = pl.ds(pl.multiple_of(me.c * 96, 96), 96)
     keep = [
         pltpu.make_async_copy(wq_s, wq.at[mine], s_l.at[0]),
@@ -550,6 +553,7 @@
     lax.fori_loop(0, tokens // 64, norm_rows, 0)
     weights.near()
     weights.pair()
+    feed[0].go(0)
     outs.near()
     outs.pair()
     emits[4].start()
@@ -566,7 +570,7 @@
     outw.begin()
     keep[0].wait()
     weights.end()
-    feed[0].begin()
+    feed[1].go(1, 2, 9)
     emits[0].start()
 
     def project(i, carry):
@@ -576,6 +580,7 @@
 
     lax.fori_loop(0, tokens // 256, project, 0)
     emits[3].start()
+    feed[0].near()
     query_gain, key_gain = gain_columns(wq)
     cosine, sine = cos_ref[...], sin_ref[...]
 
@@ -593,8 +598,8 @@
             turned(raw[64 * h : 64 * h + 64], query_gain) * (LOG2E / 8.0)
         ).astype(BF)
     emits[2].start()
+    feed[0].pair()
     outw.near()
-    feed[1].begin()
     acc[...] = jnp.zeros_like(acc)
     ones = jnp.concatenate([jnp.ones((1, 1024), BF), jnp.zeros((15, 1024), BF)], axis=0)
     apart = lax.broadcasted_iota(jnp.int32, (256, 256), 0) - lax.broadcasted_iota(
@@ -636,39 +641,44 @@
         @pl.when(step == 1)
         def _():
             keys.near()
+            feed[1].go(0)
             outw.pair()
             keys.got(11)
 
         @pl.when(step == 2)
         def _():
             keys.pair()
+            feed[1].near()
+            feed[2].go(0)
             keys.got(12)
 
         @pl.when(step == 3)
         def _():
             keys.got(10)
-            feed[0].near()
 
         @pl.when(step == 4)
         def _():
             keys.far()
+            feed[0].far()
+            feed[2].go(1, 2, 9)
             outw.far()
             keys.got(13)
 
         @pl.when(step == 5)
         def _():
+            feed[1].pair()
             keys.got(14)
-            feed[0].pair()
 
         @pl.when(step == 6)
         def _():
             keys.last()
             keys.got(15)
-            feed[2].begin()
 
         @pl.when(step == 7)
         def _():
             keys.got(16)
+            feed[0].last()
+            feed[2].near()
             outw.last()
             emits[1].start()
 
@@ -687,14 +697,9 @@
     close(0)
 
     def more_heads(i, carry):
-        @pl.when(i == 0)
-        def _():
-            feed[1].near()
-
         @pl.when(i == 1)
         def _():
-            feed[0].far()
-            feed[1].pair()
+            feed[2].pair()
 
         @pl.when(i == 2)
         def _():
@@ -703,19 +708,17 @@
 
         @pl.when(i == 3)
         def _():
-            feed[0].last()
+            feed[1].far()
             share[0].far()
 
         @pl.when(i == 4)
         def _():
             close(1)
             share[0].last()
-            feed[2].near()
 
         @pl.when(i == 5)
         def _():
-            feed[1].far()
-            feed[2].pair()
+            feed[1].last()
 
         @pl.when(i == 6)
         def _():
@@ -724,7 +727,7 @@
 
         @pl.when(i == 7)
         def _():
-            feed[1].last()
+            feed[2].far()
             share[1].far()
 
         h = 1 + i // 4
@@ -751,28 +754,34 @@
         inverse = rms_inverse(value)
         mid[rows] = value
         inv[rows] = jnp.broadcast_to(inverse, (256, 128))
-        hidden = (value * inverse).astype(BF)
-        low[rows] = hidden
-
-        @pl.when(i == 0)
-        def _():
-            keep[2].wait()
-            feed[0].end()
-            keep[3].wait()
-            feed[1].end()
-            feed[2].far()
-
-        g = dot(hidden, wf[0])
-        u = dot(hidden, wf[1])
-        gate[rows] = g
+        low[rows] = (value * inverse).astype(BF)
+        return carry
+
+    lax.fori_loop(0, 2, forward_rows, 0)
+    emits[5].start()
+    keep[2].wait()
+    feed[0].end()
+    feed[2].last()
+
+    def gate_rows(i, carry):
+        rows = pl.ds(pl.multiple_of(i * 256, 256), 256)
+        gate[rows] = dot(low[rows], wf[0])
+        return carry
+
+    lax.fori_loop(0, 2, gate_rows, 0)
+    keep[3].wait()
+    feed[1].end()
+
+    def up_rows(i, carry):
+        rows = pl.ds(pl.multiple_of(i * 256, 256), 256)
+        u = dot(low[rows], wf[1])
         up[rows] = u
+        g = gate[rows]
         act[rows] = (g * jax.nn.sigmoid(g) * u).astype(BF)
         return carry
 
-    lax.fori_loop(0, 2, forward_rows, 0)
-    emits[5].start()
+    lax.fori_loop(0, 2, up_rows, 0)
     emits[6].start()
-    feed[2].last()
     keep[4].wait()
     feed[2].end()
 
@@ -887,7 +896,7 @@
     sums, att_own, u_ref, mid_own, col_sum, gain_two, p_all, cot, x_in, cos_ref, sin_ref,
     blk, gin, own_q, own_w, gains,
     wq, kv, qt, raw, share_ref, x_ref, col_z,
-    mid_rows, branch, gt, drift, dq, gk, gk_sib, wg, sib_w, pw, sib_p, back, pre, extra,
+    mid_rows, branch, gt, drift, dq, gk, gk_sib, wg, sib_w, pw, sib_p, po, sib_o, back, pre, extra,
     s_blk, r_blk, s_br, r_br, s_in, r_in, s_ex, r_ex, s_sib, r_sib, s_loc, s_p,
     *rest,
 ):
@@ -896,7 +905,7 @@
     tn = tp_neighbours(me)
     sib = cn[3]
     tokens = 512
-    scratch = [rest[8 * k : 8 * k + 8] for k in range(8)]
+    scratch = [rest[8 * k : 8 * k + 8] for k in range(9)]
     crossing = tp_cross(me)
     greet([*cn, *tn, *crossing, (me.c, me.tp(0, 2)), (me.c, me.tp(1, 2))])
 
@@ -932,6 +941,9 @@
     sum_q = ring(
         lambda k, part: pw.at[chip(k), me.core, pl.ds(48 * part, 48)], 48, scratch[7], cn
     )
+    sum_o = ring(
+        lambda k, part: po.at[chip(k), me.core, pl.ds(48 * part, 48)], 48, scratch[8], cn
+    )
     put_two = Gather(blk, 64, me.tp, *tn, None, s_blk, r_blk, over=True)
     put_br = Gather(branch, 64, me.tp, *tn, None, s_br, r_br)
     put_in = Gather(gin, 64, me.tp, *tn, None, s_in, r_in)
@@ -963,6 +975,7 @@
 
     swap_w = [to_sibling(8 + p, wg.at[p, :, 1 - me.core], sib_w.at[p]) for p in range(3)]
     swap_p = to_sibling(11, pw.at[:, 1 - me.core], sib_p)
+    swap_o = to_sibling(13, po.at[:, 1 - me.core], sib_o)
     cross = pltpu.make_async_remote_copy(
         src_ref=col_sum.at[1],
         dst_ref=col_z,
@@ -1161,6 +1174,15 @@
     def finale(normed):
         fetch = pltpu.make_async_copy(normed_in, normed, s_loc.at[5])
         fetch.start()
+        att_n = jnp.concatenate(
+            [att_own[...].astype(F32), jnp.zeros((64, tokens), F32)], axis=0
+        ).T.astype(BF)
+        for i in range(4):
+            at = slice(384 * i, 384 * i + 384)
+            whole = dot(branch[:, at].T, att_n).astype(BF)
+            for q in range(4):
+                po[2 * i + q // 2, q % 2] = whole[96 * q : 96 * q + 96]
+        swap_o.start()
         query_gain, key_gain = gain_columns(wq)
         cosine, sine = cos_ref[...], sin_ref[...]
 
@@ -1200,6 +1222,14 @@
                 back[rows].astype(F32) * normed[rows].astype(F32), axis=0, keepdims=True
             )
         sum_w[2].column()
+        swap_o.wait_recv()
+
+        def join_o(j, carry):
+            add_into(po.at[j, me.core], po.at[j, me.core], sib_o.at[j])
+            return carry
+
+        lax.fori_loop(0, 8, join_o, 0)
+        sum_o.begin()
         lane = lax.broadcasted_iota(jnp.int32, (64, 1536), 1)
         unit = lax.broadcasted_iota(jnp.int32, (64, 1536), 0)
         spot = lane == (unit // 4) * 96 + lax.rem(unit, 4)
@@ -1220,15 +1250,14 @@
         )
         sides = lines.T
         sum_b.relay()
-        att_n = jnp.concatenate([att_own[...].astype(F32), jnp.zeros((64, tokens), F32)], axis=0).T.astype(BF)
         for i in range(4):
             at = slice(384 * i, 384 * i + 384)
             part = dot(normed[:, at].T, pre_n)
-            part = jnp.concatenate([part[:, 0:256], part[:, 256:384] + sides[at]], axis=1)
-            whole = jnp.concatenate([part, dot(branch[:, at].T, att_n)], axis=1).astype(BF)
+            whole = jnp.concatenate([part[:, 0:256], part[:, 256:384] + sides[at]], axis=1).astype(BF)
             for q in range(4):
                 pw[2 * i + q // 2, q % 2] = whole[96 * q : 96 * q + 96]
         swap_p.start()
+        sum_o.relay()
         swap_p.wait_recv()
 
         def join_p(j, carry):
@@ -1251,14 +1280,17 @@
                 own_w[p, 48 * half : 48 * half + 48] = sum_w[p].finish(half)
         put_in.near()
         sum_q.relay()
+        sum_o.column()
         put_in.pair()
         sum_q.column()
         put_in.far()
         for half in range(2):
-            own_q[48 * half : 48 * half + 48] = sum_q.finish(half)
+            own_q[48 * half : 48 * half + 48, 0:384] = sum_q.finish(half)
         extra[0] = own_q[:, 256:384].T[64:72]
         for p in put_ex:
             p.start()
+        for half in range(2):
+            own_q[48 * half : 48 * half + 48, 384:640] = sum_o.finish(half)
         put_in.last()
         for p in put_ex:
             p.wait()
@@ -1266,11 +1298,11 @@
         for b in range(1, 8):
             total += extra[b]
         gains[...] = total
-        for s in [sum_u, sum_two, sum_b, sum_kv, sum_q, *sum_w, put_two, put_br, put_in]:
+        for s in [sum_u, sum_two, sum_b, sum_kv, sum_q, sum_o, *sum_w, put_two, put_br, put_in]:
             s.sent()
         for k in range(8):
             key_swap(k).wait_send()
-        for s in [*swap_w, swap_p, cross]:
+        for s in [*swap_w, swap_p, swap_o, cross]:
             s.wait_send()
 
     pl.run_scoped(finale, pltpu.VMEM((tokens, 1536), BF))
@@ -1302,14 +1334,16 @@
         pltpu.VMEM((8, 128, 512), BF),
         pltpu.VMEM((3, 8, 2, 96, 896), BF),
         pltpu.VMEM((3, 8, 96, 896), BF),
-        pltpu.VMEM((8, 2, 96, 640), BF),
-        pltpu.VMEM((8, 96, 640), BF),
+        pltpu.VMEM((8, 2, 96, 384), BF),
+        pltpu.VMEM((8, 96, 384), BF),
+        pltpu.VMEM((8, 2, 96, 256), BF),
+        pltpu.VMEM((8, 96, 256), BF),
         pltpu.VMEM((tokens, 1536), BF),
         pltpu.VMEM((384, tokens), F32),
         pltpu.VMEM((8, 8, 96), F32),
         *[DMA((9,))] * 8,
-        DMA((13,)),
-        DMA((13,)),
+        DMA((14,)),
+        DMA((14,)),
         DMA((21,)),
         DMA((3,)),
         *ring_scratch(96, 512, True),
@@ -1317,7 +1351,8 @@
         *ring_scratch(32, 1536),
         *ring_scratch(64, 512),
         *ring_scratch(48, 896) * 3,
-        *ring_scratch(48, 640),
+        *ring_scratch(48, 384),
+        *ring_scratch(48, 256),
     ]
     return pl.pallas_call(
         backward_kernel,

time: 243 us -> 235 us (0.967)
  Pallas kernels: 242 us -> 234 us
    pallas_call x1, Pallas kernels: 116 us -> 110 us  [forward_part(): pl.pallas_call(forward_kernel, out_shape=shapes, in_specs=[SM] + [VM] * 7...]
    pallas_call x1, Pallas kernels: 118 us -> 115 us  [backward_part(): pl.pallas_call(backward_kernel, out_shape=shapes, in_specs=[HB] * 10 + [V...]
where the time goes in v5:
time: 235 us
  Pallas kernels  234 us (100%)
    pallas_call x1, Pallas kernels, backward_part(): pl.pallas_call(backward_kernel, out_shape=shapes, in_specs=[HB] * 10 + [V...  115 us
    pallas_call x1, Pallas kernels, forward_part(): pl.pallas_call(forward_kernel, out_shape=shapes, in_specs=[SM] + [VM] * 7...  110 us
    pallas_call x1, Pallas kernels, conclude(): pl.pallas_call(conclude_kernel, out_shape=[jax.ShapeDtypeStruct(*d) for d...  5.38 us

profile of v5, /device:TPU:0, one launch (start us, length us, event | category | flops | bytes accessed | tf_op | source)
XLA Modules:
  0.0 234.6 jit_solution(17900428090666588136)
XLA Ops:
  0.6 2.7 %prepare.1 = (bf16[96,384]{1,0:T(8,128)(2,1)}, bf16[96,256]{1,0:T(8,128)(2,1)}, bf16[96,2688]{1,0:T(8,128)(2,1)}, f32[32,512]{1,0:T(8,128)}, f32[32,512]{1,0:T(8,128)}) custom-call(s32[1,8192]{1,0:T(1,128)} %bitcast.16, bf16[1,96]{1,0:T(2,128)(2,1)} %bitcast.19, bf16[1,96]{1,0:T(2,128)(2,1)} %bitcast.21, bf16[1,4]{1,0:T(2,128)(2,1)} %bitcast.23, ...), custom_call_target="tpu_custom_call" | custom-call | tf_op jit(solution)/shard_map/prepare/pallas_call | solution.py:423
  3.3 110.4 %forward_part.1 = (bf16[1536,384]{1,0:T(8,128)(2,1)}, bf16[8192,128]{1,0:T(8,128)(2,1)}, bf16[128,1536]{1,0:T(8,128)(2,1)}, f32[384,512]{1,0:T(8,128)}, bf16[512...) custom-call(s32[8192]{0:T(1024)} %kb.1, ...), custom_call_target="tpu_custom_call" | custom-call | tf_op jit(solution)/shard_map/forward_part/pallas_call | solution.py:881
  113.7 115.4 %backward_part.1 = (bf16[512,1536]{1,0:T(8,128)(2,1)}, bf16[512,1536]{1,0:T(8,128)(2,1)}, f32[96,640]{1,0:T(8,128)}, f32[3,96,896]{2,1,0:T(8,128)}, f32[8,96]{1,0:T(8,128)}) custom-call(bf16[1536,384]{1,0:T(8,128)(2,1)} %get-tuple-element.58.wq_in, bf16[8192,128]{1,0:T(8,128)(2,1)} %get-tuple-element.59.kv_in, bf16[128,1536]{1,0:T(8,128)(2,1)} %get-tuple-element.60.qt_in, ...), custom_call_target="tpu_custom_call" | custom-call | tf_op jit(solution)/shard_map/backward_part/pallas_call | solution.py:1357
  229.1 5.4 %conclude.1 = (bf16[512,1536]{1,0:T(8,128)(2,1)}, f32[512,1536]{1,0:T(8,128)}, f32[1,96]{1,0:T(1,128)}, f32[96,192]{1,0:T(8,128)}, f32[64,96]{1,0:T(8,128)}, /*i...) custom-call(bf16[1,96]{1,0:T(2,128)(2,1)} %bitcast.20, ...), custom_call_target="tpu_custom_call" | custom-call | tf_op jit(solution)/shard_map/conclude/pallas_call | solution.py:462

commit v6 on v5

--- a/solution.py
+++ b/solution.py
@@ -633,7 +633,12 @@
         att[pl.ds(pl.multiple_of(me.t * 192 + 64 * h, 64), 64)] = value
         share[h].begin()
 
-    def first_head(step, carry):
+    def task(h, step, slot):
+        place = chip_of(me, step, PAIRS)
+        acc[h] += attend(h, place, slot)
+        store(h, place, slot).start()
+
+    def arriving(step, carry):
         @pl.when(step == 0)
         def _():
             keys.got(9)
@@ -655,96 +660,77 @@
         @pl.when(step == 3)
         def _():
             keys.got(10)
-
-        @pl.when(step == 4)
+            outw.far()
+
+        @pl.when(step >= 2)
+        def _():
+            for h in range(3):
+                store(h, 0, 3 * lax.rem(step, 2) + h).wait()
+
+        for h in range(3):
+            task(h, step, 3 * lax.rem(step, 2) + h)
+        return carry
+
+    lax.fori_loop(0, 4, arriving, 0)
+
+    def arrived(i, carry):
+        @pl.when(i == 0)
         def _():
             keys.far()
             feed[0].far()
             feed[2].go(1, 2, 9)
-            outw.far()
             keys.got(13)
-
-        @pl.when(step == 5)
+            keys.got(14)
+
+        @pl.when(i == 1)
         def _():
             feed[1].pair()
-            keys.got(14)
-
-        @pl.when(step == 6)
-        def _():
             keys.last()
             keys.got(15)
-
-        @pl.when(step == 7)
+            keys.got(16)
+            emits[1].start()
+
+        @pl.when(i == 2)
         def _():
-            keys.got(16)
+            close(0)
             feed[0].last()
+            outw.last()
+
+        @pl.when(i == 3)
+        def _():
             feed[2].near()
-            outw.last()
-            emits[1].start()
-
-        place = chip_of(me, step, PAIRS)
-        slot = lax.rem(step, 4)
-
-        @pl.when(step >= 4)
+
+        @pl.when(i == 4)
         def _():
-            store(0, place, slot).wait()
-
-        acc[0] += attend(0, place, slot)
-        store(0, place, slot).start()
-        return carry
-
-    lax.fori_loop(0, 8, first_head, 0)
-    close(0)
-
-    def more_heads(i, carry):
-        @pl.when(i == 1)
-        def _():
+            close(1)
             feed[2].pair()
 
-        @pl.when(i == 2)
+        @pl.when(i == 5)
         def _():
             share[0].near()
             share[0].pair()
 
-        @pl.when(i == 3)
-        def _():
-            feed[1].far()
-            share[0].far()
-
-        @pl.when(i == 4)
-        def _():
-            close(1)
-            share[0].last()
-
-        @pl.when(i == 5)
-        def _():
-            feed[1].last()
-
-        @pl.when(i == 6)
-        def _():
-            share[1].near()
-            share[1].pair()
-
-        @pl.when(i == 7)
-        def _():
-            feed[2].far()
-            share[1].far()
-
-        h = 1 + i // 4
+        h = i // 2
         for half in range(2):
-            place = chip_of(me, 2 * lax.rem(i, 4) + half, PAIRS)
-            slot = 2 * lax.rem(i, 2) + half
-            store(h, place, slot).wait()
-            acc[h] += attend(h, place, slot)
-            store(h, place, slot).start()
+            slot = lax.rem(2 * i + half, 6)
+            store(h, 0, slot).wait()
+            task(h, 4 + 2 * lax.rem(i, 2) + half, slot)
         return carry
 
-    lax.fori_loop(0, 8, more_heads, 0)
+    lax.fori_loop(0, 6, arrived, 0)
     close(2)
-    share[1].last()
+    feed[1].far()
+    share[0].far()
+    share[1].near()
+    share[1].pair()
+    share[1].far()
     share[2].near()
     share[2].pair()
     share[2].far()
+    feed[2].far()
+    share[0].last()
+    share[1].last()
+    feed[1].last()
     share[2].last()
     outw.end()
 
@@ -829,7 +815,7 @@
     sum_f.sent()
     for s in share:
         s.sent()
-    for slot in range(4):
+    for slot in range(6):
         store(0, 0, slot).wait()
 
 
@@ -863,7 +849,7 @@
         pltpu.VMEM((1536, 1536), BF),
         pltpu.VMEM((1536, tokens), BF),
         pltpu.VMEM((3, 80, tokens), F32),
-        pltpu.VMEM((4, 1024, tokens), BF),
+        pltpu.VMEM((6, 1024, tokens), BF),
         pltpu.VMEM((tokens, 1536), F32),
         pltpu.VMEM((tokens, 128), F32),
         pltpu.VMEM((tokens, 896), F32),
@@ -874,7 +860,7 @@
         *[DMA((17,))] * 4,
         *[DMA((3, 9))] * 2,
         DMA((5,)),
-        DMA((4,)),
+        DMA((6,)),
         DMA((10,)),
         *ring_scratch(32, 1536),
     ]

time: 235 us -> 233 us (level)
    pallas_call x1, Pallas kernels: 110 us -> 107 us  [forward_part(): pl.pallas_call(forward_kernel, out_shape=shapes, in_specs=[SM] + [VM] * 7...]
where the time goes in v6:
time: 233 us
  Pallas kernels  232 us (100%)
    pallas_call x1, Pallas kernels, backward_part(): pl.pallas_call(backward_kernel, out_shape=shapes, in_specs=[HB] * 10 + [V...  117 us
    pallas_call x1, Pallas kernels, forward_part(): pl.pallas_call(forward_kernel, out_shape=shapes, in_specs=[SM] + [VM] * 7...  107 us
    pallas_call x1, Pallas kernels, conclude(): pl.pallas_call(conclude_kernel, out_shape=[jax.ShapeDtypeStruct(*d) for d...  5.38 us

profile of v6, /device:TPU:0, one launch (start us, length us, event | category | flops | bytes accessed | tf_op | source)
XLA Modules:
  0.0 232.7 jit_solution(6372746671379599516)
XLA Ops:
  0.6 2.7 %prepare.1 = (bf16[96,384]{1,0:T(8,128)(2,1)}, bf16[96,256]{1,0:T(8,128)(2,1)}, bf16[96,2688]{1,0:T(8,128)(2,1)}, f32[32,512]{1,0:T(8,128)}, f32[32,512]{1,0:T(8,128)}) custom-call(s32[1,8192]{1,0:T(1,128)} %bitcast.16, bf16[1,96]{1,0:T(2,128)(2,1)} %bitcast.19, bf16[1,96]{1,0:T(2,128)(2,1)} %bitcast.21, bf16[1,4]{1,0:T(2,128)(2,1)} %bitcast.23, ...), custom_call_target="tpu_custom_call" | custom-call | tf_op jit(solution)/shard_map/prepare/pallas_call | solution.py:423
  3.3 106.9 %forward_part.1 = (bf16[1536,384]{1,0:T(8,128)(2,1)}, bf16[8192,128]{1,0:T(8,128)(2,1)}, bf16[128,1536]{1,0:T(8,128)(2,1)}, f32[384,512]{1,0:T(8,128)}, bf16[512...) custom-call(s32[8192]{0:T(1024)} %kb.1, ...), custom_call_target="tpu_custom_call" | custom-call | tf_op jit(solution)/shard_map/forward_part/pallas_call | solution.py:867
  110.3 117.0 %backward_part.1 = (bf16[512,1536]{1,0:T(8,128)(2,1)}, bf16[512,1536]{1,0:T(8,128)(2,1)}, f32[96,640]{1,0:T(8,128)}, f32[3,96,896]{2,1,0:T(8,128)}, f32[8,96]{1,0:T(8,128)}) custom-call(bf16[1536,384]{1,0:T(8,128)(2,1)} %get-tuple-element.58.wq_in, bf16[8192,128]{1,0:T(8,128)(2,1)} %get-tuple-element.59.kv_in, bf16[128,1536]{1,0:T(8,128)(2,1)} %get-tuple-element.60.qt_in, ...), custom_call_target="tpu_custom_call" | custom-call | tf_op jit(solution)/shard_map/backward_part/pallas_call | solution.py:1343
  227.2 5.4 %conclude.1 = (bf16[512,1536]{1,0:T(8,128)(2,1)}, f32[512,1536]{1,0:T(8,128)}, f32[1,96]{1,0:T(1,128)}, f32[96,192]{1,0:T(8,128)}, f32[64,96]{1,0:T(8,128)}, /*i...) custom-call(bf16[1,96]{1,0:T(2,128)(2,1)} %bitcast.20, ...), custom_call_target="tpu_custom_call" | custom-call | tf_op jit(solution)/shard_map/conclude/pallas_call | solution.py:462

commit v7 on v6

--- a/solution.py
+++ b/solution.py
@@ -893,7 +893,6 @@
     tokens = 512
     scratch = [rest[8 * k : 8 * k + 8] for k in range(9)]
     crossing = tp_cross(me)
-    greet([*cn, *tn, *crossing, (me.c, me.tp(0, 2)), (me.c, me.tp(1, 2))])
 
     def tp_block(k):
         return me.tp(*SLOTS[k])
@@ -984,8 +983,6 @@
         )
     ]
 
-    sum_u.begin()
-    cross.start()
 
     def weight_grads(b_low, b_cot, b_one, b_two):
         def load(k, here, there):
@@ -995,6 +992,9 @@
         loads += [load(3, cot, b_cot), load(4, act, b_one)]
         for k in loads[0:4] + takes:
             k.start()
+        greet([*cn, *tn, *crossing, (me.c, me.tp(0, 2)), (me.c, me.tp(1, 2))])
+        sum_u.begin()
+        cross.start()
         loads[0].wait()
         for p, (left, right) in enumerate([(b_low, b_one), (b_low, b_two), (b_cot, b_one)]):
             loads[(1, 2, 4)[p]].wait()
@@ -1002,6 +1002,12 @@
                 loads[3].wait()
 
             def chunk(i, carry, p=p, left=left, right=right):
+                if p == 1:
+
+                    @pl.when(i == 3)
+                    def _():
+                        sum_u.relay()
+
                 at = pl.ds(pl.multiple_of(384 * i, 384), 384)
                 whole = dot(left[:, at].T, right[...]).astype(BF)
                 for q in range(4):
@@ -1012,7 +1018,6 @@
             swap_w[p].start()
             if p == 0:
                 loads[4].start()
-                sum_u.relay()
 
     pl.run_scoped(
         weight_grads,

time: 233 us -> 233 us (level)
  no operation moved by 1% of the time
where the time goes in v7:
time: 233 us
  Pallas kernels  232 us (100%)
    pallas_call x1, Pallas kernels, backward_part(): pl.pallas_call(backward_kernel, out_shape=shapes, in_specs=[HB] * 10 + [V...  117 us
    pallas_call x1, Pallas kernels, forward_part(): pl.pallas_call(forward_kernel, out_shape=shapes, in_specs=[SM] + [VM] * 7...  107 us
    pallas_call x1, Pallas kernels, conclude(): pl.pallas_call(conclude_kernel, out_shape=[jax.ShapeDtypeStruct(*d) for d...  5.38 us

profile of v7, /device:TPU:0, one launch (start us, length us, event | category | flops | bytes accessed | tf_op | source)
XLA Modules:
  0.0 232.7 jit_solution(17143726867317221405)
XLA Ops:
  0.6 2.7 %prepare.1 = (bf16[96,384]{1,0:T(8,128)(2,1)}, bf16[96,256]{1,0:T(8,128)(2,1)}, bf16[96,2688]{1,0:T(8,128)(2,1)}, f32[32,512]{1,0:T(8,128)}, f32[32,512]{1,0:T(8,128)}) custom-call(s32[1,8192]{1,0:T(1,128)} %bitcast.16, bf16[1,96]{1,0:T(2,128)(2,1)} %bitcast.19, bf16[1,96]{1,0:T(2,128)(2,1)} %bitcast.21, bf16[1,4]{1,0:T(2,128)(2,1)} %bitcast.23, ...), custom_call_target="tpu_custom_call" | custom-call | tf_op jit(solution)/shard_map/prepare/pallas_call | solution.py:423
  3.3 106.9 %forward_part.1 = (bf16[1536,384]{1,0:T(8,128)(2,1)}, bf16[8192,128]{1,0:T(8,128)(2,1)}, bf16[128,1536]{1,0:T(8,128)(2,1)}, f32[384,512]{1,0:T(8,128)}, bf16[512...) custom-call(s32[8192]{0:T(1024)} %kb.1, ...), custom_call_target="tpu_custom_call" | custom-call | tf_op jit(solution)/shard_map/forward_part/pallas_call | solution.py:867
  110.3 117.0 %backward_part.1 = (bf16[512,1536]{1,0:T(8,128)(2,1)}, bf16[512,1536]{1,0:T(8,128)(2,1)}, f32[96,640]{1,0:T(8,128)}, f32[3,96,896]{2,1,0:T(8,128)}, f32[8,96]{1,0:T(8,128)}) custom-call(bf16[1536,384]{1,0:T(8,128)(2,1)} %get-tuple-element.58.wq_in, bf16[8192,128]{1,0:T(8,128)(2,1)} %get-tuple-element.59.kv_in, bf16[128,1536]{1,0:T(8,128)(2,1)} %get-tuple-element.60.qt_in, ...), custom_call_target="tpu_custom_call" | custom-call | tf_op jit(solution)/shard_map/backward_part/pallas_call | solution.py:1348
  227.2 5.4 %conclude.1 = (bf16[512,1536]{1,0:T(8,128)(2,1)}, f32[512,1536]{1,0:T(8,128)}, f32[1,96]{1,0:T(1,128)}, f32[96,192]{1,0:T(8,128)}, f32[64,96]{1,0:T(8,128)}, /*i...) custom-call(bf16[1,96]{1,0:T(2,128)(2,1)} %bitcast.20, ...), custom_call_target="tpu_custom_call" | custom-call | tf_op jit(solution)/shard_map/conclude/pallas_call | solution.py:462
